TPU v7x, 32 devices: a whole 2x2x4 slice. The times are simulated.
32 devices in a mesh: cells: 16 (over z, y, x), sub: 2 (over core).
Axes of the slice: x: 2, y: 2, z: 4, core: 2. Of those that a mesh axis runs over, the one named last changes fastest.
Arguments:
- snapshots: float32 [16384, 256], P(('cells', 'sub')), may hold values from -10 to 10, as said below
- volumes: float32 [16384], P(('cells', 'sub')), may hold values from 0.1 to 10
- live_rows: int32 [32], P(('cells', 'sub')), may hold values from 256 to 512, as said below
- probes: float32 [64, 16384], P(None, ('cells', 'sub')), may hold values from -6 to 6
Outputs:
- basis: float32 [16384, 256], P(('cells', 'sub'))
- factor: float32 [256, 256], replicated
- coefficients: float32 [64, 256], replicated
Inputs may be any that keep to these rules, and one draw needn't show every extreme that they name: `live_rows`: each entry is the live row count of one device's block of 512 row slots; live rows come first in the block. Some device has all 512 live, some has 256. `snapshots`: the columns are linearly independent.
All inputs are finite; a program needn't handle non-finite values.
Results may differ from a plain program's by a relative error of at most 0.00013.
Values sent between devices are 32-bit elements; how exact they have to be, the bound alone decides.
No kernel may reach another device: no remote copies, remote signals or barrier semaphores. Data moves between devices by JAX's collectives and lax.ppermute only.
A program may use at most 64 MiB of HBM per device.

v0:
```python
import jax
import jax.numpy as jnp
from jax import lax
from jax.sharding import PartitionSpec as P

HIGHEST = lax.Precision.HIGHEST


def reduce_all(terms):
    return lax.psum((terms[0], terms[1]), ("cells", "sub"))


def matmul(left, right):
    return jnp.dot(left, right, precision=HIGHEST, preferred_element_type=jnp.float32)


def small_cholesky(block):
    width = block.shape[0]
    positions = lax.iota(jnp.int32, width)

    def column_step(index, lower):
        unit = (positions == index).astype(jnp.float32)
        column = matmul(block, unit)
        lower_row = matmul(unit, lower)
        remain = column - matmul(lower, lower_row)
        pivot = jnp.sqrt(jnp.sum(remain * unit))
        filled = jnp.where(positions >= index, remain / pivot, jnp.float32(0.0))
        return lower + filled[:, None] * unit[None, :]

    return lax.fori_loop(0, width, column_step, jnp.zeros((width, width), jnp.float32))


def small_lower_inverse(lower):
    width = lower.shape[0]
    positions = lax.iota(jnp.int32, width)

    def row_step(index, result):
        unit = (positions == index).astype(jnp.float32)
        lower_row = matmul(unit, lower)
        pivot = jnp.sum(lower_row * unit)
        before = jnp.where(positions < index, lower_row, jnp.float32(0.0))
        solved = (unit - matmul(before, result)) / pivot
        return result + unit[:, None] * solved[None, :]

    return lax.fori_loop(0, width, row_step, jnp.zeros((width, width), jnp.float32))


def factorize(gram_matrix):
    order = gram_matrix.shape[0]
    block = 16
    count = order // block
    working = gram_matrix
    lower_full = jnp.zeros((order, order), jnp.float32)
    diagonal_inverses = []
    for outer in range(count):
        start = outer * block
        finish = start + block
        lower_block = small_cholesky(working[start:finish, start:finish])
        inverse_block = small_lower_inverse(lower_block)
        diagonal_inverses.append(inverse_block)
        lower_full = lower_full.at[start:finish, start:finish].set(lower_block)
        if finish < order:
            panel = matmul(working[finish:, start:finish], inverse_block.T)
            lower_full = lower_full.at[finish:, start:finish].set(panel)
            trailing = working[finish:, finish:] - lax.dot_general(
                panel,
                panel,
                (((1,), (1,)), ((), ())),
                precision=HIGHEST,
                preferred_element_type=jnp.float32,
            )
            working = working.at[finish:, finish:].set(trailing)
    lower_inverse = jnp.zeros((order, order), jnp.float32)
    for outer in range(count):
        start = outer * block
        finish = start + block
        lower_inverse = lower_inverse.at[start:finish, start:finish].set(diagonal_inverses[outer])
        for inner in range(outer):
            begin = inner * block
            mixed = matmul(
                lower_full[start:finish, begin:start],
                lower_inverse[begin:start, begin : begin + block],
            )
            lower_inverse = lower_inverse.at[start:finish, begin : begin + block].set(
                -matmul(diagonal_inverses[outer], mixed)
            )
    return (lower_full.T, lower_inverse.T)


def per_device(snapshots, volumes, live_rows, probes):
    row_count = snapshots.shape[0]
    total_rows = row_count * lax.axis_size("cells") * lax.axis_size("sub")
    root_total = jnp.sqrt(jnp.float32(total_rows))
    live_mask = lax.iota(jnp.int32, row_count) < live_rows[0]
    row_scale = jnp.where(live_mask, jnp.sqrt(volumes), jnp.float32(0.0))
    weighted = snapshots * row_scale[:, None]
    probe_weighted = probes * row_scale[None, :]
    gram_local = lax.dot_general(
        weighted,
        weighted,
        (((0,), (0,)), ((), ())),
        precision=HIGHEST,
        preferred_element_type=jnp.float32,
    ) / jnp.float32(total_rows)
    cross_terms = (
        jnp.dot(probe_weighted, weighted, precision=HIGHEST, preferred_element_type=jnp.float32)
        / root_total
    )
    gram_matrix, cross_total = reduce_all((gram_local, cross_terms))
    factor, inverse = factorize(gram_matrix)
    basis_block = jnp.dot(weighted, inverse, precision=HIGHEST, preferred_element_type=jnp.float32)
    coefficients = jnp.dot(
        cross_total, inverse, precision=HIGHEST, preferred_element_type=jnp.float32
    )
    return (basis_block, factor, coefficients)


def solution(mesh):
    placed = (
        P(("cells", "sub"), None),
        P(("cells", "sub")),
        P(("cells", "sub")),
        P(None, ("cells", "sub")),
    )
    return jax.shard_map(
        per_device,
        mesh=mesh,
        in_specs=placed,
        out_specs=(P(("cells", "sub"), None), P(), P()),
        check_vma=False,
    )
```

profile of v0, /device:TPU:0, one launch (start us, length us, event | category | flops | bytes accessed | tf_op | source)
XLA Modules:
  0.0 1251.7 jit_solution(12585585912450452736)
XLA Ops:
  8.0 3.1 convolution_multiply_fusion
  11.1 1.1 convolution_multiply_fusion.1
  12.5 130.1 %all-reduce.5.cloned.1.call-done = (f32[256,256]{1,0:T(8,128)}, f32[64,256]{1,0:T(8,128)}) async-done(((f32[256,256]{1,0:T(8,128)}, f32[64,256]{1,0:T(8,128)}), (f32[256,256]{1,0:T(8,128)}, f32[64,256]{1,0:T(8,128)})) %all-reduce.5.cloned.1.call-update) | async-done | bytes 327696 | tf_op jit(solution)/shard_map/psum | solution.py:10
  143.4 28.8 %while.662 = (s32[]{:T(128)}, f32[16,16]{1,0:T(8,128)S(1)}, f32[16,16]{1,0:T(8,128)S(1)}, s32[]{:T(128)}, s32[]{:T(128)}) while((s32[]{:T(128)}, f32[16,16]{1,0:T(8,128)S(1)}, f32[16,16]{1,0:T(8,128)S(1)}, s32[]{:T(128)}, s32[]{:T(128)}) %tuple.1794), condition=%wide.region_3.0_spmd.clone.clone, body=%wide.region_1.0_spmd.clone.clone.sunk | while | flops 10674 | bytes 5869 | solution.py:30
  172.2 25.4 %while.663 = (s32[]{:T(128)}, f32[16,16]{1,0:T(8,128)S(1)}, f32[16,16]{1,0:T(8,128)S(1)}, s32[]{:T(128)}, s32[]{:T(128)}) while((s32[]{:T(128)}, f32[16,16]{1,0:T(8,128)S(1)}, f32[16,16]{1,0:T(8,128)S(1)}, s32[]{:T(128)}, s32[]{:T(128)}) %tuple.1797), condition=%wide.region_6.7_spmd.clone.clone, body=%wide.region_4.6_spmd.clone.clone.sunk | while | flops 7362 | bytes 4572 | solution.py:45
  197.6 1.2 fusion.571
  199.2 28.8 %while.664 = (s32[]{:T(128)}, f32[16,16]{1,0:T(8,128)S(1)}, f32[16,16]{1,0:T(8,128)S(1)}, s32[]{:T(128)}, s32[]{:T(128)}) while((s32[]{:T(128)}, f32[16,16]{1,0:T(8,128)S(1)}, f32[16,16]{1,0:T(8,128)S(1)}, s32[]{:T(128)}, s32[]{:T(128)}) %tuple.1800), condition=%wide.region_9.10_spmd.clone.clone, body=%wide.region_7.9_spmd.clone.clone.sunk | while | flops 10674 | bytes 5869 | solution.py:30
  228.1 25.4 %while.665 = (s32[]{:T(128)}, f32[16,16]{1,0:T(8,128)S(1)}, f32[16,16]{1,0:T(8,128)S(1)}, s32[]{:T(128)}, s32[]{:T(128)}) while((s32[]{:T(128)}, f32[16,16]{1,0:T(8,128)S(1)}, f32[16,16]{1,0:T(8,128)S(1)}, s32[]{:T(128)}, s32[]{:T(128)}) %tuple.1803), condition=%wide.region_12.13_spmd.clone.clone, body=%wide.region_10.12_spmd.clone.clone.sunk | while | flops 7362 | bytes 4572 | solution.py:45
  254.2 28.8 %while.666 = (s32[]{:T(128)}, f32[16,16]{1,0:T(8,128)S(1)}, f32[16,16]{1,0:T(8,128)S(1)}, s32[]{:T(128)}, s32[]{:T(128)}) while((s32[]{:T(128)}, f32[16,16]{1,0:T(8,128)S(1)}, f32[16,16]{1,0:T(8,128)S(1)}, s32[]{:T(128)}, s32[]{:T(128)}) %tuple.1806), condition=%wide.region_15.16_spmd.clone.clone, body=%wide.region_13.15_spmd.clone.clone.sunk | while | flops 10674 | bytes 5869 | solution.py:30
  283.0 25.4 %while.667 = (s32[]{:T(128)}, f32[16,16]{1,0:T(8,128)S(1)}, f32[16,16]{1,0:T(8,128)S(1)}, s32[]{:T(128)}, s32[]{:T(128)}) while((s32[]{:T(128)}, f32[16,16]{1,0:T(8,128)S(1)}, f32[16,16]{1,0:T(8,128)S(1)}, s32[]{:T(128)}, s32[]{:T(128)}) %tuple.1809), condition=%wide.region_18.19_spmd.clone.clone, body=%wide.region_16.18_spmd.clone.clone.sunk | while | flops 7362 | bytes 4572 | solution.py:45
  309.1 28.8 %while.668 = (s32[]{:T(128)}, f32[16,16]{1,0:T(8,128)S(1)}, f32[16,16]{1,0:T(8,128)S(1)}, s32[]{:T(128)}, s32[]{:T(128)}) while((s32[]{:T(128)}, f32[16,16]{1,0:T(8,128)S(1)}, f32[16,16]{1,0:T(8,128)S(1)}, s32[]{:T(128)}, s32[]{:T(128)}) %tuple.1812), condition=%wide.region_21.22_spmd.clone.clone, body=%wide.region_19.21_spmd.clone.clone.sunk | while | flops 10674 | bytes 5869 | solution.py:30
  338.0 25.4 %while.669 = (s32[]{:T(128)}, f32[16,16]{1,0:T(8,128)S(1)}, f32[16,16]{1,0:T(8,128)S(1)}, s32[]{:T(128)}, s32[]{:T(128)}) while((s32[]{:T(128)}, f32[16,16]{1,0:T(8,128)S(1)}, f32[16,16]{1,0:T(8,128)S(1)}, s32[]{:T(128)}, s32[]{:T(128)}) %tuple.1815), condition=%wide.region_24.25_spmd.clone.clone, body=%wide.region_22.24_spmd.clone.clone.sunk | while | flops 7362 | bytes 4572 | solution.py:45
  364.0 28.8 %while.670 = (s32[]{:T(128)}, f32[16,16]{1,0:T(8,128)S(1)}, f32[16,16]{1,0:T(8,128)S(1)}, s32[]{:T(128)}, s32[]{:T(128)}) while((s32[]{:T(128)}, f32[16,16]{1,0:T(8,128)S(1)}, f32[16,16]{1,0:T(8,128)S(1)}, s32[]{:T(128)}, s32[]{:T(128)}) %tuple.1818), condition=%wide.region_27.28_spmd.clone.clone, body=%wide.region_25.27_spmd.clone.clone.sunk | while | flops 10674 | bytes 5869 | solution.py:30
  392.9 25.4 %while.671 = (s32[]{:T(128)}, f32[16,16]{1,0:T(8,128)S(1)}, f32[16,16]{1,0:T(8,128)S(1)}, s32[]{:T(128)}, s32[]{:T(128)}) while((s32[]{:T(128)}, f32[16,16]{1,0:T(8,128)S(1)}, f32[16,16]{1,0:T(8,128)S(1)}, s32[]{:T(128)}, s32[]{:T(128)}) %tuple.1821), condition=%wide.region_30.31_spmd.clone.clone, body=%wide.region_28.30_spmd.clone.clone.sunk | while | flops 7362 | bytes 4572 | solution.py:45
  418.9 28.8 %while.672 = (s32[]{:T(128)}, f32[16,16]{1,0:T(8,128)S(1)}, f32[16,16]{1,0:T(8,128)S(1)}, s32[]{:T(128)}, s32[]{:T(128)}) while((s32[]{:T(128)}, f32[16,16]{1,0:T(8,128)S(1)}, f32[16,16]{1,0:T(8,128)S(1)}, s32[]{:T(128)}, s32[]{:T(128)}) %tuple.1824), condition=%wide.region_33.34_spmd.clone.clone, body=%wide.region_31.33_spmd.clone.clone.sunk | while | flops 10674 | bytes 5869 | solution.py:30
  447.8 25.4 %while.673 = (s32[]{:T(128)}, f32[16,16]{1,0:T(8,128)S(1)}, f32[16,16]{1,0:T(8,128)S(1)}, s32[]{:T(128)}, s32[]{:T(128)}) while((s32[]{:T(128)}, f32[16,16]{1,0:T(8,128)S(1)}, f32[16,16]{1,0:T(8,128)S(1)}, s32[]{:T(128)}, s32[]{:T(128)}) %tuple.1827), condition=%wide.region_36.37_spmd.clone.clone, body=%wide.region_34.36_spmd.clone.clone.sunk | while | flops 7362 | bytes 4572 | solution.py:45
  473.8 28.8 %while.674 = (s32[]{:T(128)}, f32[16,16]{1,0:T(8,128)S(1)}, f32[16,16]{1,0:T(8,128)S(1)}, s32[]{:T(128)}, s32[]{:T(128)}) while((s32[]{:T(128)}, f32[16,16]{1,0:T(8,128)S(1)}, f32[16,16]{1,0:T(8,128)S(1)}, s32[]{:T(128)}, s32[]{:T(128)}) %tuple.1830), condition=%wide.region_39.40_spmd.clone.clone, body=%wide.region_37.39_spmd.clone.clone.sunk | while | flops 10674 | bytes 5869 | solution.py:30
  502.6 25.4 %while.675 = (s32[]{:T(128)}, f32[16,16]{1,0:T(8,128)S(1)}, f32[16,16]{1,0:T(8,128)S(1)}, s32[]{:T(128)}, s32[]{:T(128)}) while((s32[]{:T(128)}, f32[16,16]{1,0:T(8,128)S(1)}, f32[16,16]{1,0:T(8,128)S(1)}, s32[]{:T(128)}, s32[]{:T(128)}) %tuple.1833), condition=%wide.region_42.43_spmd.clone.clone, body=%wide.region_40.42_spmd.clone.clone.sunk | while | flops 7362 | bytes 4572 | solution.py:45
  528.6 28.8 %while.676 = (s32[]{:T(128)}, f32[16,16]{1,0:T(8,128)S(1)}, f32[16,16]{1,0:T(8,128)S(1)}, s32[]{:T(128)}, s32[]{:T(128)}) while((s32[]{:T(128)}, f32[16,16]{1,0:T(8,128)S(1)}, f32[16,16]{1,0:T(8,128)S(1)}, s32[]{:T(128)}, s32[]{:T(128)}) %tuple.1836), condition=%wide.region_45.46_spmd.clone.clone, body=%wide.region_43.45_spmd.clone.clone.sunk | while | flops 10674 | bytes 5869 | solution.py:30
  557.5 25.4 %while.677 = (s32[]{:T(128)}, f32[16,16]{1,0:T(8,128)S(1)}, f32[16,16]{1,0:T(8,128)S(1)}, s32[]{:T(128)}, s32[]{:T(128)}) while((s32[]{:T(128)}, f32[16,16]{1,0:T(8,128)S(1)}, f32[16,16]{1,0:T(8,128)S(1)}, s32[]{:T(128)}, s32[]{:T(128)}) %tuple.1839), condition=%wide.region_48.49_spmd.clone.clone, body=%wide.region_46.48_spmd.clone.clone.sunk | while | flops 7362 | bytes 4572 | solution.py:45
  583.8 1.0 scatter.564
  585.7 1.0 scatter.566
  587.6 1.0 scatter.570
  589.5 1.0 scatter.574
  591.4 1.0 scatter.576
  593.3 1.0 scatter.580
  595.3 1.0 scatter.584
  596.8 28.8 %while.678 = (s32[]{:T(128)}, f32[16,16]{1,0:T(8,128)S(1)}, f32[16,16]{1,0:T(8,128)S(1)}, s32[]{:T(128)}, s32[]{:T(128)}) while((s32[]{:T(128)}, f32[16,16]{1,0:T(8,128)S(1)}, f32[16,16]{1,0:T(8,128)S(1)}, s32[]{:T(128)}, s32[]{:T(128)}) %tuple.1842), condition=%wide.region_51.52_spmd.clone.clone, body=%wide.region_49.51_spmd.clone.clone.sunk | while | flops 10674 | bytes 5869 | solution.py:30
  625.6 25.4 %while.679 = (s32[]{:T(128)}, f32[16,16]{1,0:T(8,128)S(1)}, f32[16,16]{1,0:T(8,128)S(1)}, s32[]{:T(128)}, s32[]{:T(128)}) while((s32[]{:T(128)}, f32[16,16]{1,0:T(8,128)S(1)}, f32[16,16]{1,0:T(8,128)S(1)}, s32[]{:T(128)}, s32[]{:T(128)}) %tuple.1845), condition=%wide.region_54.55_spmd.clone.clone, body=%wide.region_52.54_spmd.clone.clone.sunk | while | flops 7362 | bytes 4572 | solution.py:45
  651.5 28.8 %while.680 = (s32[]{:T(128)}, f32[16,16]{1,0:T(8,128)S(1)}, f32[16,16]{1,0:T(8,128)S(1)}, s32[]{:T(128)}, s32[]{:T(128)}) while((s32[]{:T(128)}, f32[16,16]{1,0:T(8,128)S(1)}, f32[16,16]{1,0:T(8,128)S(1)}, s32[]{:T(128)}, s32[]{:T(128)}) %tuple.1848), condition=%wide.region_57.58_spmd.clone.clone, body=%wide.region_55.57_spmd.clone.clone.sunk | while | flops 10674 | bytes 5869 | solution.py:30
  680.2 25.4 %while.681 = (s32[]{:T(128)}, f32[16,16]{1,0:T(8,128)S(1)}, f32[16,16]{1,0:T(8,128)S(1)}, s32[]{:T(128)}, s32[]{:T(128)}) while((s32[]{:T(128)}, f32[16,16]{1,0:T(8,128)S(1)}, f32[16,16]{1,0:T(8,128)S(1)}, s32[]{:T(128)}, s32[]{:T(128)}) %tuple.1851), condition=%wide.region_60.61_spmd.clone.clone, body=%wide.region_58.60_spmd.clone.clone.sunk | while | flops 7362 | bytes 4572 | solution.py:45
  706.1 28.8 %while.682 = (s32[]{:T(128)}, f32[16,16]{1,0:T(8,128)S(1)}, f32[16,16]{1,0:T(8,128)S(1)}, s32[]{:T(128)}, s32[]{:T(128)}) while((s32[]{:T(128)}, f32[16,16]{1,0:T(8,128)S(1)}, f32[16,16]{1,0:T(8,128)S(1)}, s32[]{:T(128)}, s32[]{:T(128)}) %tuple.1854), condition=%wide.region_63.64_spmd.clone.clone, body=%wide.region_61.63_spmd.clone.clone.sunk | while | flops 10674 | bytes 5869 | solution.py:30
  734.9 25.4 %while.683 = (s32[]{:T(128)}, f32[16,16]{1,0:T(8,128)S(1)}, f32[16,16]{1,0:T(8,128)S(1)}, s32[]{:T(128)}, s32[]{:T(128)}) while((s32[]{:T(128)}, f32[16,16]{1,0:T(8,128)S(1)}, f32[16,16]{1,0:T(8,128)S(1)}, s32[]{:T(128)}, s32[]{:T(128)}) %tuple.1857), condition=%wide.region_66.67_spmd.clone.clone, body=%wide.region_64.66_spmd.clone.clone.sunk | while | flops 7362 | bytes 4572 | solution.py:45
  760.8 28.8 %while.684 = (s32[]{:T(128)}, f32[16,16]{1,0:T(8,128)S(1)}, f32[16,16]{1,0:T(8,128)S(1)}, s32[]{:T(128)}, s32[]{:T(128)}) while((s32[]{:T(128)}, f32[16,16]{1,0:T(8,128)S(1)}, f32[16,16]{1,0:T(8,128)S(1)}, s32[]{:T(128)}, s32[]{:T(128)}) %tuple.1860), condition=%wide.region_69.70_spmd.clone.clone, body=%wide.region_67.69_spmd.clone.clone.sunk | while | flops 10674 | bytes 5869 | solution.py:30
  789.5 25.7 %while.685 = (s32[]{:T(128)}, f32[16,16]{1,0:T(8,128)S(1)}, f32[16,16]{1,0:T(8,128)S(1)}, s32[]{:T(128)}, s32[]{:T(128)}) while((s32[]{:T(128)}, f32[16,16]{1,0:T(8,128)S(1)}, f32[16,16]{1,0:T(8,128)S(1)}, s32[]{:T(128)}, s32[]{:T(128)}) %tuple.1863), condition=%wide.region_72.73_spmd.clone.clone, body=%wide.region_70.72_spmd.clone.clone.sunk | while | flops 7362 | bytes 4572 | solution.py:45
  815.7 28.8 %while.686 = (s32[]{:T(128)}, f32[16,16]{1,0:T(8,128)S(1)}, f32[16,16]{1,0:T(8,128)S(1)}, s32[]{:T(128)}, s32[]{:T(128)}) while((s32[]{:T(128)}, f32[16,16]{1,0:T(8,128)S(1)}, f32[16,16]{1,0:T(8,128)S(1)}, s32[]{:T(128)}, s32[]{:T(128)}) %tuple.1866), condition=%wide.region_75.76_spmd.clone.clone, body=%wide.region_73.75_spmd.clone.clone.sunk | while | flops 10674 | bytes 5869 | solution.py:30
  844.5 25.4 %while.687 = (s32[]{:T(128)}, f32[16,16]{1,0:T(8,128)S(1)}, f32[16,16]{1,0:T(8,128)S(1)}, s32[]{:T(128)}, s32[]{:T(128)}) while((s32[]{:T(128)}, f32[16,16]{1,0:T(8,128)S(1)}, f32[16,16]{1,0:T(8,128)S(1)}, s32[]{:T(128)}, s32[]{:T(128)}) %tuple.1869), condition=%wide.region_78.79_spmd.clone.clone, body=%wide.region_76.78_spmd.clone.clone.sunk | while | flops 7362 | bytes 4572 | solution.py:45
  870.3 28.8 %while.688 = (s32[]{:T(128)}, f32[16,16]{1,0:T(8,128)S(1)}, f32[16,16]{1,0:T(8,128)S(1)}, s32[]{:T(128)}, s32[]{:T(128)}) while((s32[]{:T(128)}, f32[16,16]{1,0:T(8,128)S(1)}, f32[16,16]{1,0:T(8,128)S(1)}, s32[]{:T(128)}, s32[]{:T(128)}) %tuple.1872), condition=%wide.region_81.82_spmd.clone.clone, body=%wide.region_79.81_spmd.clone.clone.sunk | while | flops 10674 | bytes 5869 | solution.py:30
  899.1 25.4 %while.689 = (s32[]{:T(128)}, f32[16,16]{1,0:T(8,128)S(1)}, f32[16,16]{1,0:T(8,128)S(1)}, s32[]{:T(128)}, s32[]{:T(128)}) while((s32[]{:T(128)}, f32[16,16]{1,0:T(8,128)S(1)}, f32[16,16]{1,0:T(8,128)S(1)}, s32[]{:T(128)}, s32[]{:T(128)}) %tuple.1875), condition=%wide.region_84.85_spmd.clone.clone, body=%wide.region_82.84_spmd.clone.clone.sunk | while | flops 7362 | bytes 4572 | solution.py:45
  924.9 28.8 %while.690 = (s32[]{:T(128)}, f32[16,16]{1,0:T(8,128)S(1)}, f32[16,16]{1,0:T(8,128)S(1)}, s32[]{:T(128)}, s32[]{:T(128)}) while((s32[]{:T(128)}, f32[16,16]{1,0:T(8,128)S(1)}, f32[16,16]{1,0:T(8,128)S(1)}, s32[]{:T(128)}, s32[]{:T(128)}) %tuple.1878), condition=%wide.region_87.88_spmd.clone.clone, body=%wide.region_85.87_spmd.clone.clone.sunk | while | flops 10674 | bytes 5869 | solution.py:30
  953.6 25.4 %while.691 = (s32[]{:T(128)}, f32[16,16]{1,0:T(8,128)S(1)}, f32[16,16]{1,0:T(8,128)S(1)}, s32[]{:T(128)}, s32[]{:T(128)}) while((s32[]{:T(128)}, f32[16,16]{1,0:T(8,128)S(1)}, f32[16,16]{1,0:T(8,128)S(1)}, s32[]{:T(128)}, s32[]{:T(128)}) %tuple.1881), condition=%wide.region_90.91_spmd.clone.clone, body=%wide.region_88.90_spmd.clone.clone.sunk | while | flops 7362 | bytes 4572 | solution.py:45
  979.9 28.8 %while.692 = (s32[]{:T(128)}, f32[16,16]{1,0:T(8,128)S(1)}, f32[16,16]{1,0:T(8,128)S(1)}, s32[]{:T(128)}, s32[]{:T(128)}) while((s32[]{:T(128)}, f32[16,16]{1,0:T(8,128)S(1)}, f32[16,16]{1,0:T(8,128)S(1)}, s32[]{:T(128)}, s32[]{:T(128)}) %tuple.1884), condition=%wide.region_93.94_spmd.clone.clone, body=%wide.region_91.93_spmd.clone.clone.sunk | while | flops 10674 | bytes 5869 | solution.py:30
  1031.8 1.2 scatter.625
  1063.8 1.2 scatter.664
  1093.5 1.2 scatter.700
  1125.5 1.0 scatter.739
  1155.6 1.2 scatter.774
  1183.9 25.4 %while.693 = (s32[]{:T(128)}, f32[16,16]{1,0:T(8,128)S(1)}, f32[16,16]{1,0:T(8,128)S(1)}, s32[]{:T(128)}, s32[]{:T(128)}) while((s32[]{:T(128)}, f32[16,16]{1,0:T(8,128)S(1)}, f32[16,16]{1,0:T(8,128)S(1)}, s32[]{:T(128)}, s32[]{:T(128)}) %tuple.1887), condition=%wide.region_96.97_spmd.clone.clone, body=%wide.region_94.96_spmd.clone.clone.sunk | while | flops 7362 | bytes 4572 | solution.py:45
  1210.3 1.3 fusion.568
  1212.4 1.3 fusion.573
  1214.8 1.3 fusion.581
  1217.1 1.2 fusion.592
  1219.4 1.2 fusion.606
  1221.7 1.2 fusion.623
  1224.0 1.2 fusion.643
  1226.3 1.1 fusion.666
  1228.5 1.1 fusion.693
  1230.3 1.1 fusion.722
  1232.4 1.1 fusion.754
  1234.4 1.0 fusion.789
  1236.4 1.0 fusion.827
  1238.4 1.0 fusion.868
  1242.0 1.4 fusion.561
  1243.4 1.0 fusion.959
  (3166 shorter events, 883.2 us)
Async XLA Ops:
  7.2 0.8 copy-start.5
  7.2 3.9 copy-start.1
  7.2 135.5 %all-reduce.5.cloned.1.call-start = ((), (), s32[]{:S(2)}) async-start(), calls=%async_computation | async-start | bytes 655360 | tf_op jit(solution)/shard_map/psum | solution.py:10
  8.0 3.1 copy-start.3
  143.4 55.5 %copy-start.2 = (f32[256,256]{1,0:T(8,128)S(1)}, f32[256,256]{1,0:T(8,128)}, u32[]{:S(2)}) copy-start(f32[256,256]{1,0:T(8,128)} %get-tuple-element.5867) | copy-start | bytes 786436
  1021.7 160.9 %copy-start = (f32[256,256]{0,1:T(8,128)}, f32[256,256]{0,1:T(8,128)S(1)}, u32[]{:S(2)}) copy-start(f32[256,256]{0,1:T(8,128)S(1)} %scatter.610) | copy-start | bytes 786436
  1242.0 1.4 copy-start.4
Sparse Core Ops, SparseCore 0:
  14.0 128.6 all-reduce.4
where the time goes:
time: 1270 us; the launch traced here: 1250 us
  matrix products  728 us (57%)
  loops' own time  185 us (15%)
  local copies, waits for them, and re-layouts  149 us (12%)
  waiting for transfers between devices  130 us (10%)
  other arithmetic  42 us (3%)
  between operations  17.3 us (1%)
    dot_general x1535, matrix products, matmul(): jnp.dot(left, right, precision=HIGHEST, preferred_element_type=jnp.float32)  717 us
    another operation x16, loops' own time, small_cholesky(): lax.fori_loop(0, width, column_step, jnp.zeros((width, width), jnp.float32))  182 us
    psum x1, waiting for transfers between devices, reduce_all(): return lax.psum((terms[0], terms[1]), ('cells', 'sub'))  130 us
    scatter x120, local copies, waits for them, and re-layouts, factorize(): lower_inverse.at[start:finish, begin:begin + block]  99.4 us
  transfers between devices with their start and end apart: 1, of which 1 were waited for; matrix products, arithmetic and copies ran while one was open for 0% of the time, Pallas kernels for 0%

commit v1 on v0

v1 whole, which is shorter than its diff:
```python
import functools
import jax
import jax.numpy as jnp
from jax import lax
from jax.experimental import pallas as pl
from jax.experimental.pallas import tpu as pltpu
from jax.sharding import PartitionSpec as P

HIGHEST = lax.Precision.HIGHEST
LANES = 128
BLOCK = 8
F32 = jnp.float32


def recip(value):
    guess = pl.reciprocal(value, approx=True)
    guess = guess * (2.0 - value * guess)
    return guess * (2.0 - value * guess)


def lanes_of(tile, column):
    return jnp.broadcast_to(tile[:, column : column + 1], (BLOCK, LANES))


def row_of(tile, index):
    return jnp.broadcast_to(tile[index : index + 1, :], (BLOCK, LANES))


def eliminate(work, factor_ref, linv_ref, order, panel):
    tiles = order // LANES
    sub_ids = lax.broadcasted_iota(jnp.int32, (BLOCK, LANES), 0)
    lane_ids = lax.broadcasted_iota(jnp.int32, (BLOCK, LANES), 1)
    zero = jnp.zeros((BLOCK, LANES), F32)
    one = jnp.ones((BLOCK, LANES), F32)

    def load(row, tile):
        return work[row : row + BLOCK, tile * LANES : (tile + 1) * LANES]

    for start in range(0, order, BLOCK):
        first = (start // panel) * panel
        last = first + panel
        home, offset = start // LANES, start % LANES
        in_block = (lane_ids >= offset) & (lane_ids < offset + BLOCK)
        own = [load(start, t) for t in range(tiles)]
        diag_tile = own[home]
        columns = [lanes_of(diag_tile, offset + c) for c in range(BLOCK)]
        entry = {(r, c): row_of(columns[c], r) for c in range(BLOCK) for r in range(c + 1)}
        rows = [[row_of(own[t], r) for t in range(tiles)] for r in range(BLOCK)]
        kept = [rows[r][home] for r in range(BLOCK)]
        for r in range(BLOCK):
            rows[r][home] = jnp.where(in_block, jnp.where(lane_ids == offset + r, one, zero), rows[r][home])
        ahead = start + BLOCK
        follows = ahead < last
        if follows:
            below = [load(ahead, t) for t in range(tiles)]
            below_columns = [lanes_of(below[home], offset + c) for c in range(BLOCK)]
            below[home] = jnp.where(in_block, zero, below[home])
        inverse_pivot, scaled = [], {}
        for i in range(BLOCK):
            inv = recip(entry[i, i])
            inverse_pivot.append(inv)
            for r in range(i + 1, BLOCK):
                scaled[r, i] = entry[i, r] * inv
            for r in range(i + 1, BLOCK):
                for c in range(r, BLOCK):
                    entry[r, c] = entry[r, c] - scaled[r, i] * entry[i, c]
            if follows:
                weight = below_columns[i] * inv
                for c in range(i + 1, BLOCK):
                    below_columns[c] = below_columns[c] - below_columns[i] * scaled[c, i]
                for t in range(tiles):
                    below[t] = below[t] - weight * rows[i][t]
            for r in range(i + 1, BLOCK):
                for t in range(tiles):
                    rows[r][t] = rows[r][t] - scaled[r, i] * rows[i][t]
                kept[r] = kept[r] - scaled[r, i] * kept[i]
        if follows:
            for t in range(tiles):
                work[ahead : ahead + BLOCK, t * LANES : (t + 1) * LANES] = below[t]
        roots = [jnp.sqrt(entry[i, i]) * inverse_pivot[i] for i in range(BLOCK)]

        def gather(parts):
            total = parts[0]
            for r in range(1, BLOCK):
                total = jnp.where(sub_ids == r, parts[r], total)
            return total

        root = gather(roots)
        for t in range(tiles):
            merged = gather([rows[r][t] for r in range(BLOCK)]) * root
            column_ids = lane_ids + t * LANES
            lower = jnp.where(column_ids <= start + sub_ids, merged, zero)
            if t == home:
                merged_kept = gather(kept) * root
                upper = jnp.where(in_block, merged_kept, merged)
            else:
                upper = merged
            upper = jnp.where(column_ids >= start + sub_ids, upper, zero)
            factor_ref[start : start + BLOCK, t * LANES : (t + 1) * LANES] = upper
            linv_ref[start : start + BLOCK, t * LANES : (t + 1) * LANES] = lower
        if ahead + BLOCK < last:
            solved = [None] * BLOCK
            for r in reversed(range(BLOCK)):
                solved[r] = [rows[r][t] * inverse_pivot[r] for t in range(tiles)]
                for c in range(r + 1, BLOCK):
                    for t in range(tiles):
                        solved[r][t] = solved[r][t] - scaled[c, r] * solved[c][t]
            for row in range(ahead + BLOCK, last, BLOCK):
                target = [load(row, t) for t in range(tiles)]
                source = target[home]
                target[home] = jnp.where(in_block, zero, source)
                for c in range(BLOCK):
                    weight = lanes_of(source, offset + c)
                    for t in range(tiles):
                        target[t] = target[t] - weight * solved[c][t]
                for t in range(tiles):
                    work[row : row + BLOCK, t * LANES : (t + 1) * LANES] = target[t]
        if ahead == last and last < order:
            left = factor_ref[first:last, last:]
            mixed = jnp.concatenate([linv_ref[first:last, :last], factor_ref[first:last, last:]], axis=1)
            product = lax.dot_general(
                left, mixed, (((0,), (0,)), ((), ())), precision=HIGHEST, preferred_element_type=F32
            )
            ids = lax.broadcasted_iota(jnp.int32, (order - last, order), 1)
            previous = jnp.where((ids >= first) & (ids < last), 0.0, work[last:, :])
            work[last:, :] = previous - product


def finish_kernel(panel, gram_ref, cross_ref, weighted_ref, basis_ref, factor_ref, coef_ref, work, linv):
    order = gram_ref.shape[0]
    work[...] = gram_ref[...]
    eliminate(work, factor_ref, linv, order, panel)
    dims = (((1,), (1,)), ((), ()))
    basis_ref[...] = lax.dot_general(
        weighted_ref[...], linv[...], dims, precision=HIGHEST, preferred_element_type=F32
    )
    coef_ref[...] = lax.dot_general(
        cross_ref[...], linv[...], dims, precision=HIGHEST, preferred_element_type=F32
    )


def finish(gram, cross, weighted, panel=128):
    order = gram.shape[0]
    rows, probes = weighted.shape[0], cross.shape[0]
    whole = pl.BlockSpec(memory_space=pltpu.VMEM)
    return pl.pallas_call(
        functools.partial(finish_kernel, panel),
        out_shape=(
            jax.ShapeDtypeStruct((rows, order), F32),
            jax.ShapeDtypeStruct((order, order), F32),
            jax.ShapeDtypeStruct((probes, order), F32),
        ),
        in_specs=[whole] * 3,
        out_specs=(whole,) * 3,
        scratch_shapes=[pltpu.VMEM((order, order), F32), pltpu.VMEM((order, order), F32)],
        compiler_params=pltpu.CompilerParams(vmem_limit_bytes=32 * 1024 * 1024),
    )(gram, cross, weighted)


def exchange(value, axis, bit):
    size = lax.axis_size(axis)
    return lax.ppermute(value, axis, [(i, i ^ bit) for i in range(size)])


def reduce_all(value):
    half = value.shape[0] // 2
    core = lax.axis_index("sub") % 2
    low, high = value[:half], value[half:]
    mine = jnp.where(core == 0, low, high)
    mine = mine + exchange(jnp.where(core == 0, high, low), "sub", 1)
    for axis, begin in (("cells", 1), ("sub", 2)):
        bit = begin
        while bit < lax.axis_size(axis):
            mine = mine + exchange(mine, axis, bit)
            bit *= 2
    other = exchange(mine, "sub", 1)
    low = jnp.where(core == 0, mine, other)
    high = jnp.where(core == 0, other, mine)
    return jnp.concatenate([low, high], axis=0)


def per_device(snapshots, volumes, live_rows, probes):
    row_count, order = snapshots.shape
    total_rows = row_count * lax.axis_size("cells") * lax.axis_size("sub")
    root_total = jnp.sqrt(jnp.float32(total_rows))
    live_mask = lax.iota(jnp.int32, row_count) < live_rows[0]
    row_scale = jnp.where(live_mask, jnp.sqrt(volumes), jnp.float32(0.0))
    weighted = snapshots * row_scale[:, None]
    probe_weighted = probes * row_scale[None, :]
    gram_local = lax.dot_general(
        weighted, weighted, (((0,), (0,)), ((), ())), precision=HIGHEST, preferred_element_type=F32
    ) / jnp.float32(total_rows)
    cross_local = jnp.dot(probe_weighted, weighted, precision=HIGHEST, preferred_element_type=F32) / root_total
    total = reduce_all(jnp.concatenate([gram_local, cross_local], axis=0))
    return finish(total[:order], total[order:], weighted)


def solution(mesh):
    placed = (
        P(("cells", "sub"), None),
        P(("cells", "sub")),
        P(("cells", "sub")),
        P(None, ("cells", "sub")),
    )
    return jax.shard_map(
        per_device,
        mesh=mesh,
        in_specs=placed,
        out_specs=(P(("cells", "sub"), None), P(), P()),
        check_vma=False,
    )
```

time: 1270 us -> 47.8 us (0.04); the launches traced: 1250 us -> 47.6 us
  matrix products: 728 us -> 1.42 us
  loops' own time: 185 us -> 0 us
  local copies, waits for them, and re-layouts: 149 us -> 0.03 us
  waiting for transfers between devices: 130 us -> 20.2 us
  other arithmetic: 42 us -> 1.35 us
  between operations: 17.3 us -> 1.4 us
  Pallas kernels: 0 us -> 13.6 us
    dot_general x1552 -> x0, matrix products: 724 us -> none  [the longest x1535 717 us: matmul(): jnp.dot(left, right, precision=HIGHEST, preferred_element_type=jnp.float32)]
    another operation x32 -> x0, loops' own time: 185 us -> none  [the longest x16 182 us: small_cholesky(): lax.fori_loop(0, width, column_step, jnp.zeros((width, width), jnp.float32))]
    scatter x166 -> x0, local copies, waits for them, and re-layouts: 139 us -> none  [the longest x120 99.4 us: factorize(): lower_inverse.at[start:finish, begin:begin + block]]
    psum x1 -> x0, waiting for transfers between devices: 130 us -> none  [reduce_all(): return lax.psum((terms[0], terms[1]), ('cells', 'sub'))]
    add x512 -> x5, other arithmetic: 38.7 us -> 0.11 us  [the longest x4 0.08 us: reduce_all(): mine = mine + exchange(mine, axis, bit)]
    ppermute x0 -> x6, waiting for transfers between devices: none -> 20.2 us  [exchange(): return lax.ppermute(value, axis, [(i, i ^ bit) for i in range(size)])]
    pallas_call x0 -> x1, Pallas kernels: none -> 13.6 us  [finish(): pl.pallas_call(functools.partial(finish_kernel, panel), out_shape=(jax.Sh...]
  transfers between devices with their start and end apart: 1 -> 6, of which waited for: 1 -> 6; matrix products, arithmetic and copies ran while one was open for 0% -> 0% of each run, Pallas kernels for 0% -> 0%
where the time goes in v1:
time: 47.8 us; the launch traced here: 47.6 us
  waiting for transfers between devices  20.2 us (42%)
  Pallas kernels  13.6 us (28%)
  starting transfers between devices  9.62 us (20%)
  matrix products  1.42 us (3%)
  between operations  1.4 us (3%)
  other arithmetic  1.35 us (3%)
    ppermute x6, waiting for transfers between devices, exchange(): return lax.ppermute(value, axis, [(i, i ^ bit) for i in range(size)])  20.2 us
    pallas_call x1, Pallas kernels, finish(): pl.pallas_call(functools.partial(finish_kernel, panel), out_shape=(jax.Sh...  13.6 us
    ppermute x6, starting transfers between devices, exchange(): return lax.ppermute(value, axis, [(i, i ^ bit) for i in range(size)])  9.62 us
    mul x1, other arithmetic, per_device(): weighted = snapshots * row_scale[:, None]  1.17 us
    dot_general x1, matrix products, per_device(): lax.dot_general(weighted, weighted, (((0,), (0,)), ((), ())), precision=H...  1.02 us
  transfers between devices with their start and end apart: 6, of which 6 were waited for; matrix products, arithmetic and copies ran while one was open for 0% of the time, Pallas kernels for 0%

profile of v1, /device:TPU:0, one launch (start us, length us, event | category | flops | bytes accessed | tf_op | source)
XLA Modules:
  0.0 47.6 jit_solution(7284501815925187640)
XLA Ops:
  0.6 0.0 copy-start.1
  1.3 0.0 copy-done.1
  1.3 1.2 %broadcast_multiply_fusion.weighted_ref = f32[512,256]{1,0:T(8,128)S(1)} fusion(f32[512,256]{1,0:T(8,128)} %param.4, f32[512]{0:T(512)S(1)} %sqrt_select_fusion), kind=kLoop, calls=%fused_computation.3 | loop fusion | flops 131072 | bytes 1050624 | tf_op jit(solution)/shard_map/mul | solution.py:188
  2.5 0.0 copy-start
  2.5 1.0 %convolution_multiply_fusion = f32[256,256]{1,0:T(8,128)S(1)} fusion(f32[512,256]{1,0:T(8,128)S(1)} %broadcast_multiply_fusion.weighted_ref), kind=kOutput, calls=%fused_computation | convolution fusion | flops 402718720 | bytes 786432 | tf_op jit(solution)/shard_map/dot_general | solution.py:190
  3.6 0.0 copy-done
  3.6 0.4 convolution_multiply_fusion.1
  4.0 0.5 %collective-permute-start = (f32[160,256]{1,0:T(8,128)S(1)}, f32[160,256]{1,0:T(8,128)S(1)}, u32[]{:S(2)}, u32[]{:S(2)}) collective-permute-start(f32[160,256]{1,0:T(8,128)S(1)} %slice_select_fusion), channel_id=1, source_target_pairs={{0,1},{1,0},{2,3},{3,2},{4,5},{5,4},{6,7},{7,6},{8,9},{9,8},{10,11... | collective-permute-start | bytes 491528 | tf_op jit(solution)/shard_map/ppermute | solution.py:162
  4.5 1.0 %collective-permute-done = f32[160,256]{1,0:T(8,128)S(1)} collective-permute-done((f32[160,256]{1,0:T(8,128)S(1)}, f32[160,256]{1,0:T(8,128)S(1)}, u32[]{:S(2)}, u32[]{:S(2)}) %collective-permute-start) | collective-permute-done | bytes 163872 | tf_op jit(solution)/shard_map/ppermute | solution.py:162
  5.6 2.9 %collective-permute-start.1 = (f32[160,256]{1,0:T(8,128)S(1)}, f32[160,256]{1,0:T(8,128)S(1)}, u32[]{:S(2)}, u32[]{:S(2)}) collective-permute-start(f32[160,256]{1,0:T(8,128)S(1)} %select_add_fusion), channel_id=1, source_target_pairs={{0,2},{2,0},{4,6},{6,4},{8,10},{10,8},{12,14},{14,12},{16,18},{18,... | collective-permute-start | bytes 491528 | tf_op jit(solution)/shard_map/ppermute | solution.py:162
  8.5 4.5 %collective-permute-done.1 = f32[160,256]{1,0:T(8,128)S(1)} collective-permute-done((f32[160,256]{1,0:T(8,128)S(1)}, f32[160,256]{1,0:T(8,128)S(1)}, u32[]{:S(2)}, u32[]{:S(2)}) %collective-permute-start.1) | collective-permute-done | bytes 163872 | tf_op jit(solution)/shard_map/ppermute | solution.py:162
  13.0 1.8 %collective-permute-start.2 = (f32[160,256]{1,0:T(8,128)S(1)}, f32[160,256]{1,0:T(8,128)S(1)}, u32[]{:S(2)}, u32[]{:S(2)}) collective-permute-start(f32[160,256]{1,0:T(8,128)S(1)} %add.21), channel_id=1, source_target_pairs={{0,4},{2,6},{4,0},{6,2},{8,12},{10,14},{12,8},{14,10},{16,20},{18,... | collective-permute-start | bytes 491528 | tf_op jit(solution)/shard_map/ppermute | solution.py:162
  14.9 4.0 %collective-permute-done.2 = f32[160,256]{1,0:T(8,128)S(1)} collective-permute-done((f32[160,256]{1,0:T(8,128)S(1)}, f32[160,256]{1,0:T(8,128)S(1)}, u32[]{:S(2)}, u32[]{:S(2)}) %collective-permute-start.2) | collective-permute-done | bytes 163872 | tf_op jit(solution)/shard_map/ppermute | solution.py:162
  18.8 1.6 %collective-permute-start.3 = (f32[160,256]{1,0:T(8,128)S(1)}, f32[160,256]{1,0:T(8,128)S(1)}, u32[]{:S(2)}, u32[]{:S(2)}) collective-permute-start(f32[160,256]{1,0:T(8,128)S(1)} %add.22), channel_id=1, source_target_pairs={{0,8},{2,10},{4,12},{6,14},{8,0},{10,2},{12,4},{14,6},{16,24},{18,... | collective-permute-start | bytes 491528 | tf_op jit(solution)/shard_map/ppermute | solution.py:162
  20.4 3.8 %collective-permute-done.3 = f32[160,256]{1,0:T(8,128)S(1)} collective-permute-done((f32[160,256]{1,0:T(8,128)S(1)}, f32[160,256]{1,0:T(8,128)S(1)}, u32[]{:S(2)}, u32[]{:S(2)}) %collective-permute-start.3) | collective-permute-done | bytes 163872 | tf_op jit(solution)/shard_map/ppermute | solution.py:162
  24.3 2.7 %collective-permute-start.4 = (f32[160,256]{1,0:T(8,128)S(1)}, f32[160,256]{1,0:T(8,128)S(1)}, u32[]{:S(2)}, u32[]{:S(2)}) collective-permute-start(f32[160,256]{1,0:T(8,128)S(1)} %add.23), channel_id=1, source_target_pairs={{0,16},{2,18},{4,20},{6,22},{8,24},{10,26},{12,28},{14,30},{16,0},... | collective-permute-start | bytes 491528 | tf_op jit(solution)/shard_map/ppermute | solution.py:162
  27.0 5.5 %collective-permute-done.4 = f32[160,256]{1,0:T(8,128)S(1)} collective-permute-done((f32[160,256]{1,0:T(8,128)S(1)}, f32[160,256]{1,0:T(8,128)S(1)}, u32[]{:S(2)}, u32[]{:S(2)}) %collective-permute-start.4) | collective-permute-done | bytes 163872 | tf_op jit(solution)/shard_map/ppermute | solution.py:162
  32.4 0.1 collective-permute-start.5
  32.5 1.4 %collective-permute-done.5 = f32[160,256]{1,0:T(8,128)S(1)} collective-permute-done((f32[160,256]{1,0:T(8,128)S(1)}, f32[160,256]{1,0:T(8,128)S(1)}, u32[]{:S(2)}, u32[]{:S(2)}) %collective-permute-start.5) | collective-permute-done | bytes 163872 | tf_op jit(solution)/shard_map/ppermute | solution.py:162
  34.0 13.6 %shard_map.67 = (f32[512,256]{1,0:T(8,128)}, f32[256,256]{1,0:T(8,128)}, f32[64,256]{1,0:T(8,128)}) custom-call(f32[256,256]{1,0:T(8,128)S(1)} %pad_maximum_fusion.gram_ref, f32[64,256]{1,0:T(8,128)S(1)} %slice.17.cross_ref, f32[512,256]{1,0:T(8,128)S(1)} %broadcast_multiply_fusion.weighted_ref), custom_call_target="tpu_custom_call" | custom-call | tf_op jit(solution)/shard_map/pallas_call | solution.py:146
  (10 shorter events, 0.2 us)
Async XLA Ops:
  0.6 0.7 %copy-start.1 = (f32[512]{0:T(512)S(1)}, f32[512]{0:T(512)}, u32[]{:S(2)}) copy-start(f32[512]{0:T(512)} %param.5) | copy-start | bytes 6148
  2.5 1.0 %copy-start = (f32[64,512]{1,0:T(8,128)S(1)}, f32[64,512]{1,0:T(8,128)}, u32[]{:S(2)}) copy-start(f32[64,512]{1,0:T(8,128)} %param.7) | copy-start | bytes 393220
  4.0 1.5 %collective-permute-start = (f32[160,256]{1,0:T(8,128)S(1)}, f32[160,256]{1,0:T(8,128)S(1)}, u32[]{:S(2)}, u32[]{:S(2)}) collective-permute-start(f32[160,256]{1,0:T(8,128)S(1)} %slice_select_fusion), channel_id=1, source_target_pairs={{0,1},{1,0},{2,3},{3,2},{4,5},{5,4},{6,7},{7,6},{8,9},{9,8},{10,11... | collective-permute-start | bytes 491528 | tf_op jit(solution)/shard_map/ppermute | solution.py:162
  5.6 7.4 %collective-permute-start.1 = (f32[160,256]{1,0:T(8,128)S(1)}, f32[160,256]{1,0:T(8,128)S(1)}, u32[]{:S(2)}, u32[]{:S(2)}) collective-permute-start(f32[160,256]{1,0:T(8,128)S(1)} %select_add_fusion), channel_id=1, source_target_pairs={{0,2},{2,0},{4,6},{6,4},{8,10},{10,8},{12,14},{14,12},{16,18},{18,... | collective-permute-start | bytes 491528 | tf_op jit(solution)/shard_map/ppermute | solution.py:162
  13.0 5.8 %collective-permute-start.2 = (f32[160,256]{1,0:T(8,128)S(1)}, f32[160,256]{1,0:T(8,128)S(1)}, u32[]{:S(2)}, u32[]{:S(2)}) collective-permute-start(f32[160,256]{1,0:T(8,128)S(1)} %add.21), channel_id=1, source_target_pairs={{0,4},{2,6},{4,0},{6,2},{8,12},{10,14},{12,8},{14,10},{16,20},{18,... | collective-permute-start | bytes 491528 | tf_op jit(solution)/shard_map/ppermute | solution.py:162
  18.8 5.4 %collective-permute-start.3 = (f32[160,256]{1,0:T(8,128)S(1)}, f32[160,256]{1,0:T(8,128)S(1)}, u32[]{:S(2)}, u32[]{:S(2)}) collective-permute-start(f32[160,256]{1,0:T(8,128)S(1)} %add.22), channel_id=1, source_target_pairs={{0,8},{2,10},{4,12},{6,14},{8,0},{10,2},{12,4},{14,6},{16,24},{18,... | collective-permute-start | bytes 491528 | tf_op jit(solution)/shard_map/ppermute | solution.py:162
  24.3 8.2 %collective-permute-start.4 = (f32[160,256]{1,0:T(8,128)S(1)}, f32[160,256]{1,0:T(8,128)S(1)}, u32[]{:S(2)}, u32[]{:S(2)}) collective-permute-start(f32[160,256]{1,0:T(8,128)S(1)} %add.23), channel_id=1, source_target_pairs={{0,16},{2,18},{4,20},{6,22},{8,24},{10,26},{12,28},{14,30},{16,0},... | collective-permute-start | bytes 491528 | tf_op jit(solution)/shard_map/ppermute | solution.py:162
  32.4 1.5 %collective-permute-start.5 = (f32[160,256]{1,0:T(8,128)S(1)}, f32[160,256]{1,0:T(8,128)S(1)}, u32[]{:S(2)}, u32[]{:S(2)}) collective-permute-start(f32[160,256]{1,0:T(8,128)S(1)} %add.24), channel_id=1, source_target_pairs={{0,1},{1,0},{2,3},{3,2},{4,5},{5,4},{6,7},{7,6},{8,9},{9,8},{10,11... | collective-permute-start | bytes 491528 | tf_op jit(solution)/shard_map/ppermute | solution.py:162

commit v2 on v1

--- a/solution.py
+++ b/solution.py
@@ -126,73 +126,152 @@
             work[last:, :] = previous - product
 
 
-def finish_kernel(panel, gram_ref, cross_ref, weighted_ref, basis_ref, factor_ref, coef_ref, work, linv):
-    order = gram_ref.shape[0]
-    work[...] = gram_ref[...]
+def packed_rows(order, probes):
+    return -(-(order // 2 + probes + 1) // (2 * BLOCK)) * 2 * BLOCK
+
+
+def live_volumes(volumes_ref, live_ref, begin):
+    ids = lax.broadcasted_iota(jnp.int32, (1, LANES), 1) + begin
+    part = volumes_ref[pl.ds(begin, LANES)].reshape(1, LANES)
+    return jnp.where(ids < live_ref[0], part, 0.0)
+
+
+def sums_kernel(total_rows, snapshots_ref, volumes_ref, live_ref, probes_ref, core_ref, keep_ref, send_ref, packed):
+    row_count, order = snapshots_ref.shape
+    probes = probes_ref.shape[0]
+    half = order // 2
+    volume = jnp.concatenate([live_volumes(volumes_ref, live_ref, b) for b in range(0, row_count, LANES)], axis=1)
+    snapshots = snapshots_ref[...]
+    scaled = snapshots.T * (volume * (1.0 / total_rows))
+    gram = jnp.dot(scaled, snapshots, precision=HIGHEST, preferred_element_type=F32)
+    probe_scaled = probes_ref[...] * (volume * (1.0 / total_rows**0.5))
+    cross = jnp.dot(probe_scaled, snapshots, precision=HIGHEST, preferred_element_type=F32)
+    row_ids = lax.broadcasted_iota(jnp.int32, (half, half), 0)
+    column_ids = lax.broadcasted_iota(jnp.int32, (half, half), 1)
+    packed[:half, :half] = jnp.where(row_ids <= column_ids, gram[:half, :half], gram[half:, half:])
+    packed[:half, half:] = gram[:half, half:]
+    packed[half : half + probes, :] = cross
+    rest = packed.shape[0] - half - probes
+    packed[half + probes :, :] = jnp.zeros((rest, order), F32)
+    diagonal = jnp.sum(jnp.where(row_ids == column_ids, gram[half:, half:], 0.0), axis=0, keepdims=True)
+    packed[half + probes : half + probes + 1, :half] = diagonal
+    middle = packed.shape[0] // 2
+    low = core_ref[0] == 0
+
+    @pl.when(low)
+    def _():
+        keep_ref[...] = packed[:middle, :]
+        send_ref[...] = packed[middle:, :]
+
+    @pl.when(jnp.logical_not(low))
+    def _():
+        keep_ref[...] = packed[middle:, :]
+        send_ref[...] = packed[:middle, :]
+
+
+def local_sums(total_rows, snapshots, volumes, live_rows, probes, core):
+    order = snapshots.shape[1]
+    size = packed_rows(order, probes.shape[0])
+    whole = pl.BlockSpec(memory_space=pltpu.VMEM)
+    scalar = pl.BlockSpec(memory_space=pltpu.SMEM)
+    return pl.pallas_call(
+        functools.partial(sums_kernel, total_rows),
+        out_shape=(jax.ShapeDtypeStruct((size // 2, order), F32),) * 2,
+        in_specs=[whole, whole, scalar, whole, scalar],
+        out_specs=(whole, whole),
+        scratch_shapes=[pltpu.VMEM((size, order), F32)],
+        compiler_params=pltpu.CompilerParams(vmem_limit_bytes=24 * 1024 * 1024),
+    )(snapshots, volumes, live_rows, probes, core)
+
+
+def finish_kernel(panel, mine_ref, other_ref, snapshots_ref, volumes_ref, live_ref, core_ref, basis_ref, factor_ref, coef_ref, work, linv, packed):
+    row_count, order = snapshots_ref.shape
+    probes = coef_ref.shape[0]
+    half = order // 2
+    middle = mine_ref.shape[0]
+    low = core_ref[0] == 0
+
+    @pl.when(low)
+    def _():
+        packed[:middle, :] = mine_ref[...]
+        packed[middle:, :] = other_ref[...]
+
+    @pl.when(jnp.logical_not(low))
+    def _():
+        packed[middle:, :] = mine_ref[...]
+        packed[:middle, :] = other_ref[...]
+
+    row_ids = lax.broadcasted_iota(jnp.int32, (half, half), 0)
+    column_ids = lax.broadcasted_iota(jnp.int32, (half, half), 1)
+    square = packed[:half, :half]
+    turned = square.T
+    work[:half, :half] = jnp.where(row_ids <= column_ids, square, turned)
+    work[:half, half:] = packed[:half, half:]
+    second = jnp.where(row_ids > column_ids, square, turned)
+    diagonal = packed[half + probes : half + probes + 1, :half]
+    work[half:, half:] = jnp.where(row_ids == column_ids, diagonal, second)
+    work[half:, :half] = jnp.zeros((half, half), F32)
     eliminate(work, factor_ref, linv, order, panel)
     dims = (((1,), (1,)), ((), ()))
-    basis_ref[...] = lax.dot_general(
-        weighted_ref[...], linv[...], dims, precision=HIGHEST, preferred_element_type=F32
+    inverse = linv[...]
+    coef_ref[...] = lax.dot_general(
+        packed[half : half + probes, :], inverse, dims, precision=HIGHEST, preferred_element_type=F32
     )
-    coef_ref[...] = lax.dot_general(
-        cross_ref[...], linv[...], dims, precision=HIGHEST, preferred_element_type=F32
-    )
-
-
-def finish(gram, cross, weighted, panel=128):
-    order = gram.shape[0]
-    rows, probes = weighted.shape[0], cross.shape[0]
+    for begin in range(0, row_count, LANES):
+        scale = jnp.sqrt(live_volumes(volumes_ref, live_ref, begin))
+        scale = jnp.broadcast_to(scale, (LANES, LANES)).T
+        weighted = snapshots_ref[begin : begin + LANES, :] * jnp.concatenate([scale] * (order // LANES), axis=1)
+        basis_ref[begin : begin + LANES, :] = lax.dot_general(
+            weighted, inverse, dims, precision=HIGHEST, preferred_element_type=F32
+        )
+
+
+def finish(mine, other, snapshots, volumes, live_rows, core, probes):
+    row_count, order = snapshots.shape
     whole = pl.BlockSpec(memory_space=pltpu.VMEM)
+    scalar = pl.BlockSpec(memory_space=pltpu.SMEM)
     return pl.pallas_call(
-        functools.partial(finish_kernel, panel),
+        functools.partial(finish_kernel, order // 2),
         out_shape=(
-            jax.ShapeDtypeStruct((rows, order), F32),
+            jax.ShapeDtypeStruct((row_count, order), F32),
             jax.ShapeDtypeStruct((order, order), F32),
             jax.ShapeDtypeStruct((probes, order), F32),
         ),
-        in_specs=[whole] * 3,
+        in_specs=[whole] * 4 + [scalar] * 2,
         out_specs=(whole,) * 3,
-        scratch_shapes=[pltpu.VMEM((order, order), F32), pltpu.VMEM((order, order), F32)],
+        scratch_shapes=[
+            pltpu.VMEM((order, order), F32),
+            pltpu.VMEM((order, order), F32),
+            pltpu.VMEM((2 * mine.shape[0], order), F32),
+        ],
         compiler_params=pltpu.CompilerParams(vmem_limit_bytes=32 * 1024 * 1024),
-    )(gram, cross, weighted)
-
-
-def exchange(value, axis, bit):
-    size = lax.axis_size(axis)
-    return lax.ppermute(value, axis, [(i, i ^ bit) for i in range(size)])
-
-
-def reduce_all(value):
-    half = value.shape[0] // 2
-    core = lax.axis_index("sub") % 2
-    low, high = value[:half], value[half:]
-    mine = jnp.where(core == 0, low, high)
-    mine = mine + exchange(jnp.where(core == 0, high, low), "sub", 1)
-    for axis, begin in (("cells", 1), ("sub", 2)):
-        bit = begin
-        while bit < lax.axis_size(axis):
-            mine = mine + exchange(mine, axis, bit)
-            bit *= 2
-    other = exchange(mine, "sub", 1)
-    low = jnp.where(core == 0, mine, other)
-    high = jnp.where(core == 0, other, mine)
-    return jnp.concatenate([low, high], axis=0)
+    )(mine, other, snapshots, volumes, live_rows, core)
+
+
+def exchange(value, bits):
+    count = lax.axis_size("cells") * lax.axis_size("sub")
+    return lax.ppermute(value, ("cells", "sub"), [(i, i ^ bits[i % 2]) for i in range(count)])
+
+
+def reduce_halves(keep, send):
+    count = lax.axis_size("cells") * lax.axis_size("sub")
+    bits = [1 << k for k in range(1, count.bit_length() - 1)]
+    split = len(bits) // 2
+    mine = keep + exchange(send, (1, 1))
+    for first, second in zip(bits[:split], bits[split : 2 * split]):
+        mine = mine + exchange(mine, (first, second))
+        mine = mine + exchange(mine, (second, first))
+    for bit in bits[2 * split :]:
+        mine = mine + exchange(mine, (bit, bit))
+    return mine, exchange(mine, (1, 1))
 
 
 def per_device(snapshots, volumes, live_rows, probes):
-    row_count, order = snapshots.shape
-    total_rows = row_count * lax.axis_size("cells") * lax.axis_size("sub")
-    root_total = jnp.sqrt(jnp.float32(total_rows))
-    live_mask = lax.iota(jnp.int32, row_count) < live_rows[0]
-    row_scale = jnp.where(live_mask, jnp.sqrt(volumes), jnp.float32(0.0))
-    weighted = snapshots * row_scale[:, None]
-    probe_weighted = probes * row_scale[None, :]
-    gram_local = lax.dot_general(
-        weighted, weighted, (((0,), (0,)), ((), ())), precision=HIGHEST, preferred_element_type=F32
-    ) / jnp.float32(total_rows)
-    cross_local = jnp.dot(probe_weighted, weighted, precision=HIGHEST, preferred_element_type=F32) / root_total
-    total = reduce_all(jnp.concatenate([gram_local, cross_local], axis=0))
-    return finish(total[:order], total[order:], weighted)
+    count = lax.axis_size("cells") * lax.axis_size("sub")
+    core = (lax.axis_index("sub") % 2).astype(jnp.int32).reshape(1)
+    keep, send = local_sums(snapshots.shape[0] * count, snapshots, volumes, live_rows, probes, core)
+    mine, other = reduce_halves(keep, send)
+    return finish(mine, other, snapshots, volumes, live_rows, core, probes.shape[0])
 
 
 def solution(mesh):

time: 47.8 us -> 43.7 us (0.914)
  waiting for transfers between devices: 20.2 us -> 13 us
  local copies, waits for them, and re-layouts: 0.03 us -> 2.62 us
  Pallas kernels: 13.6 us -> 15.2 us
  matrix products: 1.42 us -> 0 us
  other arithmetic: 1.35 us -> 0.08 us
  starting transfers between devices: 9.62 us -> 10.8 us
    ppermute x6, waiting for transfers between devices: 20.2 us -> 13 us  [exchange(): lax.ppermute(value, ('cells', 'sub'), [(i, i ^ bits[i % 2]) for i in rang...]
    unnamed x4 -> x8, local copies, waits for them, and re-layouts: 0.02 us -> 2.62 us
    pallas_call x1 -> x2, Pallas kernels: 13.6 us -> 15.2 us  [the longest x1 14.3 us: finish(): pl.pallas_call(functools.partial(finish_kernel, order // 2), out_shape=(j...]
    dot_general x2 -> x0, matrix products: 1.42 us -> none  [the longest x1 1.02 us: per_device(): lax.dot_general(weighted, weighted, (((0,), (0,)), ((), ())), precision=H...]
    mul x1 -> x0, other arithmetic: 1.17 us -> none  [per_device(): weighted = snapshots * row_scale[:, None]]
    ppermute x6, starting transfers between devices: 9.62 us -> 10.8 us  [exchange(): lax.ppermute(value, ('cells', 'sub'), [(i, i ^ bits[i % 2]) for i in rang...]
where the time goes in v2:
time: 43.7 us; the launch traced here: 43.1 us
  Pallas kernels  15.2 us (35%)
  waiting for transfers between devices  13 us (30%)
  starting transfers between devices  10.8 us (25%)
  local copies, waits for them, and re-layouts  2.62 us (6%)
  between operations  1.33 us (3%)
    pallas_call x1, Pallas kernels, finish(): pl.pallas_call(functools.partial(finish_kernel, order // 2), out_shape=(j...  14.3 us
    ppermute x6, waiting for transfers between devices, exchange(): lax.ppermute(value, ('cells', 'sub'), [(i, i ^ bits[i % 2]) for i in rang...  13 us
    ppermute x6, starting transfers between devices, exchange(): lax.ppermute(value, ('cells', 'sub'), [(i, i ^ bits[i % 2]) for i in rang...  10.8 us
    unnamed x8, local copies, waits for them, and re-layouts  2.62 us
    pallas_call x1, Pallas kernels, local_sums(): pl.pallas_call(functools.partial(sums_kernel, total_rows), out_shape=(jax...  0.9 us
  transfers between devices with their start and end apart: 6, of which 6 were waited for; matrix products, arithmetic and copies ran while one was open for 0% of the time, Pallas kernels for 0%

profile of v2, /device:TPU:0, one launch (start us, length us, event | category | flops | bytes accessed | tf_op | source)
XLA Modules:
  0.0 43.1 jit_solution(3229322066037236311)
XLA Ops:
  1.3 0.0 copy-start.3
  1.3 0.7 %copy-done.3 = f32[512]{0:T(512)S(1)} copy-done((f32[512]{0:T(512)S(1)}, f32[512]{0:T(512)}, u32[]{:S(2)}) %copy-start.3) | copy-done | bytes 2072
  2.0 0.0 copy-start
  2.0 1.0 %copy-done = f32[512,256]{1,0:T(8,128)S(1)} copy-done((f32[512,256]{1,0:T(8,128)S(1)}, f32[512,256]{1,0:T(8,128)}, u32[]{:S(2)}) %copy-start) | copy-done | bytes 524312
  3.0 0.0 copy-start.2
  3.0 0.9 %copy-done.2 = f32[64,512]{1,0:T(8,128)S(1)} copy-done((f32[64,512]{1,0:T(8,128)S(1)}, f32[64,512]{1,0:T(8,128)}, u32[]{:S(2)}) %copy-start.2) | copy-done | bytes 131096
  3.9 0.9 %shard_map.67 = (f32[104,256]{1,0:T(8,128)S(1)}, f32[104,256]{1,0:T(8,128)S(1)}) custom-call(f32[512,256]{1,0:T(8,128)S(1)} %copy-done, f32[512]{0:T(512)S(1)} %copy-done.3, s32[1]{0:T(128)S(6)} %copy.7.live_ref, f32[64,512]{1,0:T(8,128)S(1)} %copy-done.2, s32[1]{0:T(128)} %bitcast.core_ref), custom_call_target="tpu_custom_call" | custom-call | tf_op jit(solution)/shard_map/pallas_call | solution.py:177
  4.8 0.5 %collective-permute-start = (f32[104,256]{1,0:T(8,128)S(1)}, f32[104,256]{1,0:T(8,128)S(1)}, u32[]{:S(2)}, u32[]{:S(2)}) collective-permute-start(f32[104,256]{1,0:T(8,128)S(1)} %get-tuple-element.6), channel_id=1, source_target_pairs={{0,1},{1,0},{2,3},{3,2},{4,5},{5,4},{6,7},{7,6},{8,9},{9,8},{10,11... | collective-permute-start | bytes 319496 | tf_op jit(solution)/shard_map/ppermute | solution.py:253
  5.3 1.0 %collective-permute-done = f32[104,256]{1,0:T(8,128)S(1)} collective-permute-done((f32[104,256]{1,0:T(8,128)S(1)}, f32[104,256]{1,0:T(8,128)S(1)}, u32[]{:S(2)}, u32[]{:S(2)}) %collective-permute-start) | collective-permute-done | bytes 106528 | tf_op jit(solution)/shard_map/ppermute | solution.py:253
  6.3 2.9 %collective-permute-start.1 = (f32[104,256]{1,0:T(8,128)S(1)}, f32[104,256]{1,0:T(8,128)S(1)}, u32[]{:S(2)}, u32[]{:S(2)}) collective-permute-start(f32[104,256]{1,0:T(8,128)S(1)} %add.20), channel_id=1, source_target_pairs={{0,2},{1,9},{2,0},{3,11},{4,6},{5,13},{6,4},{7,15},{8,10},{9,1},{1... | collective-permute-start | bytes 319496 | tf_op jit(solution)/shard_map/ppermute | solution.py:253
  9.2 2.7 %collective-permute-done.1 = f32[104,256]{1,0:T(8,128)S(1)} collective-permute-done((f32[104,256]{1,0:T(8,128)S(1)}, f32[104,256]{1,0:T(8,128)S(1)}, u32[]{:S(2)}, u32[]{:S(2)}) %collective-permute-start.1) | collective-permute-done | bytes 106528 | tf_op jit(solution)/shard_map/ppermute | solution.py:253
  11.9 0.0 copy-start.1
  11.9 2.2 %collective-permute-start.2 = (f32[104,256]{1,0:T(8,128)S(1)}, f32[104,256]{1,0:T(8,128)S(1)}, u32[]{:S(2)}, u32[]{:S(2)}) collective-permute-start(f32[104,256]{1,0:T(8,128)S(1)} %add.21), channel_id=1, source_target_pairs={{0,8},{1,3},{2,10},{3,1},{4,12},{5,7},{6,14},{7,5},{8,0},{9,11},{1... | collective-permute-start | bytes 319496 | tf_op jit(solution)/shard_map/ppermute | solution.py:253
  14.1 2.7 %collective-permute-done.2 = f32[104,256]{1,0:T(8,128)S(1)} collective-permute-done((f32[104,256]{1,0:T(8,128)S(1)}, f32[104,256]{1,0:T(8,128)S(1)}, u32[]{:S(2)}, u32[]{:S(2)}) %collective-permute-start.2) | collective-permute-done | bytes 106528 | tf_op jit(solution)/shard_map/ppermute | solution.py:253
  16.8 2.0 %collective-permute-start.3 = (f32[104,256]{1,0:T(8,128)S(1)}, f32[104,256]{1,0:T(8,128)S(1)}, u32[]{:S(2)}, u32[]{:S(2)}) collective-permute-start(f32[104,256]{1,0:T(8,128)S(1)} %add.22), channel_id=1, source_target_pairs={{0,4},{1,17},{2,6},{3,19},{4,0},{5,21},{6,2},{7,23},{8,12},{9,25},... | collective-permute-start | bytes 319496 | tf_op jit(solution)/shard_map/ppermute | solution.py:253
  18.8 2.7 %collective-permute-done.3 = f32[104,256]{1,0:T(8,128)S(1)} collective-permute-done((f32[104,256]{1,0:T(8,128)S(1)}, f32[104,256]{1,0:T(8,128)S(1)}, u32[]{:S(2)}, u32[]{:S(2)}) %collective-permute-start.3) | collective-permute-done | bytes 106528 | tf_op jit(solution)/shard_map/ppermute | solution.py:253
  21.6 3.1 %collective-permute-start.4 = (f32[104,256]{1,0:T(8,128)S(1)}, f32[104,256]{1,0:T(8,128)S(1)}, u32[]{:S(2)}, u32[]{:S(2)}) collective-permute-start(f32[104,256]{1,0:T(8,128)S(1)} %add.23), channel_id=1, source_target_pairs={{0,16},{1,5},{2,18},{3,7},{4,20},{5,1},{6,22},{7,3},{8,24},{9,13},... | collective-permute-start | bytes 319496 | tf_op jit(solution)/shard_map/ppermute | solution.py:253
  24.7 2.7 %collective-permute-done.4 = f32[104,256]{1,0:T(8,128)S(1)} collective-permute-done((f32[104,256]{1,0:T(8,128)S(1)}, f32[104,256]{1,0:T(8,128)S(1)}, u32[]{:S(2)}, u32[]{:S(2)}) %collective-permute-start.4) | collective-permute-done | bytes 106528 | tf_op jit(solution)/shard_map/ppermute | solution.py:253
  27.4 0.1 collective-permute-start.5
  27.5 1.3 %collective-permute-done.5.other_ref = f32[104,256]{1,0:T(8,128)S(1)} collective-permute-done((f32[104,256]{1,0:T(8,128)S(1)}, f32[104,256]{1,0:T(8,128)S(1)}, u32[]{:S(2)}, u32[]{:S(2)}) %collective-permute-start.5) | collective-permute-done | bytes 106528 | tf_op jit(solution)/shard_map/ppermute | solution.py:253
  28.8 0.0 copy-done.1
  28.8 14.3 %shard_map.68 = (f32[512,256]{1,0:T(8,128)}, f32[256,256]{1,0:T(8,128)}, f32[64,256]{1,0:T(8,128)}) custom-call(f32[104,256]{1,0:T(8,128)S(1)} %add.24.mine_ref, f32[104,256]{1,0:T(8,128)S(1)} %collective-permute-done.5.other_ref, f32[512,256]{1,0:T(8,128)S(1)} %copy-done.1, f32[512]{0:T(512)S(1)} %copy-done.3, s32[1]{0:T(128)S(6)} %copy.7.live_ref, ...), custom_call_target="tpu_custom_call" | custom-call | tf_op jit(solution)/shard_map/pallas_call | solution.py:233
  (5 shorter events, 0.1 us)
Async XLA Ops:
  1.3 0.7 %copy-start.3 = (f32[512]{0:T(512)S(1)}, f32[512]{0:T(512)}, u32[]{:S(2)}) copy-start(f32[512]{0:T(512)} %volumes_ref.3) | copy-start | bytes 6148
  2.0 1.0 %copy-start = (f32[512,256]{1,0:T(8,128)S(1)}, f32[512,256]{1,0:T(8,128)}, u32[]{:S(2)}) copy-start(f32[512,256]{1,0:T(8,128)} %snapshots_ref.3) | copy-start | bytes 1572868
  3.0 0.9 %copy-start.2 = (f32[64,512]{1,0:T(8,128)S(1)}, f32[64,512]{1,0:T(8,128)}, u32[]{:S(2)}) copy-start(f32[64,512]{1,0:T(8,128)} %probes_ref.1) | copy-start | bytes 393220
  4.8 1.5 %collective-permute-start = (f32[104,256]{1,0:T(8,128)S(1)}, f32[104,256]{1,0:T(8,128)S(1)}, u32[]{:S(2)}, u32[]{:S(2)}) collective-permute-start(f32[104,256]{1,0:T(8,128)S(1)} %get-tuple-element.6), channel_id=1, source_target_pairs={{0,1},{1,0},{2,3},{3,2},{4,5},{5,4},{6,7},{7,6},{8,9},{9,8},{10,11... | collective-permute-start | bytes 319496 | tf_op jit(solution)/shard_map/ppermute | solution.py:253
  6.3 5.6 %collective-permute-start.1 = (f32[104,256]{1,0:T(8,128)S(1)}, f32[104,256]{1,0:T(8,128)S(1)}, u32[]{:S(2)}, u32[]{:S(2)}) collective-permute-start(f32[104,256]{1,0:T(8,128)S(1)} %add.20), channel_id=1, source_target_pairs={{0,2},{1,9},{2,0},{3,11},{4,6},{5,13},{6,4},{7,15},{8,10},{9,1},{1... | collective-permute-start | bytes 319496 | tf_op jit(solution)/shard_map/ppermute | solution.py:253
  11.9 16.9 %copy-start.1 = (f32[512,256]{1,0:T(8,128)S(1)}, f32[512,256]{1,0:T(8,128)}, u32[]{:S(2)}) copy-start(f32[512,256]{1,0:T(8,128)} %snapshots_ref.3) | copy-start | bytes 1572868
  11.9 4.9 %collective-permute-start.2 = (f32[104,256]{1,0:T(8,128)S(1)}, f32[104,256]{1,0:T(8,128)S(1)}, u32[]{:S(2)}, u32[]{:S(2)}) collective-permute-start(f32[104,256]{1,0:T(8,128)S(1)} %add.21), channel_id=1, source_target_pairs={{0,8},{1,3},{2,10},{3,1},{4,12},{5,7},{6,14},{7,5},{8,0},{9,11},{1... | collective-permute-start | bytes 319496 | tf_op jit(solution)/shard_map/ppermute | solution.py:253
  16.8 4.8 %collective-permute-start.3 = (f32[104,256]{1,0:T(8,128)S(1)}, f32[104,256]{1,0:T(8,128)S(1)}, u32[]{:S(2)}, u32[]{:S(2)}) collective-permute-start(f32[104,256]{1,0:T(8,128)S(1)} %add.22), channel_id=1, source_target_pairs={{0,4},{1,17},{2,6},{3,19},{4,0},{5,21},{6,2},{7,23},{8,12},{9,25},... | collective-permute-start | bytes 319496 | tf_op jit(solution)/shard_map/ppermute | solution.py:253
  21.6 5.8 %collective-permute-start.4 = (f32[104,256]{1,0:T(8,128)S(1)}, f32[104,256]{1,0:T(8,128)S(1)}, u32[]{:S(2)}, u32[]{:S(2)}) collective-permute-start(f32[104,256]{1,0:T(8,128)S(1)} %add.23), channel_id=1, source_target_pairs={{0,16},{1,5},{2,18},{3,7},{4,20},{5,1},{6,22},{7,3},{8,24},{9,13},... | collective-permute-start | bytes 319496 | tf_op jit(solution)/shard_map/ppermute | solution.py:253
  27.4 1.4 %collective-permute-start.5 = (f32[104,256]{1,0:T(8,128)S(1)}, f32[104,256]{1,0:T(8,128)S(1)}, u32[]{:S(2)}, u32[]{:S(2)}) collective-permute-start(f32[104,256]{1,0:T(8,128)S(1)} %add.24.mine_ref), channel_id=1, source_target_pairs={{0,1},{1,0},{2,3},{3,2},{4,5},{5,4},{6,7},{7,6},{8,9},{9,8},{10,11... | collective-permute-start | bytes 319496 | tf_op jit(solution)/shard_map/ppermute | solution.py:253

commit v3 on v2

--- a/solution.py
+++ b/solution.py
@@ -126,8 +126,9 @@
             work[last:, :] = previous - product
 
 
-def packed_rows(order, probes):
-    return -(-(order // 2 + probes + 1) // (2 * BLOCK)) * 2 * BLOCK
+def piece_rows(order, probes, count):
+    total = (3 * (order // 2) + probes * 2) * (order // 2 // LANES)
+    return -(-total // (count * BLOCK)) * BLOCK
 
 
 def live_volumes(volumes_ref, live_ref, begin):
@@ -136,87 +137,73 @@
     return jnp.where(ids < live_ref[0], part, 0.0)
 
 
-def sums_kernel(total_rows, snapshots_ref, volumes_ref, live_ref, probes_ref, core_ref, keep_ref, send_ref, packed):
+def sums_kernel(total_rows, snapshots_hbm, volumes_hbm, live_ref, probes_hbm, packed, snapshots_ref, volumes_ref, probes_ref, sems):
+    copies = [
+        pltpu.make_async_copy(source, target, sems.at[i])
+        for i, (source, target) in enumerate(
+            ((volumes_hbm, volumes_ref), (snapshots_hbm, snapshots_ref), (probes_hbm, probes_ref))
+        )
+    ]
+    for copy in copies:
+        copy.start()
     row_count, order = snapshots_ref.shape
     probes = probes_ref.shape[0]
     half = order // 2
+    copies[0].wait()
     volume = jnp.concatenate([live_volumes(volumes_ref, live_ref, b) for b in range(0, row_count, LANES)], axis=1)
+    copies[1].wait()
     snapshots = snapshots_ref[...]
     scaled = snapshots.T * (volume * (1.0 / total_rows))
     gram = jnp.dot(scaled, snapshots, precision=HIGHEST, preferred_element_type=F32)
+    packed[:half, :] = gram[:half, :half]
+    packed[half : 2 * half, :] = gram[:half, half:]
+    packed[2 * half : 3 * half, :] = gram[half:, half:]
+    copies[2].wait()
     probe_scaled = probes_ref[...] * (volume * (1.0 / total_rows**0.5))
     cross = jnp.dot(probe_scaled, snapshots, precision=HIGHEST, preferred_element_type=F32)
-    row_ids = lax.broadcasted_iota(jnp.int32, (half, half), 0)
-    column_ids = lax.broadcasted_iota(jnp.int32, (half, half), 1)
-    packed[:half, :half] = jnp.where(row_ids <= column_ids, gram[:half, :half], gram[half:, half:])
-    packed[:half, half:] = gram[:half, half:]
-    packed[half : half + probes, :] = cross
-    rest = packed.shape[0] - half - probes
-    packed[half + probes :, :] = jnp.zeros((rest, order), F32)
-    diagonal = jnp.sum(jnp.where(row_ids == column_ids, gram[half:, half:], 0.0), axis=0, keepdims=True)
-    packed[half + probes : half + probes + 1, :half] = diagonal
-    middle = packed.shape[0] // 2
-    low = core_ref[0] == 0
-
-    @pl.when(low)
-    def _():
-        keep_ref[...] = packed[:middle, :]
-        send_ref[...] = packed[middle:, :]
-
-    @pl.when(jnp.logical_not(low))
-    def _():
-        keep_ref[...] = packed[middle:, :]
-        send_ref[...] = packed[:middle, :]
-
-
-def local_sums(total_rows, snapshots, volumes, live_rows, probes, core):
+    packed[3 * half : 3 * half + probes, :] = cross[:, :half]
+    packed[3 * half + probes : 3 * half + 2 * probes, :] = cross[:, half:]
+    rest = packed.shape[0] - 3 * half - 2 * probes
+    if rest > 0:
+        packed[3 * half + 2 * probes :, :] = jnp.zeros((rest, half), F32)
+
+
+def local_sums(count, snapshots, volumes, live_rows, probes):
     order = snapshots.shape[1]
-    size = packed_rows(order, probes.shape[0])
+    rows = piece_rows(order, probes.shape[0], count) * count
+    hbm = pl.BlockSpec(memory_space=pltpu.HBM)
     whole = pl.BlockSpec(memory_space=pltpu.VMEM)
     scalar = pl.BlockSpec(memory_space=pltpu.SMEM)
     return pl.pallas_call(
-        functools.partial(sums_kernel, total_rows),
-        out_shape=(jax.ShapeDtypeStruct((size // 2, order), F32),) * 2,
-        in_specs=[whole, whole, scalar, whole, scalar],
-        out_specs=(whole, whole),
-        scratch_shapes=[pltpu.VMEM((size, order), F32)],
-        compiler_params=pltpu.CompilerParams(vmem_limit_bytes=24 * 1024 * 1024),
-    )(snapshots, volumes, live_rows, probes, core)
-
-
-def finish_kernel(panel, mine_ref, other_ref, snapshots_ref, volumes_ref, live_ref, core_ref, basis_ref, factor_ref, coef_ref, work, linv, packed):
+        functools.partial(sums_kernel, snapshots.shape[0] * count),
+        out_shape=jax.ShapeDtypeStruct((rows, order // 2), F32),
+        in_specs=[hbm, hbm, scalar, hbm],
+        out_specs=whole,
+        scratch_shapes=[
+            pltpu.VMEM(snapshots.shape, F32),
+            pltpu.VMEM(volumes.shape, F32),
+            pltpu.VMEM(probes.shape, F32),
+            pltpu.SemaphoreType.DMA((3,)),
+        ],
+        compiler_params=pltpu.CompilerParams(vmem_limit_bytes=60 * 1024 * 1024),
+    )(snapshots, volumes, live_rows, probes)
+
+
+def finish_kernel(panel, packed, snapshots_ref, volumes_ref, live_ref, basis_ref, factor_ref, coef_ref, work, linv):
     row_count, order = snapshots_ref.shape
     probes = coef_ref.shape[0]
     half = order // 2
-    middle = mine_ref.shape[0]
-    low = core_ref[0] == 0
-
-    @pl.when(low)
-    def _():
-        packed[:middle, :] = mine_ref[...]
-        packed[middle:, :] = other_ref[...]
-
-    @pl.when(jnp.logical_not(low))
-    def _():
-        packed[middle:, :] = mine_ref[...]
-        packed[:middle, :] = other_ref[...]
-
-    row_ids = lax.broadcasted_iota(jnp.int32, (half, half), 0)
-    column_ids = lax.broadcasted_iota(jnp.int32, (half, half), 1)
-    square = packed[:half, :half]
-    turned = square.T
-    work[:half, :half] = jnp.where(row_ids <= column_ids, square, turned)
-    work[:half, half:] = packed[:half, half:]
-    second = jnp.where(row_ids > column_ids, square, turned)
-    diagonal = packed[half + probes : half + probes + 1, :half]
-    work[half:, half:] = jnp.where(row_ids == column_ids, diagonal, second)
+    work[:half, :half] = packed[:half, :]
+    work[:half, half:] = packed[half : 2 * half, :]
+    work[half:, half:] = packed[2 * half : 3 * half, :]
     work[half:, :half] = jnp.zeros((half, half), F32)
     eliminate(work, factor_ref, linv, order, panel)
     dims = (((1,), (1,)), ((), ()))
     inverse = linv[...]
-    coef_ref[...] = lax.dot_general(
-        packed[half : half + probes, :], inverse, dims, precision=HIGHEST, preferred_element_type=F32
+    cross = jnp.concatenate(
+        [packed[3 * half : 3 * half + probes, :], packed[3 * half + probes : 3 * half + 2 * probes, :]], axis=1
     )
+    coef_ref[...] = lax.dot_general(cross, inverse, dims, precision=HIGHEST, preferred_element_type=F32)
     for begin in range(0, row_count, LANES):
         scale = jnp.sqrt(live_volumes(volumes_ref, live_ref, begin))
         scale = jnp.broadcast_to(scale, (LANES, LANES)).T
@@ -226,7 +213,7 @@
         )
 
 
-def finish(mine, other, snapshots, volumes, live_rows, core, probes):
+def finish(packed, snapshots, volumes, live_rows, probes):
     row_count, order = snapshots.shape
     whole = pl.BlockSpec(memory_space=pltpu.VMEM)
     scalar = pl.BlockSpec(memory_space=pltpu.SMEM)
@@ -237,41 +224,25 @@
             jax.ShapeDtypeStruct((order, order), F32),
             jax.ShapeDtypeStruct((probes, order), F32),
         ),
-        in_specs=[whole] * 4 + [scalar] * 2,
+        in_specs=[whole] * 3 + [scalar],
         out_specs=(whole,) * 3,
-        scratch_shapes=[
-            pltpu.VMEM((order, order), F32),
-            pltpu.VMEM((order, order), F32),
-            pltpu.VMEM((2 * mine.shape[0], order), F32),
-        ],
+        scratch_shapes=[pltpu.VMEM((order, order), F32), pltpu.VMEM((order, order), F32)],
         compiler_params=pltpu.CompilerParams(vmem_limit_bytes=32 * 1024 * 1024),
-    )(mine, other, snapshots, volumes, live_rows, core)
-
-
-def exchange(value, bits):
+    )(packed, snapshots, volumes, live_rows)
+
+
+def sum_everywhere(packed):
+    axes = ("cells", "sub")
     count = lax.axis_size("cells") * lax.axis_size("sub")
-    return lax.ppermute(value, ("cells", "sub"), [(i, i ^ bits[i % 2]) for i in range(count)])
-
-
-def reduce_halves(keep, send):
-    count = lax.axis_size("cells") * lax.axis_size("sub")
-    bits = [1 << k for k in range(1, count.bit_length() - 1)]
-    split = len(bits) // 2
-    mine = keep + exchange(send, (1, 1))
-    for first, second in zip(bits[:split], bits[split : 2 * split]):
-        mine = mine + exchange(mine, (first, second))
-        mine = mine + exchange(mine, (second, first))
-    for bit in bits[2 * split :]:
-        mine = mine + exchange(mine, (bit, bit))
-    return mine, exchange(mine, (1, 1))
+    pieces = packed.reshape(count, packed.shape[0] // count, packed.shape[1])
+    mine = jnp.sum(lax.all_to_all(pieces, axes, 0, 0), axis=0)
+    return lax.all_to_all(jnp.broadcast_to(mine, pieces.shape), axes, 0, 0).reshape(packed.shape)
 
 
 def per_device(snapshots, volumes, live_rows, probes):
     count = lax.axis_size("cells") * lax.axis_size("sub")
-    core = (lax.axis_index("sub") % 2).astype(jnp.int32).reshape(1)
-    keep, send = local_sums(snapshots.shape[0] * count, snapshots, volumes, live_rows, probes, core)
-    mine, other = reduce_halves(keep, send)
-    return finish(mine, other, snapshots, volumes, live_rows, core, probes.shape[0])
+    packed = local_sums(count, snapshots, volumes, live_rows, probes)
+    return finish(sum_everywhere(packed), snapshots, volumes, live_rows, probes.shape[0])
 
 
 def solution(mesh):

time: 43.7 us -> 49.7 us (1.14)
  blocking collectives: 0 us -> 30.7 us
  waiting for transfers between devices: 13 us -> 0 us
  starting transfers between devices: 10.8 us -> 0 us
  local copies, waits for them, and re-layouts: 2.62 us -> 0.03 us
  Pallas kernels: 15.2 us -> 17.4 us
    all_to_all x0 -> x2, blocking collectives: none -> 30.7 us  [the longest x1 17.9 us: sum_everywhere(): mine = jnp.sum(lax.all_to_all(pieces, axes, 0, 0), axis=0)]
    ppermute x6 -> x0, waiting for transfers between devices: 13 us -> none  [exchange(): lax.ppermute(value, ('cells', 'sub'), [(i, i ^ bits[i % 2]) for i in rang...]
    ppermute x6 -> x0, starting transfers between devices: 10.8 us -> none  [exchange(): lax.ppermute(value, ('cells', 'sub'), [(i, i ^ bits[i % 2]) for i in rang...]
    unnamed x8 -> x4, local copies, waits for them, and re-layouts: 2.62 us -> 0.01 us
    pallas_call x1, Pallas kernels: 0.9 us -> 3.16 us  [local_sums(): pl.pallas_call(functools.partial(sums_kernel, snapshots.shape[0] * count)...]
  transfers between devices with their start and end apart: 6 -> 0, of which waited for: 6 -> 0; matrix products, arithmetic and copies ran while one was open for 0% -> 0% of each run, Pallas kernels for 0% -> 0%
where the time goes in v3:
time: 49.7 us; the launch traced here: 49.5 us
  blocking collectives  30.7 us (62%)
  Pallas kernels  17.4 us (35%)
  between operations  1.31 us (3%)
    all_to_all x1, blocking collectives, sum_everywhere(): mine = jnp.sum(lax.all_to_all(pieces, axes, 0, 0), axis=0)  17.9 us
    pallas_call x1, Pallas kernels, finish(): pl.pallas_call(functools.partial(finish_kernel, order // 2), out_shape=(j...  14.2 us
    all_to_all x1, blocking collectives, sum_everywhere(): lax.all_to_all(jnp.broadcast_to(mine, pieces.shape), axes, 0, 0)  12.8 us
    pallas_call x1, Pallas kernels, local_sums(): pl.pallas_call(functools.partial(sums_kernel, snapshots.shape[0] * count)...  3.16 us

profile of v3, /device:TPU:0, one launch (start us, length us, event | category | flops | bytes accessed | tf_op | source)
XLA Modules:
  0.0 49.5 jit_solution(15342591107553317834)
XLA Ops:
  1.3 3.2 %shard_map.67 = f32[512,128]{1,0:T(8,128)} custom-call(f32[512,256]{1,0:T(8,128)} %snapshots_ref.1, f32[512]{0:T(512)} %volumes_ref.1, s32[1]{0:T(128)S(6)} %copy.7.live_ref, f32[64,512]{1,0:T(8,128)} %probes_hbm.1), custom_call_target="tpu_custom_call" | custom-call | tf_op jit(solution)/shard_map/pallas_call | solution.py:177
  4.4 17.9 %all_to_all.10 = f32[32,16,128]{2,1,0:T(8,128)S(1)} all-to-all(f32[32,16,128]{2,1,0:T(8,128)} %bitcast.3), channel_id=1, replica_groups=mesh['cells'=16,'sub'=2] {'cells','sub'}, dimensions={0} | all-to-all | bytes 524288 | tf_op jit(solution)/shard_map/all_to_all | solution.py:238
  22.4 0.0 copy-start
  22.4 0.0 copy-start.1
  22.4 12.8 %all_to_all.11 = f32[32,16,128]{2,1,0:T(8,128)S(1)} all-to-all(f32[32,16,128]{2,1,0:T(8,128)S(1)} %broadcast_in_dim.3), channel_id=1, replica_groups=mesh['cells'=16,'sub'=2] {'cells','sub'}, dimensions={0} | all-to-all | bytes 524288 | tf_op jit(solution)/shard_map/all_to_all | solution.py:239
  35.2 0.0 copy-done
  35.2 0.0 copy-done.1
  35.3 14.2 %shard_map.68 = (f32[512,256]{1,0:T(8,128)}, f32[256,256]{1,0:T(8,128)}, f32[64,256]{1,0:T(8,128)}) custom-call(f32[512,128]{1,0:T(8,128)S(1)} %bitcast.2, f32[512,256]{1,0:T(8,128)S(1)} %copy-done, f32[512]{0:T(512)S(1)} %copy-done.1, s32[1]{0:T(128)S(6)} %copy.7.live_ref), custom_call_target="tpu_custom_call" | custom-call | tf_op jit(solution)/shard_map/pallas_call | solution.py:220
  (2 shorter events, 0.1 us)
Async XLA Ops:
  22.4 12.9 %copy-start = (f32[512,256]{1,0:T(8,128)S(1)}, f32[512,256]{1,0:T(8,128)}, u32[]{:S(2)}) copy-start(f32[512,256]{1,0:T(8,128)} %snapshots_ref.1) | copy-start | bytes 1572868
  22.4 12.8 %copy-start.1 = (f32[512]{0:T(512)S(1)}, f32[512]{0:T(512)}, u32[]{:S(2)}) copy-start(f32[512]{0:T(512)} %volumes_ref.1) | copy-start | bytes 6148

commit v4 on v2

v4 whole, which is shorter than its diff:
```python
import functools
import jax
import jax.numpy as jnp
from jax import lax
from jax.experimental import pallas as pl
from jax.experimental.pallas import tpu as pltpu
from jax.sharding import PartitionSpec as P

HIGHEST = lax.Precision.HIGHEST
LANES = 128
BLOCK = 8
AHEAD = 2
F32 = jnp.float32


def lanes_of(tile, column):
    return jnp.broadcast_to(tile[:, column : column + 1], tile.shape)


def row_of(tile, index):
    return jnp.broadcast_to(tile[index : index + 1, :], tile.shape)


def product(left, right, dims):
    return lax.dot_general(left, right, (dims, ((), ())), precision=HIGHEST, preferred_element_type=F32)


def eliminate(matrix):
    width = matrix.shape[1]
    count = width // BLOCK
    shape = (BLOCK, width)
    tiles = [matrix[k * BLOCK : (k + 1) * BLOCK, :] for k in range(count)]
    sub_ids = lax.broadcasted_iota(jnp.int32, shape, 0)
    lane_ids = lax.broadcasted_iota(jnp.int32, shape, 1)
    spread_ids = lane_ids - sub_ids

    def gather(parts):
        total = parts[0]
        for r in range(1, BLOCK):
            total = jnp.where(sub_ids == r, parts[r], total)
        return total

    upper_rows, lower_rows = [], []
    columns = [lanes_of(tiles[0], c) for c in range(BLOCK)]
    for block in range(count):
        offset = block * BLOCK
        in_block = (lane_ids >= offset) & (lane_ids < offset + BLOCK)
        own = tiles[block]
        entry = {(r, c): row_of(columns[c], r) for c in range(BLOCK) for r in range(c + 1)}
        kept = [row_of(own, r) for r in range(BLOCK)]
        own = jnp.where(in_block, jnp.where(spread_ids == offset, 1.0, 0.0), own)
        rows = [row_of(own, r) for r in range(BLOCK)]
        near = range(block + 1, min(block + 1 + AHEAD, count))
        weights = {k: [lanes_of(tiles[k], offset + c) for c in range(BLOCK)] for k in near}
        if block + 1 < count:
            columns = [lanes_of(tiles[block + 1], offset + BLOCK + c) for c in range(BLOCK)]
        for k in near:
            tiles[k] = jnp.where(in_block, 0.0, tiles[k])
        inverse, scaled = [], {}
        for i in range(BLOCK):
            inv = pl.reciprocal(entry[i, i], approx=True)
            inverse.append(inv)
            if i + 1 < BLOCK:
                square = entry[i, i + 1] * entry[i, i + 1]
                entry[i + 1, i + 1] = entry[i + 1, i + 1] - square * inv
            for r in range(i + 1, BLOCK):
                scaled[r, i] = entry[i, r] * inv
            for r in range(i + 1, BLOCK):
                for c in range(r, BLOCK):
                    if (r, c) != (i + 1, i + 1):
                        entry[r, c] = entry[r, c] - scaled[r, i] * entry[i, c]
            for k in near:
                here = weights[k][i]
                weight = here * inv
                if k == block + 1:
                    for c in range(BLOCK):
                        columns[c] = columns[c] - weight * row_of(here, c)
                for c in range(i + 1, BLOCK):
                    weights[k][c] = weights[k][c] - here * scaled[c, i]
                tiles[k] = tiles[k] - weight * rows[i]
            for r in range(i + 1, BLOCK):
                rows[r] = rows[r] - scaled[r, i] * rows[i]
                kept[r] = kept[r] - scaled[r, i] * kept[i]
        root = gather([lax.rsqrt(entry[i, i]) for i in range(BLOCK)])
        merged = gather(rows) * root
        diagonal = gather(kept) * root
        lower_rows.append(jnp.where(spread_ids <= offset, merged, 0.0))
        upper_rows.append(jnp.where(spread_ids >= offset, jnp.where(in_block, diagonal, merged), 0.0))
        if block + 1 + AHEAD < count:
            solved = [None] * BLOCK
            for r in reversed(range(BLOCK)):
                solved[r] = rows[r] * inverse[r]
                for c in range(r + 1, BLOCK):
                    solved[r] = solved[r] - scaled[c, r] * solved[c]
            for k in range(block + 1 + AHEAD, count):
                terms = [lanes_of(tiles[k], offset + c) * solved[c] for c in range(BLOCK)]
                while len(terms) > 1:
                    terms = [terms[t] + terms[t + 1] for t in range(0, len(terms), 2)]
                tiles[k] = jnp.where(in_block, 0.0, tiles[k]) - terms[0]
    return jnp.concatenate(upper_rows, axis=0), jnp.concatenate(lower_rows, axis=0)


def packed_rows(order, probes):
    return -(-(order // 2 + probes + 1) // (2 * BLOCK)) * 2 * BLOCK


def live_volumes(volumes_ref, live_ref, begin):
    ids = lax.broadcasted_iota(jnp.int32, (1, LANES), 1) + begin
    part = volumes_ref[pl.ds(begin, LANES)].reshape(1, LANES)
    return jnp.where(ids < live_ref[0], part, 0.0)


def sums_kernel(total_rows, snapshots_hbm, volumes_hbm, live_ref, probes_hbm, core_ref, keep_ref, send_ref, snapshots_ref, volumes_ref, probes_ref, packed, sems):
    copies = [
        pltpu.make_async_copy(source, target, sems.at[i])
        for i, (source, target) in enumerate(
            ((volumes_hbm, volumes_ref), (snapshots_hbm, snapshots_ref), (probes_hbm, probes_ref))
        )
    ]
    for copy in copies:
        copy.start()
    row_count, order = snapshots_ref.shape
    probes = probes_ref.shape[0]
    half = order // 2
    copies[0].wait()
    volume = jnp.concatenate([live_volumes(volumes_ref, live_ref, b) for b in range(0, row_count, LANES)], axis=1)
    copies[1].wait()
    snapshots = snapshots_ref[...]
    scaled = snapshots.T * (volume * (1.0 / total_rows))
    gram = product(scaled, snapshots, ((1,), (0,)))
    row_ids = lax.broadcasted_iota(jnp.int32, (half, half), 0)
    column_ids = lax.broadcasted_iota(jnp.int32, (half, half), 1)
    packed[:half, :half] = jnp.where(row_ids <= column_ids, gram[:half, :half], gram[half:, half:])
    packed[:half, half:] = gram[:half, half:]
    rest = packed.shape[0] - half - probes
    diagonal = jnp.sum(jnp.where(row_ids == column_ids, gram[half:, half:], 0.0), axis=0, keepdims=True)
    packed[half + probes :, :] = jnp.concatenate([jnp.broadcast_to(diagonal, (rest, half))] * 2, axis=1)
    copies[2].wait()
    probe_scaled = probes_ref[...] * (volume * (1.0 / total_rows**0.5))
    packed[half : half + probes, :] = product(probe_scaled, snapshots, ((1,), (0,)))
    middle = packed.shape[0] // 2
    low = core_ref[0] == 0

    @pl.when(low)
    def _():
        keep_ref[...] = packed[:middle, :]
        send_ref[...] = packed[middle:, :]

    @pl.when(jnp.logical_not(low))
    def _():
        keep_ref[...] = packed[middle:, :]
        send_ref[...] = packed[:middle, :]


def local_sums(total_rows, snapshots, volumes, live_rows, probes, core):
    order = snapshots.shape[1]
    size = packed_rows(order, probes.shape[0])
    hbm = pl.BlockSpec(memory_space=pltpu.HBM)
    whole = pl.BlockSpec(memory_space=pltpu.VMEM)
    scalar = pl.BlockSpec(memory_space=pltpu.SMEM)
    return pl.pallas_call(
        functools.partial(sums_kernel, total_rows),
        out_shape=(jax.ShapeDtypeStruct((size // 2, order), F32),) * 2,
        in_specs=[hbm, hbm, scalar, hbm, scalar],
        out_specs=(whole, whole),
        scratch_shapes=[
            pltpu.VMEM(snapshots.shape, F32),
            pltpu.VMEM(volumes.shape, F32),
            pltpu.VMEM(probes.shape, F32),
            pltpu.VMEM((size, order), F32),
            pltpu.SemaphoreType.DMA((3,)),
        ],
        compiler_params=pltpu.CompilerParams(vmem_limit_bytes=60 * 1024 * 1024),
    )(snapshots, volumes, live_rows, probes, core)


def finish_kernel(mine_ref, other_ref, snapshots_ref, volumes_ref, live_ref, core_ref, basis_ref, factor_ref, coef_ref):
    row_count, order = snapshots_ref.shape
    probes = coef_ref.shape[0]
    half = order // 2
    low = core_ref[0] == 0
    mine, other = mine_ref[...], other_ref[...]
    packed = jnp.concatenate([jnp.where(low, mine, other), jnp.where(low, other, mine)], axis=0)
    row_ids = lax.broadcasted_iota(jnp.int32, (half, half), 0)
    column_ids = lax.broadcasted_iota(jnp.int32, (half, half), 1)
    square = packed[:half, :half]
    turned = square.T
    cross = packed[half : half + probes, :]
    diagonal = packed[half + probes : half + probes + 1, :half]

    upper, inverse = eliminate(jnp.where(row_ids <= column_ids, square, turned))
    factor_ref[:half, :half] = upper
    factor_ref[half:, :half] = jnp.zeros((half, half), F32)
    beside = product(inverse, packed[:half, half:], ((1,), (0,)))
    factor_ref[:half, half:] = beside
    second = jnp.where(row_ids > column_ids, square, turned)
    second = jnp.where(row_ids == column_ids, diagonal, second) - product(beside, beside, ((0,), (0,)))

    def first_columns(block):
        left = product(block[:, :half], inverse, ((1,), (1,)))
        return left, block[:, half:] - product(left, beside, ((1,), (0,)))

    left, cross_rest = first_columns(cross)
    coef_ref[:, :half] = left
    rest = []
    for begin in range(0, row_count, LANES):
        scale = jnp.sqrt(live_volumes(volumes_ref, live_ref, begin))
        scale = jnp.broadcast_to(scale, (LANES, LANES)).T
        weighted = snapshots_ref[begin : begin + LANES, :] * jnp.concatenate([scale] * (order // LANES), axis=1)
        left, right = first_columns(weighted)
        basis_ref[begin : begin + LANES, :half] = left
        rest.append(right)

    upper, inverse_second = eliminate(second)
    factor_ref[half:, half:] = upper
    coef_ref[:, half:] = product(cross_rest, inverse_second, ((1,), (1,)))
    for begin in range(0, row_count, LANES):
        basis_ref[begin : begin + LANES, half:] = product(rest[begin // LANES], inverse_second, ((1,), (1,)))


def finish(mine, other, snapshots, volumes, live_rows, core, probes):
    row_count, order = snapshots.shape
    whole = pl.BlockSpec(memory_space=pltpu.VMEM)
    scalar = pl.BlockSpec(memory_space=pltpu.SMEM)
    return pl.pallas_call(
        finish_kernel,
        out_shape=(
            jax.ShapeDtypeStruct((row_count, order), F32),
            jax.ShapeDtypeStruct((order, order), F32),
            jax.ShapeDtypeStruct((probes, order), F32),
        ),
        in_specs=[whole] * 4 + [scalar] * 2,
        out_specs=(whole,) * 3,
        compiler_params=pltpu.CompilerParams(vmem_limit_bytes=32 * 1024 * 1024),
    )(mine, other, snapshots, volumes, live_rows, core)


def exchange(value, bits):
    count = lax.axis_size("cells") * lax.axis_size("sub")
    return lax.ppermute(value, ("cells", "sub"), [(i, i ^ bits[i % 2]) for i in range(count)])


def reduce_halves(keep, send):
    count = lax.axis_size("cells") * lax.axis_size("sub")
    bits = [1 << k for k in range(1, count.bit_length() - 1)]
    split = len(bits) // 2
    mine = keep + exchange(send, (1, 1))
    for first, second in zip(bits[:split], bits[split : 2 * split]):
        mine = mine + exchange(mine, (first, second))
        mine = mine + exchange(mine, (second, first))
    for bit in bits[2 * split :]:
        mine = mine + exchange(mine, (bit, bit))
    return mine, exchange(mine, (1, 1))


def per_device(snapshots, volumes, live_rows, probes):
    count = lax.axis_size("cells") * lax.axis_size("sub")
    core = (lax.axis_index("sub") % 2).astype(jnp.int32).reshape(1)
    keep, send = local_sums(snapshots.shape[0] * count, snapshots, volumes, live_rows, probes, core)
    mine, other = reduce_halves(keep, send)
    return finish(mine, other, snapshots, volumes, live_rows, core, probes.shape[0])


def solution(mesh):
    placed = (
        P(("cells", "sub"), None),
        P(("cells", "sub")),
        P(("cells", "sub")),
        P(None, ("cells", "sub")),
    )
    return jax.shard_map(
        per_device,
        mesh=mesh,
        in_specs=placed,
        out_specs=(P(("cells", "sub"), None), P(), P()),
        check_vma=False,
    )
```

time: 43.7 us -> 38.7 us (0.89)
  Pallas kernels: 15.2 us -> 11.8 us
  local copies, waits for them, and re-layouts: 2.62 us -> 0.01 us
  other arithmetic: 0.08 us -> 0.98 us
    pallas_call x1, Pallas kernels: 14.3 us -> 8.67 us  [finish(): pl.pallas_call(finish_kernel, out_shape=(jax.ShapeDtypeStruct((row_count,...]
    unnamed x8 -> x4, local copies, waits for them, and re-layouts: 2.62 us -> 0.01 us
    pallas_call x1, Pallas kernels: 0.9 us -> 3.16 us  [local_sums(): pl.pallas_call(functools.partial(sums_kernel, total_rows), out_shape=(jax...]
    add x1, other arithmetic: 0.01 us -> 0.91 us  [reduce_halves(): mine = keep + exchange(send, (1, 1))]
where the time goes in v4:
time: 38.7 us; the launch traced here: 38.2 us
  waiting for transfers between devices  13.3 us (34%)
  Pallas kernels  11.8 us (30%)
  starting transfers between devices  10.8 us (28%)
  between operations  1.33 us (3%)
  other arithmetic  0.98 us (3%)
    ppermute x6, waiting for transfers between devices, exchange(): lax.ppermute(value, ('cells', 'sub'), [(i, i ^ bits[i % 2]) for i in rang...  13.3 us
    ppermute x6, starting transfers between devices, exchange(): lax.ppermute(value, ('cells', 'sub'), [(i, i ^ bits[i % 2]) for i in rang...  10.8 us
    pallas_call x1, Pallas kernels, finish(): pl.pallas_call(finish_kernel, out_shape=(jax.ShapeDtypeStruct((row_count,...  8.67 us
    pallas_call x1, Pallas kernels, local_sums(): pl.pallas_call(functools.partial(sums_kernel, total_rows), out_shape=(jax...  3.16 us
    add x1, other arithmetic, reduce_halves(): mine = keep + exchange(send, (1, 1))  0.91 us
  transfers between devices with their start and end apart: 6, of which 6 were waited for; matrix products, arithmetic and copies ran while one was open for 0% of the time, Pallas kernels for 0%

profile of v4, /device:TPU:0, one launch (start us, length us, event | category | flops | bytes accessed | tf_op | source)
XLA Modules:
  0.0 38.2 jit_solution(16997979863105098201)
XLA Ops:
  1.3 3.2 %shard_map.67 = (f32[104,256]{1,0:T(8,128)}, f32[104,256]{1,0:T(8,128)}) custom-call(f32[512,256]{1,0:T(8,128)} %snapshots_ref.1, f32[512]{0:T(512)} %volumes_ref.1, s32[1]{0:T(128)S(6)} %copy.7.live_ref, f32[64,512]{1,0:T(8,128)} %probes_hbm.1, s32[1]{0:T(128)} %bitcast.core_ref), custom_call_target="tpu_custom_call" | custom-call | tf_op jit(solution)/shard_map/pallas_call | solution.py:161
  4.5 0.5 %collective-permute-start = (f32[104,256]{1,0:T(8,128)}, f32[104,256]{1,0:T(8,128)S(1)}, u32[]{:S(2)}, u32[]{:S(2)}) collective-permute-start(f32[104,256]{1,0:T(8,128)} %get-tuple-element.6), channel_id=1, source_target_pairs={{0,1},{1,0},{2,3},{3,2},{4,5},{5,4},{6,7},{7,6},{8,9},{9,8},{10,11... | collective-permute-start | bytes 319496 | tf_op jit(solution)/shard_map/ppermute | solution.py:240
  5.0 1.2 %collective-permute-done = f32[104,256]{1,0:T(8,128)S(1)} collective-permute-done((f32[104,256]{1,0:T(8,128)}, f32[104,256]{1,0:T(8,128)S(1)}, u32[]{:S(2)}, u32[]{:S(2)}) %collective-permute-start) | collective-permute-done | bytes 106528 | tf_op jit(solution)/shard_map/ppermute | solution.py:240
  6.1 0.9 %add.20 = f32[104,256]{1,0:T(8,128)S(1)} add(f32[104,256]{1,0:T(8,128)} %get-tuple-element.5, f32[104,256]{1,0:T(8,128)S(1)} %collective-permute-done) | non-fusion elementwise | flops 26624 | bytes 319488 | tf_op jit(solution)/shard_map/add | solution.py:247
  7.1 2.9 %collective-permute-start.1 = (f32[104,256]{1,0:T(8,128)S(1)}, f32[104,256]{1,0:T(8,128)S(1)}, u32[]{:S(2)}, u32[]{:S(2)}) collective-permute-start(f32[104,256]{1,0:T(8,128)S(1)} %add.20), channel_id=1, source_target_pairs={{0,2},{1,9},{2,0},{3,11},{4,6},{5,13},{6,4},{7,15},{8,10},{9,1},{1... | collective-permute-start | bytes 319496 | tf_op jit(solution)/shard_map/ppermute | solution.py:240
  10.0 2.7 %collective-permute-done.1 = f32[104,256]{1,0:T(8,128)S(1)} collective-permute-done((f32[104,256]{1,0:T(8,128)S(1)}, f32[104,256]{1,0:T(8,128)S(1)}, u32[]{:S(2)}, u32[]{:S(2)}) %collective-permute-start.1) | collective-permute-done | bytes 106528 | tf_op jit(solution)/shard_map/ppermute | solution.py:240
  12.7 0.0 copy-start
  12.7 2.2 %collective-permute-start.2 = (f32[104,256]{1,0:T(8,128)S(1)}, f32[104,256]{1,0:T(8,128)S(1)}, u32[]{:S(2)}, u32[]{:S(2)}) collective-permute-start(f32[104,256]{1,0:T(8,128)S(1)} %add.21), channel_id=1, source_target_pairs={{0,8},{1,3},{2,10},{3,1},{4,12},{5,7},{6,14},{7,5},{8,0},{9,11},{1... | collective-permute-start | bytes 319496 | tf_op jit(solution)/shard_map/ppermute | solution.py:240
  14.8 2.7 %collective-permute-done.2 = f32[104,256]{1,0:T(8,128)S(1)} collective-permute-done((f32[104,256]{1,0:T(8,128)S(1)}, f32[104,256]{1,0:T(8,128)S(1)}, u32[]{:S(2)}, u32[]{:S(2)}) %collective-permute-start.2) | collective-permute-done | bytes 106528 | tf_op jit(solution)/shard_map/ppermute | solution.py:240
  17.5 2.0 %collective-permute-start.3 = (f32[104,256]{1,0:T(8,128)S(1)}, f32[104,256]{1,0:T(8,128)S(1)}, u32[]{:S(2)}, u32[]{:S(2)}) collective-permute-start(f32[104,256]{1,0:T(8,128)S(1)} %add.22), channel_id=1, source_target_pairs={{0,4},{1,17},{2,6},{3,19},{4,0},{5,21},{6,2},{7,23},{8,12},{9,25},... | collective-permute-start | bytes 319496 | tf_op jit(solution)/shard_map/ppermute | solution.py:240
  19.6 2.7 %collective-permute-done.3 = f32[104,256]{1,0:T(8,128)S(1)} collective-permute-done((f32[104,256]{1,0:T(8,128)S(1)}, f32[104,256]{1,0:T(8,128)S(1)}, u32[]{:S(2)}, u32[]{:S(2)}) %collective-permute-start.3) | collective-permute-done | bytes 106528 | tf_op jit(solution)/shard_map/ppermute | solution.py:240
  22.3 0.0 copy-start.1
  22.3 3.1 %collective-permute-start.4 = (f32[104,256]{1,0:T(8,128)S(1)}, f32[104,256]{1,0:T(8,128)S(1)}, u32[]{:S(2)}, u32[]{:S(2)}) collective-permute-start(f32[104,256]{1,0:T(8,128)S(1)} %add.23), channel_id=1, source_target_pairs={{0,16},{1,5},{2,18},{3,7},{4,20},{5,1},{6,22},{7,3},{8,24},{9,13},... | collective-permute-start | bytes 319496 | tf_op jit(solution)/shard_map/ppermute | solution.py:240
  25.4 2.7 %collective-permute-done.4 = f32[104,256]{1,0:T(8,128)S(1)} collective-permute-done((f32[104,256]{1,0:T(8,128)S(1)}, f32[104,256]{1,0:T(8,128)S(1)}, u32[]{:S(2)}, u32[]{:S(2)}) %collective-permute-start.4) | collective-permute-done | bytes 106528 | tf_op jit(solution)/shard_map/ppermute | solution.py:240
  28.1 0.1 collective-permute-start.5
  28.2 1.3 %collective-permute-done.5.other_ref = f32[104,256]{1,0:T(8,128)S(1)} collective-permute-done((f32[104,256]{1,0:T(8,128)S(1)}, f32[104,256]{1,0:T(8,128)S(1)}, u32[]{:S(2)}, u32[]{:S(2)}) %collective-permute-start.5) | collective-permute-done | bytes 106528 | tf_op jit(solution)/shard_map/ppermute | solution.py:240
  29.5 0.0 copy-done
  29.5 0.0 copy-done.1
  29.5 8.7 %shard_map.68 = (f32[512,256]{1,0:T(8,128)}, f32[256,256]{1,0:T(8,128)}, f32[64,256]{1,0:T(8,128)}) custom-call(f32[104,256]{1,0:T(8,128)S(1)} %add.24.mine_ref, f32[104,256]{1,0:T(8,128)S(1)} %collective-permute-done.5.other_ref, f32[512,256]{1,0:T(8,128)S(1)} %copy-done, f32[512]{0:T(512)S(1)} %copy-done.1, s32[1]{0:T(128)S(6)} %copy.7.live_ref, ...), custom_call_target="tpu_custom_call" | custom-call | tf_op jit(solution)/shard_map/pallas_call | solution.py:225
  (4 shorter events, 0.1 us)
Async XLA Ops:
  4.5 1.7 %collective-permute-start = (f32[104,256]{1,0:T(8,128)}, f32[104,256]{1,0:T(8,128)S(1)}, u32[]{:S(2)}, u32[]{:S(2)}) collective-permute-start(f32[104,256]{1,0:T(8,128)} %get-tuple-element.6), channel_id=1, source_target_pairs={{0,1},{1,0},{2,3},{3,2},{4,5},{5,4},{6,7},{7,6},{8,9},{9,8},{10,11... | collective-permute-start | bytes 319496 | tf_op jit(solution)/shard_map/ppermute | solution.py:240
  7.1 5.6 %collective-permute-start.1 = (f32[104,256]{1,0:T(8,128)S(1)}, f32[104,256]{1,0:T(8,128)S(1)}, u32[]{:S(2)}, u32[]{:S(2)}) collective-permute-start(f32[104,256]{1,0:T(8,128)S(1)} %add.20), channel_id=1, source_target_pairs={{0,2},{1,9},{2,0},{3,11},{4,6},{5,13},{6,4},{7,15},{8,10},{9,1},{1... | collective-permute-start | bytes 319496 | tf_op jit(solution)/shard_map/ppermute | solution.py:240
  12.7 16.9 %copy-start = (f32[512,256]{1,0:T(8,128)S(1)}, f32[512,256]{1,0:T(8,128)}, u32[]{:S(2)}) copy-start(f32[512,256]{1,0:T(8,128)} %snapshots_ref.1) | copy-start | bytes 1572868
  12.7 4.9 %collective-permute-start.2 = (f32[104,256]{1,0:T(8,128)S(1)}, f32[104,256]{1,0:T(8,128)S(1)}, u32[]{:S(2)}, u32[]{:S(2)}) collective-permute-start(f32[104,256]{1,0:T(8,128)S(1)} %add.21), channel_id=1, source_target_pairs={{0,8},{1,3},{2,10},{3,1},{4,12},{5,7},{6,14},{7,5},{8,0},{9,11},{1... | collective-permute-start | bytes 319496 | tf_op jit(solution)/shard_map/ppermute | solution.py:240
  17.5 4.8 %collective-permute-start.3 = (f32[104,256]{1,0:T(8,128)S(1)}, f32[104,256]{1,0:T(8,128)S(1)}, u32[]{:S(2)}, u32[]{:S(2)}) collective-permute-start(f32[104,256]{1,0:T(8,128)S(1)} %add.22), channel_id=1, source_target_pairs={{0,4},{1,17},{2,6},{3,19},{4,0},{5,21},{6,2},{7,23},{8,12},{9,25},... | collective-permute-start | bytes 319496 | tf_op jit(solution)/shard_map/ppermute | solution.py:240
  22.3 7.2 %copy-start.1 = (f32[512]{0:T(512)S(1)}, f32[512]{0:T(512)}, u32[]{:S(2)}) copy-start(f32[512]{0:T(512)} %volumes_ref.1) | copy-start | bytes 6148
  22.3 5.8 %collective-permute-start.4 = (f32[104,256]{1,0:T(8,128)S(1)}, f32[104,256]{1,0:T(8,128)S(1)}, u32[]{:S(2)}, u32[]{:S(2)}) collective-permute-start(f32[104,256]{1,0:T(8,128)S(1)} %add.23), channel_id=1, source_target_pairs={{0,16},{1,5},{2,18},{3,7},{4,20},{5,1},{6,22},{7,3},{8,24},{9,13},... | collective-permute-start | bytes 319496 | tf_op jit(solution)/shard_map/ppermute | solution.py:240
  28.1 1.4 %collective-permute-start.5 = (f32[104,256]{1,0:T(8,128)S(1)}, f32[104,256]{1,0:T(8,128)S(1)}, u32[]{:S(2)}, u32[]{:S(2)}) collective-permute-start(f32[104,256]{1,0:T(8,128)S(1)} %add.24.mine_ref), channel_id=1, source_target_pairs={{0,1},{1,0},{2,3},{3,2},{4,5},{5,4},{6,7},{7,6},{8,9},{9,8},{10,11... | collective-permute-start | bytes 319496 | tf_op jit(solution)/shard_map/ppermute | solution.py:240

commit v5 on v4

--- a/solution.py
+++ b/solution.py
@@ -110,7 +110,7 @@
     return jnp.where(ids < live_ref[0], part, 0.0)
 
 
-def sums_kernel(total_rows, snapshots_hbm, volumes_hbm, live_ref, probes_hbm, core_ref, keep_ref, send_ref, snapshots_ref, volumes_ref, probes_ref, packed, sems):
+def sums_kernel(total_rows, snapshots_hbm, volumes_hbm, live_ref, probes_hbm, part_ref, keep_ref, send_ref, snapshots_ref, volumes_ref, probes_ref, packed, sems):
     copies = [
         pltpu.make_async_copy(source, target, sems.at[i])
         for i, (source, target) in enumerate(
@@ -139,7 +139,7 @@
     probe_scaled = probes_ref[...] * (volume * (1.0 / total_rows**0.5))
     packed[half : half + probes, :] = product(probe_scaled, snapshots, ((1,), (0,)))
     middle = packed.shape[0] // 2
-    low = core_ref[0] == 0
+    low = part_ref[0] == 0
 
     @pl.when(low)
     def _():
@@ -152,7 +152,7 @@
         send_ref[...] = packed[:middle, :]
 
 
-def local_sums(total_rows, snapshots, volumes, live_rows, probes, core):
+def local_sums(total_rows, snapshots, volumes, live_rows, probes, part):
     order = snapshots.shape[1]
     size = packed_rows(order, probes.shape[0])
     hbm = pl.BlockSpec(memory_space=pltpu.HBM)
@@ -170,15 +170,15 @@
             pltpu.VMEM((size, order), F32),
             pltpu.SemaphoreType.DMA((3,)),
         ],
-        compiler_params=pltpu.CompilerParams(vmem_limit_bytes=60 * 1024 * 1024),
-    )(snapshots, volumes, live_rows, probes, core)
-
-
-def finish_kernel(mine_ref, other_ref, snapshots_ref, volumes_ref, live_ref, core_ref, basis_ref, factor_ref, coef_ref):
+        compiler_params=pltpu.CompilerParams(vmem_limit_bytes=54950 * 1024),
+    )(snapshots, volumes, live_rows, probes, part)
+
+
+def finish_kernel(mine_ref, other_ref, snapshots_ref, volumes_ref, live_ref, part_ref, basis_ref, factor_ref, coef_ref):
     row_count, order = snapshots_ref.shape
     probes = coef_ref.shape[0]
     half = order // 2
-    low = core_ref[0] == 0
+    low = part_ref[0] == 0
     mine, other = mine_ref[...], other_ref[...]
     packed = jnp.concatenate([jnp.where(low, mine, other), jnp.where(low, other, mine)], axis=0)
     row_ids = lax.broadcasted_iota(jnp.int32, (half, half), 0)
@@ -218,7 +218,7 @@
         basis_ref[begin : begin + LANES, half:] = product(rest[begin // LANES], inverse_second, ((1,), (1,)))
 
 
-def finish(mine, other, snapshots, volumes, live_rows, core, probes):
+def finish(mine, other, snapshots, volumes, live_rows, part, probes):
     row_count, order = snapshots.shape
     whole = pl.BlockSpec(memory_space=pltpu.VMEM)
     scalar = pl.BlockSpec(memory_space=pltpu.SMEM)
@@ -232,33 +232,35 @@
         in_specs=[whole] * 4 + [scalar] * 2,
         out_specs=(whole,) * 3,
         compiler_params=pltpu.CompilerParams(vmem_limit_bytes=32 * 1024 * 1024),
-    )(mine, other, snapshots, volumes, live_rows, core)
+    )(mine, other, snapshots, volumes, live_rows, part)
 
 
 def exchange(value, bits):
     count = lax.axis_size("cells") * lax.axis_size("sub")
-    return lax.ppermute(value, ("cells", "sub"), [(i, i ^ bits[i % 2]) for i in range(count)])
+    pairs = [(i, i ^ 1 ^ bits[bin(i).count("1") % 2]) for i in range(count)]
+    return lax.ppermute(value, ("cells", "sub"), pairs)
 
 
 def reduce_halves(keep, send):
     count = lax.axis_size("cells") * lax.axis_size("sub")
     bits = [1 << k for k in range(1, count.bit_length() - 1)]
     split = len(bits) // 2
-    mine = keep + exchange(send, (1, 1))
+    mine = keep + exchange(send, (0, 0))
     for first, second in zip(bits[:split], bits[split : 2 * split]):
         mine = mine + exchange(mine, (first, second))
         mine = mine + exchange(mine, (second, first))
     for bit in bits[2 * split :]:
         mine = mine + exchange(mine, (bit, bit))
-    return mine, exchange(mine, (1, 1))
+    return mine, exchange(mine, (0, 0))
 
 
 def per_device(snapshots, volumes, live_rows, probes):
     count = lax.axis_size("cells") * lax.axis_size("sub")
-    core = (lax.axis_index("sub") % 2).astype(jnp.int32).reshape(1)
-    keep, send = local_sums(snapshots.shape[0] * count, snapshots, volumes, live_rows, probes, core)
+    index = lax.axis_index("cells") * lax.axis_size("sub") + lax.axis_index("sub")
+    part = (lax.population_count(index.astype(jnp.int32)) % 2).reshape(1)
+    keep, send = local_sums(snapshots.shape[0] * count, snapshots, volumes, live_rows, probes, part)
     mine, other = reduce_halves(keep, send)
-    return finish(mine, other, snapshots, volumes, live_rows, core, probes.shape[0])
+    return finish(mine, other, snapshots, volumes, live_rows, part, probes.shape[0])
 
 
 def solution(mesh):

time: 38.7 us -> 36.1 us (0.933)
  waiting for transfers between devices: 13.3 us -> 11.5 us
  other arithmetic: 0.98 us -> 0.08 us
  Pallas kernels: 11.8 us -> 11.1 us
  local copies, waits for them, and re-layouts: 0.01 us -> 0.68 us
  starting transfers between devices: 10.8 us -> 11.2 us
    ppermute x6, waiting for transfers between devices: 13.3 us -> 11.5 us  [exchange(): return lax.ppermute(value, ('cells', 'sub'), pairs)]
    add x1, other arithmetic: 0.91 us -> 0.01 us  [reduce_halves(): mine = keep + exchange(send, (0, 0))]
    pallas_call x1, Pallas kernels: 3.16 us -> 2.46 us  [local_sums(): pl.pallas_call(functools.partial(sums_kernel, total_rows), out_shape=(jax...]
    unnamed x4, local copies, waits for them, and re-layouts: 0.01 us -> 0.68 us
    ppermute x6, starting transfers between devices: 10.8 us -> 11.2 us  [exchange(): return lax.ppermute(value, ('cells', 'sub'), pairs)]
where the time goes in v5:
time: 36.1 us; the launch traced here: 36 us
  waiting for transfers between devices  11.5 us (32%)
  starting transfers between devices  11.2 us (31%)
  Pallas kernels  11.1 us (31%)
  between operations  1.34 us (4%)
  local copies, waits for them, and re-layouts  0.68 us (2%)
    ppermute x6, waiting for transfers between devices, exchange(): return lax.ppermute(value, ('cells', 'sub'), pairs)  11.5 us
    ppermute x6, starting transfers between devices, exchange(): return lax.ppermute(value, ('cells', 'sub'), pairs)  11.2 us
    pallas_call x1, Pallas kernels, finish(): pl.pallas_call(finish_kernel, out_shape=(jax.ShapeDtypeStruct((row_count,...  8.67 us
    pallas_call x1, Pallas kernels, local_sums(): pl.pallas_call(functools.partial(sums_kernel, total_rows), out_shape=(jax...  2.46 us
  transfers between devices with their start and end apart: 6, of which 6 were waited for; matrix products, arithmetic and copies ran while one was open for 0% of the time, Pallas kernels for 0%

profile of v5, /device:TPU:0, one launch (start us, length us, event | category | flops | bytes accessed | tf_op | source)
XLA Modules:
  0.0 36.0 jit_solution(162960238578309602)
XLA Ops:
  1.3 0.0 copy-start.1
  1.3 0.7 %copy-done.1 = f32[512]{0:T(512)S(1)} copy-done((f32[512]{0:T(512)S(1)}, f32[512]{0:T(512)}, u32[]{:S(2)}) %copy-start.1) | copy-done | bytes 2072
  2.0 2.5 %shard_map.67 = (f32[104,256]{1,0:T(8,128)S(1)}, f32[104,256]{1,0:T(8,128)S(1)}) custom-call(f32[512,256]{1,0:T(8,128)} %snapshots_ref.1, f32[512]{0:T(512)S(1)} %copy-done.1, s32[1]{0:T(128)S(6)} %copy.7.live_ref, f32[64,512]{1,0:T(8,128)} %probes_hbm.1, s32[1]{0:T(128)} %bitcast.part_ref), custom_call_target="tpu_custom_call" | custom-call | tf_op jit(solution)/shard_map/pallas_call | solution.py:161
  4.4 0.5 %collective-permute-start = (f32[104,256]{1,0:T(8,128)S(1)}, f32[104,256]{1,0:T(8,128)S(1)}, u32[]{:S(2)}, u32[]{:S(2)}) collective-permute-start(f32[104,256]{1,0:T(8,128)S(1)} %get-tuple-element.6), channel_id=1, source_target_pairs={{0,1},{1,0},{2,3},{3,2},{4,5},{5,4},{6,7},{7,6},{8,9},{9,8},{10,11... | collective-permute-start | bytes 319496 | tf_op jit(solution)/shard_map/ppermute | solution.py:241
  5.0 1.0 %collective-permute-done = f32[104,256]{1,0:T(8,128)S(1)} collective-permute-done((f32[104,256]{1,0:T(8,128)S(1)}, f32[104,256]{1,0:T(8,128)S(1)}, u32[]{:S(2)}, u32[]{:S(2)}) %collective-permute-start) | collective-permute-done | bytes 106528 | tf_op jit(solution)/shard_map/ppermute | solution.py:241
  5.9 2.7 %collective-permute-start.1 = (f32[104,256]{1,0:T(8,128)S(1)}, f32[104,256]{1,0:T(8,128)S(1)}, u32[]{:S(2)}, u32[]{:S(2)}) collective-permute-start(f32[104,256]{1,0:T(8,128)S(1)} %add.24), channel_id=1, source_target_pairs={{0,3},{1,8},{2,11},{3,0},{4,13},{5,6},{6,5},{7,14},{8,1},{9,10},{1... | collective-permute-start | bytes 319496 | tf_op jit(solution)/shard_map/ppermute | solution.py:241
  8.6 2.4 %collective-permute-done.1 = f32[104,256]{1,0:T(8,128)S(1)} collective-permute-done((f32[104,256]{1,0:T(8,128)S(1)}, f32[104,256]{1,0:T(8,128)S(1)}, u32[]{:S(2)}, u32[]{:S(2)}) %collective-permute-start.1) | collective-permute-done | bytes 106528 | tf_op jit(solution)/shard_map/ppermute | solution.py:241
  11.0 0.0 copy-start
  11.0 1.9 %collective-permute-start.2 = (f32[104,256]{1,0:T(8,128)S(1)}, f32[104,256]{1,0:T(8,128)S(1)}, u32[]{:S(2)}, u32[]{:S(2)}) collective-permute-start(f32[104,256]{1,0:T(8,128)S(1)} %add.25), channel_id=1, source_target_pairs={{0,9},{1,2},{2,1},{3,10},{4,7},{5,12},{6,15},{7,4},{8,11},{9,0},{1... | collective-permute-start | bytes 319496 | tf_op jit(solution)/shard_map/ppermute | solution.py:241
  12.9 2.4 %collective-permute-done.2 = f32[104,256]{1,0:T(8,128)S(1)} collective-permute-done((f32[104,256]{1,0:T(8,128)S(1)}, f32[104,256]{1,0:T(8,128)S(1)}, u32[]{:S(2)}, u32[]{:S(2)}) %collective-permute-start.2) | collective-permute-done | bytes 106528 | tf_op jit(solution)/shard_map/ppermute | solution.py:241
  15.3 1.8 %collective-permute-start.3 = (f32[104,256]{1,0:T(8,128)S(1)}, f32[104,256]{1,0:T(8,128)S(1)}, u32[]{:S(2)}, u32[]{:S(2)}) collective-permute-start(f32[104,256]{1,0:T(8,128)S(1)} %add.26), channel_id=1, source_target_pairs={{0,5},{1,16},{2,19},{3,6},{4,21},{5,0},{6,3},{7,22},{8,25},{9,12},... | collective-permute-start | bytes 319496 | tf_op jit(solution)/shard_map/ppermute | solution.py:241
  17.1 2.4 %collective-permute-done.3 = f32[104,256]{1,0:T(8,128)S(1)} collective-permute-done((f32[104,256]{1,0:T(8,128)S(1)}, f32[104,256]{1,0:T(8,128)S(1)}, u32[]{:S(2)}, u32[]{:S(2)}) %collective-permute-start.3) | collective-permute-done | bytes 106528 | tf_op jit(solution)/shard_map/ppermute | solution.py:241
  19.5 3.1 %collective-permute-start.4 = (f32[104,256]{1,0:T(8,128)S(1)}, f32[104,256]{1,0:T(8,128)S(1)}, u32[]{:S(2)}, u32[]{:S(2)}) collective-permute-start(f32[104,256]{1,0:T(8,128)S(1)} %add.27), channel_id=1, source_target_pairs={{0,17},{1,4},{2,7},{3,18},{4,1},{5,20},{6,23},{7,2},{8,13},{9,24},... | collective-permute-start | bytes 319496 | tf_op jit(solution)/shard_map/ppermute | solution.py:241
  22.7 2.4 %collective-permute-done.4 = f32[104,256]{1,0:T(8,128)S(1)} collective-permute-done((f32[104,256]{1,0:T(8,128)S(1)}, f32[104,256]{1,0:T(8,128)S(1)}, u32[]{:S(2)}, u32[]{:S(2)}) %collective-permute-start.4) | collective-permute-done | bytes 106528 | tf_op jit(solution)/shard_map/ppermute | solution.py:241
  25.1 1.3 %collective-permute-start.5 = (f32[104,256]{1,0:T(8,128)S(1)}, f32[104,256]{1,0:T(8,128)S(1)}, u32[]{:S(2)}, u32[]{:S(2)}) collective-permute-start(f32[104,256]{1,0:T(8,128)S(1)} %add.28.mine_ref), channel_id=1, source_target_pairs={{0,1},{1,0},{2,3},{3,2},{4,5},{5,4},{6,7},{7,6},{8,9},{9,8},{10,11... | collective-permute-start | bytes 319496 | tf_op jit(solution)/shard_map/ppermute | solution.py:241
  26.3 1.0 %collective-permute-done.5.other_ref = f32[104,256]{1,0:T(8,128)S(1)} collective-permute-done((f32[104,256]{1,0:T(8,128)S(1)}, f32[104,256]{1,0:T(8,128)S(1)}, u32[]{:S(2)}, u32[]{:S(2)}) %collective-permute-start.5) | collective-permute-done | bytes 106528 | tf_op jit(solution)/shard_map/ppermute | solution.py:241
  27.3 0.0 copy-done
  27.3 8.7 %shard_map.68 = (f32[512,256]{1,0:T(8,128)}, f32[256,256]{1,0:T(8,128)}, f32[64,256]{1,0:T(8,128)}) custom-call(f32[104,256]{1,0:T(8,128)S(1)} %add.28.mine_ref, f32[104,256]{1,0:T(8,128)S(1)} %collective-permute-done.5.other_ref, f32[512,256]{1,0:T(8,128)S(1)} %copy-done, f32[512]{0:T(512)S(1)} %copy-done.1, s32[1]{0:T(128)S(6)} %copy.7.live_ref, ...), custom_call_target="tpu_custom_call" | custom-call | tf_op jit(solution)/shard_map/pallas_call | solution.py:225
  (5 shorter events, 0.1 us)
Async XLA Ops:
  1.3 0.7 %copy-start.1 = (f32[512]{0:T(512)S(1)}, f32[512]{0:T(512)}, u32[]{:S(2)}) copy-start(f32[512]{0:T(512)} %volumes_ref.1) | copy-start | bytes 6148
  4.4 1.5 %collective-permute-start = (f32[104,256]{1,0:T(8,128)S(1)}, f32[104,256]{1,0:T(8,128)S(1)}, u32[]{:S(2)}, u32[]{:S(2)}) collective-permute-start(f32[104,256]{1,0:T(8,128)S(1)} %get-tuple-element.6), channel_id=1, source_target_pairs={{0,1},{1,0},{2,3},{3,2},{4,5},{5,4},{6,7},{7,6},{8,9},{9,8},{10,11... | collective-permute-start | bytes 319496 | tf_op jit(solution)/shard_map/ppermute | solution.py:241
  5.9 5.1 %collective-permute-start.1 = (f32[104,256]{1,0:T(8,128)S(1)}, f32[104,256]{1,0:T(8,128)S(1)}, u32[]{:S(2)}, u32[]{:S(2)}) collective-permute-start(f32[104,256]{1,0:T(8,128)S(1)} %add.24), channel_id=1, source_target_pairs={{0,3},{1,8},{2,11},{3,0},{4,13},{5,6},{6,5},{7,14},{8,1},{9,10},{1... | collective-permute-start | bytes 319496 | tf_op jit(solution)/shard_map/ppermute | solution.py:241
  11.0 16.3 %copy-start = (f32[512,256]{1,0:T(8,128)S(1)}, f32[512,256]{1,0:T(8,128)}, u32[]{:S(2)}) copy-start(f32[512,256]{1,0:T(8,128)} %snapshots_ref.1) | copy-start | bytes 1572868
  11.0 4.3 %collective-permute-start.2 = (f32[104,256]{1,0:T(8,128)S(1)}, f32[104,256]{1,0:T(8,128)S(1)}, u32[]{:S(2)}, u32[]{:S(2)}) collective-permute-start(f32[104,256]{1,0:T(8,128)S(1)} %add.25), channel_id=1, source_target_pairs={{0,9},{1,2},{2,1},{3,10},{4,7},{5,12},{6,15},{7,4},{8,11},{9,0},{1... | collective-permute-start | bytes 319496 | tf_op jit(solution)/shard_map/ppermute | solution.py:241
  15.3 4.2 %collective-permute-start.3 = (f32[104,256]{1,0:T(8,128)S(1)}, f32[104,256]{1,0:T(8,128)S(1)}, u32[]{:S(2)}, u32[]{:S(2)}) collective-permute-start(f32[104,256]{1,0:T(8,128)S(1)} %add.26), channel_id=1, source_target_pairs={{0,5},{1,16},{2,19},{3,6},{4,21},{5,0},{6,3},{7,22},{8,25},{9,12},... | collective-permute-start | bytes 319496 | tf_op jit(solution)/shard_map/ppermute | solution.py:241
  19.5 5.5 %collective-permute-start.4 = (f32[104,256]{1,0:T(8,128)S(1)}, f32[104,256]{1,0:T(8,128)S(1)}, u32[]{:S(2)}, u32[]{:S(2)}) collective-permute-start(f32[104,256]{1,0:T(8,128)S(1)} %add.27), channel_id=1, source_target_pairs={{0,17},{1,4},{2,7},{3,18},{4,1},{5,20},{6,23},{7,2},{8,13},{9,24},... | collective-permute-start | bytes 319496 | tf_op jit(solution)/shard_map/ppermute | solution.py:241
  25.1 2.2 %collective-permute-start.5 = (f32[104,256]{1,0:T(8,128)S(1)}, f32[104,256]{1,0:T(8,128)S(1)}, u32[]{:S(2)}, u32[]{:S(2)}) collective-permute-start(f32[104,256]{1,0:T(8,128)S(1)} %add.28.mine_ref), channel_id=1, source_target_pairs={{0,1},{1,0},{2,3},{3,2},{4,5},{5,4},{6,7},{7,6},{8,9},{9,8},{10,11... | collective-permute-start | bytes 319496 | tf_op jit(solution)/shard_map/ppermute | solution.py:241

commit v6 on v5

--- a/solution.py
+++ b/solution.py
@@ -40,52 +40,44 @@
             total = jnp.where(sub_ids == r, parts[r], total)
         return total
 
-    upper_rows, lower_rows = [], []
-    columns = [lanes_of(tiles[0], c) for c in range(BLOCK)]
+    lower_rows = []
+    following = [lanes_of(tiles[0], c) for c in range(BLOCK)]
     for block in range(count):
         offset = block * BLOCK
         in_block = (lane_ids >= offset) & (lane_ids < offset + BLOCK)
-        own = tiles[block]
-        entry = {(r, c): row_of(columns[c], r) for c in range(BLOCK) for r in range(c + 1)}
-        kept = [row_of(own, r) for r in range(BLOCK)]
-        own = jnp.where(in_block, jnp.where(spread_ids == offset, 1.0, 0.0), own)
+        columns = following
+        own = jnp.where(in_block, jnp.where(spread_ids == offset, 1.0, 0.0), tiles[block])
         rows = [row_of(own, r) for r in range(BLOCK)]
         near = range(block + 1, min(block + 1 + AHEAD, count))
         weights = {k: [lanes_of(tiles[k], offset + c) for c in range(BLOCK)] for k in near}
         if block + 1 < count:
-            columns = [lanes_of(tiles[block + 1], offset + BLOCK + c) for c in range(BLOCK)]
+            following = [lanes_of(tiles[block + 1], offset + BLOCK + c) for c in range(BLOCK)]
         for k in near:
             tiles[k] = jnp.where(in_block, 0.0, tiles[k])
-        inverse, scaled = [], {}
+        pivots, inverse, scaled = [row_of(columns[0], 0)], [], {}
         for i in range(BLOCK):
-            inv = pl.reciprocal(entry[i, i], approx=True)
+            inv = pl.reciprocal(pivots[i], approx=True)
             inverse.append(inv)
+            beside = {c: row_of(columns[c], i) for c in range(i + 1, BLOCK)}
             if i + 1 < BLOCK:
-                square = entry[i, i + 1] * entry[i, i + 1]
-                entry[i + 1, i + 1] = entry[i + 1, i + 1] - square * inv
-            for r in range(i + 1, BLOCK):
-                scaled[r, i] = entry[i, r] * inv
-            for r in range(i + 1, BLOCK):
-                for c in range(r, BLOCK):
-                    if (r, c) != (i + 1, i + 1):
-                        entry[r, c] = entry[r, c] - scaled[r, i] * entry[i, c]
+                square = beside[i + 1] * beside[i + 1]
+                pivots.append(row_of(columns[i + 1], i + 1) - square * inv)
+            for c in range(i + 1, BLOCK):
+                scaled[c, i] = beside[c] * inv
+                columns[c] = columns[c] - columns[i] * scaled[c, i]
             for k in near:
                 here = weights[k][i]
                 weight = here * inv
                 if k == block + 1:
                     for c in range(BLOCK):
-                        columns[c] = columns[c] - weight * row_of(here, c)
+                        following[c] = following[c] - weight * row_of(here, c)
                 for c in range(i + 1, BLOCK):
                     weights[k][c] = weights[k][c] - here * scaled[c, i]
                 tiles[k] = tiles[k] - weight * rows[i]
             for r in range(i + 1, BLOCK):
                 rows[r] = rows[r] - scaled[r, i] * rows[i]
-                kept[r] = kept[r] - scaled[r, i] * kept[i]
-        root = gather([lax.rsqrt(entry[i, i]) for i in range(BLOCK)])
-        merged = gather(rows) * root
-        diagonal = gather(kept) * root
+        merged = gather(rows) * lax.rsqrt(gather(pivots))
         lower_rows.append(jnp.where(spread_ids <= offset, merged, 0.0))
-        upper_rows.append(jnp.where(spread_ids >= offset, jnp.where(in_block, diagonal, merged), 0.0))
         if block + 1 + AHEAD < count:
             solved = [None] * BLOCK
             for r in reversed(range(BLOCK)):
@@ -97,7 +89,7 @@
                 while len(terms) > 1:
                     terms = [terms[t] + terms[t + 1] for t in range(0, len(terms), 2)]
                 tiles[k] = jnp.where(in_block, 0.0, tiles[k]) - terms[0]
-    return jnp.concatenate(upper_rows, axis=0), jnp.concatenate(lower_rows, axis=0)
+    return jnp.concatenate(lower_rows, axis=0)
 
 
 def packed_rows(order, probes):
@@ -170,12 +162,34 @@
             pltpu.VMEM((size, order), F32),
             pltpu.SemaphoreType.DMA((3,)),
         ],
-        compiler_params=pltpu.CompilerParams(vmem_limit_bytes=54950 * 1024),
-    )(snapshots, volumes, live_rows, probes, part)
-
-
-def finish_kernel(mine_ref, other_ref, snapshots_ref, volumes_ref, live_ref, part_ref, basis_ref, factor_ref, coef_ref):
+        compiler_params=pltpu.CompilerParams(vmem_limit_bytes=24 * 1024 * 1024),
+    )(*(pltpu.with_memory_space_constraint(x, pltpu.HBM) for x in (snapshots, volumes)), live_rows, pltpu.with_memory_space_constraint(probes, pltpu.HBM), part)
+
+
+def weigh_kernel(snapshots_ref, volumes_ref, live_ref, weighted_ref):
     row_count, order = snapshots_ref.shape
+    for begin in range(0, row_count, LANES):
+        scale = jnp.sqrt(live_volumes(volumes_ref, live_ref, begin))
+        scale = jnp.broadcast_to(scale, (LANES, LANES)).T
+        rows = pl.ds(begin, LANES)
+        weighted_ref[rows, :] = snapshots_ref[rows, :] * jnp.concatenate([scale] * (order // LANES), axis=1)
+
+
+def weigh(snapshots, volumes, live_rows):
+    whole = pl.BlockSpec(memory_space=pltpu.VMEM)
+    scalar = pl.BlockSpec(memory_space=pltpu.SMEM)
+    return pl.pallas_call(
+        weigh_kernel,
+        out_shape=jax.ShapeDtypeStruct(snapshots.shape, F32),
+        in_specs=[whole, whole, scalar],
+        out_specs=whole,
+        compiler_params=pltpu.CompilerParams(vmem_limit_bytes=24 * 1024 * 1024),
+        cost_estimate=pl.CostEstimate(flops=snapshots.size, bytes_accessed=8 * snapshots.size, transcendentals=0),
+    )(snapshots, volumes, live_rows)
+
+
+def finish_kernel(mine_ref, other_ref, weighted_ref, part_ref, basis_ref, factor_ref, coef_ref):
+    order = weighted_ref.shape[1]
     probes = coef_ref.shape[0]
     half = order // 2
     low = part_ref[0] == 0
@@ -183,45 +197,37 @@
     packed = jnp.concatenate([jnp.where(low, mine, other), jnp.where(low, other, mine)], axis=0)
     row_ids = lax.broadcasted_iota(jnp.int32, (half, half), 0)
     column_ids = lax.broadcasted_iota(jnp.int32, (half, half), 1)
+    in_upper = row_ids <= column_ids
     square = packed[:half, :half]
     turned = square.T
     cross = packed[half : half + probes, :]
     diagonal = packed[half + probes : half + probes + 1, :half]
 
-    upper, inverse = eliminate(jnp.where(row_ids <= column_ids, square, turned))
-    factor_ref[:half, :half] = upper
-    factor_ref[half:, :half] = jnp.zeros((half, half), F32)
+    first = jnp.where(in_upper, square, turned)
+    inverse = eliminate(first)
     beside = product(inverse, packed[:half, half:], ((1,), (0,)))
-    factor_ref[:half, half:] = beside
     second = jnp.where(row_ids > column_ids, square, turned)
     second = jnp.where(row_ids == column_ids, diagonal, second) - product(beside, beside, ((0,), (0,)))
-
-    def first_columns(block):
-        left = product(block[:, :half], inverse, ((1,), (1,)))
-        return left, block[:, half:] - product(left, beside, ((1,), (0,)))
-
-    left, cross_rest = first_columns(cross)
+    factor_ref[:half, :half] = jnp.where(in_upper, product(inverse, first, ((1,), (0,))), 0.0)
+    factor_ref[:half, half:] = beside
+    factor_ref[half:, :half] = jnp.zeros((half, half), F32)
+
+    left = product(cross[:, :half], inverse, ((1,), (1,)))
     coef_ref[:, :half] = left
-    rest = []
-    for begin in range(0, row_count, LANES):
-        scale = jnp.sqrt(live_volumes(volumes_ref, live_ref, begin))
-        scale = jnp.broadcast_to(scale, (LANES, LANES)).T
-        weighted = snapshots_ref[begin : begin + LANES, :] * jnp.concatenate([scale] * (order // LANES), axis=1)
-        left, right = first_columns(weighted)
-        basis_ref[begin : begin + LANES, :half] = left
-        rest.append(right)
-
-    upper, inverse_second = eliminate(second)
-    factor_ref[half:, half:] = upper
+    cross_rest = cross[:, half:] - product(left, beside, ((1,), (0,)))
+    left = product(weighted_ref[:, :half], inverse, ((1,), (1,)))
+    basis_ref[:, :half] = left
+    rest = weighted_ref[:, half:] - product(left, beside, ((1,), (0,)))
+
+    inverse_second = eliminate(second)
     coef_ref[:, half:] = product(cross_rest, inverse_second, ((1,), (1,)))
-    for begin in range(0, row_count, LANES):
-        basis_ref[begin : begin + LANES, half:] = product(rest[begin // LANES], inverse_second, ((1,), (1,)))
-
-
-def finish(mine, other, snapshots, volumes, live_rows, part, probes):
-    row_count, order = snapshots.shape
+    basis_ref[:, half:] = product(rest, inverse_second, ((1,), (1,)))
+    factor_ref[half:, half:] = jnp.where(in_upper, product(inverse_second, second, ((1,), (0,))), 0.0)
+
+
+def finish(mine, other, weighted, part, probes):
+    row_count, order = weighted.shape
     whole = pl.BlockSpec(memory_space=pltpu.VMEM)
-    scalar = pl.BlockSpec(memory_space=pltpu.SMEM)
     return pl.pallas_call(
         finish_kernel,
         out_shape=(
@@ -229,10 +235,10 @@
             jax.ShapeDtypeStruct((order, order), F32),
             jax.ShapeDtypeStruct((probes, order), F32),
         ),
-        in_specs=[whole] * 4 + [scalar] * 2,
+        in_specs=[whole] * 3 + [pl.BlockSpec(memory_space=pltpu.SMEM)],
         out_specs=(whole,) * 3,
         compiler_params=pltpu.CompilerParams(vmem_limit_bytes=32 * 1024 * 1024),
-    )(mine, other, snapshots, volumes, live_rows, part)
+    )(mine, other, weighted, part)
 
 
 def exchange(value, bits):
@@ -260,7 +266,7 @@
     part = (lax.population_count(index.astype(jnp.int32)) % 2).reshape(1)
     keep, send = local_sums(snapshots.shape[0] * count, snapshots, volumes, live_rows, probes, part)
     mine, other = reduce_halves(keep, send)
-    return finish(mine, other, snapshots, volumes, live_rows, part, probes.shape[0])
+    return finish(mine, other, weigh(snapshots, volumes, live_rows), part, probes.shape[0])
 
 
 def solution(mesh):

time: 36.1 us -> 34.5 us (0.956)
  Pallas kernels: 11.1 us -> 10.3 us
  local copies, waits for them, and re-layouts: 0.68 us -> 0.01 us
    pallas_call x1, Pallas kernels: 8.67 us -> 7.67 us  [finish(): pl.pallas_call(finish_kernel, out_shape=(jax.ShapeDtypeStruct((row_count,...]
    unnamed x4, local copies, waits for them, and re-layouts: 0.68 us -> 0.01 us
where the time goes in v6:
time: 34.5 us; the launch traced here: 34.3 us
  waiting for transfers between devices  11.4 us (33%)
  starting transfers between devices  11.2 us (32%)
  Pallas kernels  10.3 us (30%)
  between operations  1.34 us (4%)
    ppermute x6, waiting for transfers between devices, exchange(): return lax.ppermute(value, ('cells', 'sub'), pairs)  11.4 us
    ppermute x6, starting transfers between devices, exchange(): return lax.ppermute(value, ('cells', 'sub'), pairs)  11.2 us
    pallas_call x1, Pallas kernels, finish(): pl.pallas_call(finish_kernel, out_shape=(jax.ShapeDtypeStruct((row_count,...  7.67 us
    pallas_call x1, Pallas kernels, local_sums(): pl.pallas_call(functools.partial(sums_kernel, total_rows), out_shape=(jax...  2.48 us
  transfers between devices with their start and end apart: 6, of which 6 were waited for; matrix products, arithmetic and copies ran while one was open for 0% of the time, Pallas kernels for 0%

profile of v6, /device:TPU:0, one launch (start us, length us, event | category | flops | bytes accessed | tf_op | source)
XLA Modules:
  0.0 34.3 jit_solution(2996471638449842381)
XLA Ops:
  1.3 2.5 %shard_map.67 = (f32[104,256]{1,0:T(8,128)S(1)}, f32[104,256]{1,0:T(8,128)S(1)}) custom-call(f32[512,256]{1,0:T(8,128)} %snapshots_ref.1, f32[512]{0:T(512)} %volumes_ref.1, s32[1]{0:T(128)S(6)} %copy.7.live_ref, f32[64,512]{1,0:T(8,128)} %probes_hbm.1, s32[1]{0:T(128)} %bitcast.part_ref), custom_call_target="tpu_custom_call" | custom-call | tf_op jit(solution)/shard_map/pallas_call | solution.py:153
  3.8 0.5 %collective-permute-start = (f32[104,256]{1,0:T(8,128)S(1)}, f32[104,256]{1,0:T(8,128)S(1)}, u32[]{:S(2)}, u32[]{:S(2)}) collective-permute-start(f32[104,256]{1,0:T(8,128)S(1)} %get-tuple-element.6), channel_id=1, source_target_pairs={{0,1},{1,0},{2,3},{3,2},{4,5},{5,4},{6,7},{7,6},{8,9},{9,8},{10,11... | collective-permute-start | bytes 319496 | tf_op jit(solution)/shard_map/ppermute | solution.py:247
  4.3 1.0 %collective-permute-done = f32[104,256]{1,0:T(8,128)S(1)} collective-permute-done((f32[104,256]{1,0:T(8,128)S(1)}, f32[104,256]{1,0:T(8,128)S(1)}, u32[]{:S(2)}, u32[]{:S(2)}) %collective-permute-start) | collective-permute-done | bytes 106528 | tf_op jit(solution)/shard_map/ppermute | solution.py:247
  5.3 2.7 %collective-permute-start.1 = (f32[104,256]{1,0:T(8,128)S(1)}, f32[104,256]{1,0:T(8,128)S(1)}, u32[]{:S(2)}, u32[]{:S(2)}) collective-permute-start(f32[104,256]{1,0:T(8,128)S(1)} %add.24), channel_id=1, source_target_pairs={{0,3},{1,8},{2,11},{3,0},{4,13},{5,6},{6,5},{7,14},{8,1},{9,10},{1... | collective-permute-start | bytes 319496 | tf_op jit(solution)/shard_map/ppermute | solution.py:247
  7.9 2.4 %collective-permute-done.1 = f32[104,256]{1,0:T(8,128)S(1)} collective-permute-done((f32[104,256]{1,0:T(8,128)S(1)}, f32[104,256]{1,0:T(8,128)S(1)}, u32[]{:S(2)}, u32[]{:S(2)}) %collective-permute-start.1) | collective-permute-done | bytes 106528 | tf_op jit(solution)/shard_map/ppermute | solution.py:247
  10.4 0.0 copy-start
  10.4 1.9 %collective-permute-start.2 = (f32[104,256]{1,0:T(8,128)S(1)}, f32[104,256]{1,0:T(8,128)S(1)}, u32[]{:S(2)}, u32[]{:S(2)}) collective-permute-start(f32[104,256]{1,0:T(8,128)S(1)} %add.25), channel_id=1, source_target_pairs={{0,9},{1,2},{2,1},{3,10},{4,7},{5,12},{6,15},{7,4},{8,11},{9,0},{1... | collective-permute-start | bytes 319496 | tf_op jit(solution)/shard_map/ppermute | solution.py:247
  12.3 2.4 %collective-permute-done.2 = f32[104,256]{1,0:T(8,128)S(1)} collective-permute-done((f32[104,256]{1,0:T(8,128)S(1)}, f32[104,256]{1,0:T(8,128)S(1)}, u32[]{:S(2)}, u32[]{:S(2)}) %collective-permute-start.2) | collective-permute-done | bytes 106528 | tf_op jit(solution)/shard_map/ppermute | solution.py:247
  14.7 1.7 %collective-permute-start.3 = (f32[104,256]{1,0:T(8,128)S(1)}, f32[104,256]{1,0:T(8,128)S(1)}, u32[]{:S(2)}, u32[]{:S(2)}) collective-permute-start(f32[104,256]{1,0:T(8,128)S(1)} %add.26), channel_id=1, source_target_pairs={{0,5},{1,16},{2,19},{3,6},{4,21},{5,0},{6,3},{7,22},{8,25},{9,12},... | collective-permute-start | bytes 319496 | tf_op jit(solution)/shard_map/ppermute | solution.py:247
  16.4 2.4 %collective-permute-done.3 = f32[104,256]{1,0:T(8,128)S(1)} collective-permute-done((f32[104,256]{1,0:T(8,128)S(1)}, f32[104,256]{1,0:T(8,128)S(1)}, u32[]{:S(2)}, u32[]{:S(2)}) %collective-permute-start.3) | collective-permute-done | bytes 106528 | tf_op jit(solution)/shard_map/ppermute | solution.py:247
  18.9 0.0 copy-start.1
  18.9 3.1 %collective-permute-start.4 = (f32[104,256]{1,0:T(8,128)S(1)}, f32[104,256]{1,0:T(8,128)S(1)}, u32[]{:S(2)}, u32[]{:S(2)}) collective-permute-start(f32[104,256]{1,0:T(8,128)S(1)} %add.27), channel_id=1, source_target_pairs={{0,17},{1,4},{2,7},{3,18},{4,1},{5,20},{6,23},{7,2},{8,13},{9,24},... | collective-permute-start | bytes 319496 | tf_op jit(solution)/shard_map/ppermute | solution.py:247
  22.0 2.4 %collective-permute-done.4 = f32[104,256]{1,0:T(8,128)S(1)} collective-permute-done((f32[104,256]{1,0:T(8,128)S(1)}, f32[104,256]{1,0:T(8,128)S(1)}, u32[]{:S(2)}, u32[]{:S(2)}) %collective-permute-start.4) | collective-permute-done | bytes 106528 | tf_op jit(solution)/shard_map/ppermute | solution.py:247
  24.4 1.3 %collective-permute-start.5 = (f32[104,256]{1,0:T(8,128)S(1)}, f32[104,256]{1,0:T(8,128)S(1)}, u32[]{:S(2)}, u32[]{:S(2)}) collective-permute-start(f32[104,256]{1,0:T(8,128)S(1)} %add.28.mine_ref), channel_id=1, source_target_pairs={{0,1},{1,0},{2,3},{3,2},{4,5},{5,4},{6,7},{7,6},{8,9},{9,8},{10,11... | collective-permute-start | bytes 319496 | tf_op jit(solution)/shard_map/ppermute | solution.py:247
  25.7 0.0 copy-done
  25.7 0.0 copy-done.1
  25.7 0.1 shard_map.68.weighted_ref
  25.8 0.8 %collective-permute-done.5.other_ref = f32[104,256]{1,0:T(8,128)S(1)} collective-permute-done((f32[104,256]{1,0:T(8,128)S(1)}, f32[104,256]{1,0:T(8,128)S(1)}, u32[]{:S(2)}, u32[]{:S(2)}) %collective-permute-start.5) | collective-permute-done | bytes 106528 | tf_op jit(solution)/shard_map/ppermute | solution.py:247
  26.6 7.7 %shard_map.69 = (f32[512,256]{1,0:T(8,128)}, f32[256,256]{1,0:T(8,128)}, f32[64,256]{1,0:T(8,128)}) custom-call(f32[104,256]{1,0:T(8,128)S(1)} %add.28.mine_ref, f32[104,256]{1,0:T(8,128)S(1)} %collective-permute-done.5.other_ref, f32[512,256]{1,0:T(8,128)S(1)} %shard_map.68.weighted_ref, s32[1]{0:T(128)} %bitcast.part_ref), custom_call_target="tpu_custom_call" | custom-call | tf_op jit(solution)/shard_map/pallas_call | solution.py:231
  (5 shorter events, 0.1 us)
Async XLA Ops:
  3.8 1.5 %collective-permute-start = (f32[104,256]{1,0:T(8,128)S(1)}, f32[104,256]{1,0:T(8,128)S(1)}, u32[]{:S(2)}, u32[]{:S(2)}) collective-permute-start(f32[104,256]{1,0:T(8,128)S(1)} %get-tuple-element.6), channel_id=1, source_target_pairs={{0,1},{1,0},{2,3},{3,2},{4,5},{5,4},{6,7},{7,6},{8,9},{9,8},{10,11... | collective-permute-start | bytes 319496 | tf_op jit(solution)/shard_map/ppermute | solution.py:247
  5.3 5.1 %collective-permute-start.1 = (f32[104,256]{1,0:T(8,128)S(1)}, f32[104,256]{1,0:T(8,128)S(1)}, u32[]{:S(2)}, u32[]{:S(2)}) collective-permute-start(f32[104,256]{1,0:T(8,128)S(1)} %add.24), channel_id=1, source_target_pairs={{0,3},{1,8},{2,11},{3,0},{4,13},{5,6},{6,5},{7,14},{8,1},{9,10},{1... | collective-permute-start | bytes 319496 | tf_op jit(solution)/shard_map/ppermute | solution.py:247
  10.4 15.3 %copy-start = (f32[512,256]{1,0:T(8,128)S(1)}, f32[512,256]{1,0:T(8,128)}, u32[]{:S(2)}) copy-start(f32[512,256]{1,0:T(8,128)} %snapshots_ref.1) | copy-start | bytes 1572868
  10.4 4.3 %collective-permute-start.2 = (f32[104,256]{1,0:T(8,128)S(1)}, f32[104,256]{1,0:T(8,128)S(1)}, u32[]{:S(2)}, u32[]{:S(2)}) collective-permute-start(f32[104,256]{1,0:T(8,128)S(1)} %add.25), channel_id=1, source_target_pairs={{0,9},{1,2},{2,1},{3,10},{4,7},{5,12},{6,15},{7,4},{8,11},{9,0},{1... | collective-permute-start | bytes 319496 | tf_op jit(solution)/shard_map/ppermute | solution.py:247
  14.7 4.2 %collective-permute-start.3 = (f32[104,256]{1,0:T(8,128)S(1)}, f32[104,256]{1,0:T(8,128)S(1)}, u32[]{:S(2)}, u32[]{:S(2)}) collective-permute-start(f32[104,256]{1,0:T(8,128)S(1)} %add.26), channel_id=1, source_target_pairs={{0,5},{1,16},{2,19},{3,6},{4,21},{5,0},{6,3},{7,22},{8,25},{9,12},... | collective-permute-start | bytes 319496 | tf_op jit(solution)/shard_map/ppermute | solution.py:247
  18.9 6.8 %copy-start.1 = (f32[512]{0:T(512)S(1)}, f32[512]{0:T(512)}, u32[]{:S(2)}) copy-start(f32[512]{0:T(512)} %volumes_ref.1) | copy-start | bytes 6148
  18.9 5.5 %collective-permute-start.4 = (f32[104,256]{1,0:T(8,128)S(1)}, f32[104,256]{1,0:T(8,128)S(1)}, u32[]{:S(2)}, u32[]{:S(2)}) collective-permute-start(f32[104,256]{1,0:T(8,128)S(1)} %add.27), channel_id=1, source_target_pairs={{0,17},{1,4},{2,7},{3,18},{4,1},{5,20},{6,23},{7,2},{8,13},{9,24},... | collective-permute-start | bytes 319496 | tf_op jit(solution)/shard_map/ppermute | solution.py:247
  24.4 2.2 %collective-permute-start.5 = (f32[104,256]{1,0:T(8,128)S(1)}, f32[104,256]{1,0:T(8,128)S(1)}, u32[]{:S(2)}, u32[]{:S(2)}) collective-permute-start(f32[104,256]{1,0:T(8,128)S(1)} %add.28.mine_ref), channel_id=1, source_target_pairs={{0,1},{1,0},{2,3},{3,2},{4,5},{5,4},{6,7},{7,6},{8,9},{9,8},{10,11... | collective-permute-start | bytes 319496 | tf_op jit(solution)/shard_map/ppermute | solution.py:247

commit v7 on v6

--- a/solution.py
+++ b/solution.py
@@ -241,23 +241,26 @@
     )(mine, other, weighted, part)
 
 
-def exchange(value, bits):
+def exchange(value, masks):
     count = lax.axis_size("cells") * lax.axis_size("sub")
-    pairs = [(i, i ^ 1 ^ bits[bin(i).count("1") % 2]) for i in range(count)]
+    pairs = [(i, i ^ masks[bin(i).count("1") % 2]) for i in range(count)]
     return lax.ppermute(value, ("cells", "sub"), pairs)
 
 
 def reduce_halves(keep, send):
     count = lax.axis_size("cells") * lax.axis_size("sub")
     bits = [1 << k for k in range(1, count.bit_length() - 1)]
-    split = len(bits) // 2
-    mine = keep + exchange(send, (0, 0))
-    for first, second in zip(bits[:split], bits[split : 2 * split]):
-        mine = mine + exchange(mine, (first, second))
-        mine = mine + exchange(mine, (second, first))
-    for bit in bits[2 * split :]:
-        mine = mine + exchange(mine, (bit, bit))
-    return mine, exchange(mine, (0, 0))
+    phases = [bits[k : k + 2] for k in range(0, len(bits) - 1, 2)]
+    split = len(phases) // 2
+    mine = keep + exchange(send, (1, 1))
+    for even, odd in zip(phases, phases[split:] + phases[:split]):
+        near = exchange(mine, (even[0] ^ 1, odd[0] ^ 1))
+        far = exchange(mine, (even[1] ^ 1, odd[1] ^ 1))
+        across = exchange(mine, (even[0] ^ even[1], odd[0] ^ odd[1]))
+        mine = (mine + near) + (far + across)
+    for bit in bits[2 * len(phases) :]:
+        mine = mine + exchange(mine, (bit ^ 1, bit ^ 1))
+    return mine, exchange(mine, (1, 1))
 
 
 def per_device(snapshots, volumes, live_rows, probes):

time: 34.5 us -> 32.2 us (0.933)
  starting transfers between devices: 11.2 us -> 9.11 us
    ppermute x6 -> x8, starting transfers between devices: 11.2 us -> 9.11 us  [exchange(): return lax.ppermute(value, ('cells', 'sub'), pairs)]
    ppermute x6 -> x8, waiting for transfers between devices: 11.4 us -> 11.2 us  [exchange(): return lax.ppermute(value, ('cells', 'sub'), pairs)]
  transfers between devices with their start and end apart: 6 -> 8, of which waited for: 6 -> 6; matrix products, arithmetic and copies ran while one was open for 0% -> 0% of each run, Pallas kernels for 0% -> 0%
where the time goes in v7:
time: 32.2 us; the launch traced here: 32 us
  waiting for transfers between devices  11.2 us (35%)
  Pallas kernels  10.3 us (32%)
  starting transfers between devices  9.11 us (28%)
  between operations  1.34 us (4%)
    ppermute x8, waiting for transfers between devices, exchange(): return lax.ppermute(value, ('cells', 'sub'), pairs)  11.2 us
    ppermute x8, starting transfers between devices, exchange(): return lax.ppermute(value, ('cells', 'sub'), pairs)  9.11 us
    pallas_call x1, Pallas kernels, finish(): pl.pallas_call(finish_kernel, out_shape=(jax.ShapeDtypeStruct((row_count,...  7.67 us
    pallas_call x1, Pallas kernels, local_sums(): pl.pallas_call(functools.partial(sums_kernel, total_rows), out_shape=(jax...  2.48 us
  transfers between devices with their start and end apart: 8, of which 6 were waited for; matrix products, arithmetic and copies ran while one was open for 0% of the time, Pallas kernels for 0%

profile of v7, /device:TPU:0, one launch (start us, length us, event | category | flops | bytes accessed | tf_op | source)
XLA Modules:
  0.0 32.0 jit_solution(1421907374282960826)
XLA Ops:
  1.3 2.5 %shard_map.67 = (f32[104,256]{1,0:T(8,128)S(1)}, f32[104,256]{1,0:T(8,128)S(1)}) custom-call(f32[512,256]{1,0:T(8,128)} %snapshots_ref.1, f32[512]{0:T(512)} %volumes_ref.1, s32[1]{0:T(128)S(6)} %copy.7.live_ref, f32[64,512]{1,0:T(8,128)} %probes_hbm.1, s32[1]{0:T(128)} %bitcast.part_ref), custom_call_target="tpu_custom_call" | custom-call | tf_op jit(solution)/shard_map/pallas_call | solution.py:153
  3.8 0.5 %collective-permute-start = (f32[104,256]{1,0:T(8,128)S(1)}, f32[104,256]{1,0:T(8,128)S(1)}, u32[]{:S(2)}, u32[]{:S(2)}) collective-permute-start(f32[104,256]{1,0:T(8,128)S(1)} %get-tuple-element.6), channel_id=1, source_target_pairs={{0,1},{1,0},{2,3},{3,2},{4,5},{5,4},{6,7},{7,6},{8,9},{9,8},{10,11... | collective-permute-start | bytes 319496 | tf_op jit(solution)/shard_map/ppermute | solution.py:247
  4.3 1.0 %collective-permute-done = f32[104,256]{1,0:T(8,128)S(1)} collective-permute-done((f32[104,256]{1,0:T(8,128)S(1)}, f32[104,256]{1,0:T(8,128)S(1)}, u32[]{:S(2)}, u32[]{:S(2)}) %collective-permute-start) | collective-permute-done | bytes 106528 | tf_op jit(solution)/shard_map/ppermute | solution.py:247
  5.3 0.0 copy-start
  5.3 3.9 %collective-permute-start.3 = (f32[104,256]{1,0:T(8,128)S(1)}, f32[104,256]{1,0:T(8,128)S(1)}, u32[]{:S(2)}, u32[]{:S(2)}) collective-permute-start(f32[104,256]{1,0:T(8,128)S(1)} %add.30), channel_id=1, source_target_pairs={{0,6},{1,25},{2,26},{3,5},{4,28},{5,3},{6,0},{7,31},{8,16},{9,15},... | collective-permute-start | bytes 319496 | tf_op jit(solution)/shard_map/ppermute | solution.py:247
  9.2 0.0 collective-permute-start.2
  9.2 0.4 %collective-permute-start.1 = (f32[104,256]{1,0:T(8,128)S(1)}, f32[104,256]{1,0:T(8,128)S(1)}, u32[]{:S(2)}, u32[]{:S(2)}) collective-permute-start(f32[104,256]{1,0:T(8,128)S(1)} %add.30), channel_id=1, source_target_pairs={{0,3},{1,8},{2,11},{3,0},{4,13},{5,6},{6,5},{7,14},{8,1},{9,10},{1... | collective-permute-start | bytes 319496 | tf_op jit(solution)/shard_map/ppermute | solution.py:247
  9.5 2.3 %collective-permute-done.3 = f32[104,256]{1,0:T(8,128)S(1)} collective-permute-done((f32[104,256]{1,0:T(8,128)S(1)}, f32[104,256]{1,0:T(8,128)S(1)}, u32[]{:S(2)}, u32[]{:S(2)}) %collective-permute-start.3) | collective-permute-done | bytes 106528 | tf_op jit(solution)/shard_map/ppermute | solution.py:247
  11.8 1.4 %collective-permute-done.2 = f32[104,256]{1,0:T(8,128)S(1)} collective-permute-done((f32[104,256]{1,0:T(8,128)S(1)}, f32[104,256]{1,0:T(8,128)S(1)}, u32[]{:S(2)}, u32[]{:S(2)}) %collective-permute-start.2) | collective-permute-done | bytes 106528 | tf_op jit(solution)/shard_map/ppermute | solution.py:247
  13.3 0.0 collective-permute-done.1
  13.3 0.0 copy-start.1
  13.3 3.8 %collective-permute-start.6 = (f32[104,256]{1,0:T(8,128)S(1)}, f32[104,256]{1,0:T(8,128)S(1)}, u32[]{:S(2)}, u32[]{:S(2)}) collective-permute-start(f32[104,256]{1,0:T(8,128)S(1)} %add_add_fusion.1), channel_id=1, source_target_pairs={{0,24},{1,7},{2,4},{3,27},{4,2},{5,29},{6,30},{7,1},{8,14},{9,17},... | collective-permute-start | bytes 319496 | tf_op jit(solution)/shard_map/ppermute | solution.py:247
  17.2 0.0 collective-permute-start.5
  17.2 0.4 %collective-permute-start.4 = (f32[104,256]{1,0:T(8,128)S(1)}, f32[104,256]{1,0:T(8,128)S(1)}, u32[]{:S(2)}, u32[]{:S(2)}) collective-permute-start(f32[104,256]{1,0:T(8,128)S(1)} %add_add_fusion.1), channel_id=1, source_target_pairs={{0,9},{1,2},{2,1},{3,10},{4,7},{5,12},{6,15},{7,4},{8,11},{9,0},{1... | collective-permute-start | bytes 319496 | tf_op jit(solution)/shard_map/ppermute | solution.py:247
  17.5 2.5 %collective-permute-done.6 = f32[104,256]{1,0:T(8,128)S(1)} collective-permute-done((f32[104,256]{1,0:T(8,128)S(1)}, f32[104,256]{1,0:T(8,128)S(1)}, u32[]{:S(2)}, u32[]{:S(2)}) %collective-permute-start.6) | collective-permute-done | bytes 106528 | tf_op jit(solution)/shard_map/ppermute | solution.py:247
  20.0 3.0 %collective-permute-done.5 = f32[104,256]{1,0:T(8,128)S(1)} collective-permute-done((f32[104,256]{1,0:T(8,128)S(1)}, f32[104,256]{1,0:T(8,128)S(1)}, u32[]{:S(2)}, u32[]{:S(2)}) %collective-permute-start.5) | collective-permute-done | bytes 106528 | tf_op jit(solution)/shard_map/ppermute | solution.py:247
  23.0 0.0 collective-permute-done.4
  23.0 0.2 collective-permute-start.7
  23.2 0.0 copy-done
  23.2 0.0 copy-done.1
  23.2 0.1 shard_map.68.weighted_ref
  23.3 1.0 %collective-permute-done.7.other_ref = f32[104,256]{1,0:T(8,128)S(1)} collective-permute-done((f32[104,256]{1,0:T(8,128)S(1)}, f32[104,256]{1,0:T(8,128)S(1)}, u32[]{:S(2)}, u32[]{:S(2)}) %collective-permute-start.7) | collective-permute-done | bytes 106528 | tf_op jit(solution)/shard_map/ppermute | solution.py:247
  24.4 7.7 %shard_map.69 = (f32[512,256]{1,0:T(8,128)}, f32[256,256]{1,0:T(8,128)}, f32[64,256]{1,0:T(8,128)}) custom-call(f32[104,256]{1,0:T(8,128)S(1)} %add_add_fusion.mine_ref, f32[104,256]{1,0:T(8,128)S(1)} %collective-permute-done.7.other_ref, f32[512,256]{1,0:T(8,128)S(1)} %shard_map.68.weighted_ref, s32[1]{0:T(128)} %bitcast.part_ref), custom_call_target="tpu_custom_call" | custom-call | tf_op jit(solution)/shard_map/pallas_call | solution.py:231
  (3 shorter events, 0.1 us)
Async XLA Ops:
  3.8 1.5 %collective-permute-start = (f32[104,256]{1,0:T(8,128)S(1)}, f32[104,256]{1,0:T(8,128)S(1)}, u32[]{:S(2)}, u32[]{:S(2)}) collective-permute-start(f32[104,256]{1,0:T(8,128)S(1)} %get-tuple-element.6), channel_id=1, source_target_pairs={{0,1},{1,0},{2,3},{3,2},{4,5},{5,4},{6,7},{7,6},{8,9},{9,8},{10,11... | collective-permute-start | bytes 319496 | tf_op jit(solution)/shard_map/ppermute | solution.py:247
  5.3 17.9 %copy-start = (f32[512,256]{1,0:T(8,128)S(1)}, f32[512,256]{1,0:T(8,128)}, u32[]{:S(2)}) copy-start(f32[512,256]{1,0:T(8,128)} %snapshots_ref.1) | copy-start | bytes 1572868
  5.3 6.5 %collective-permute-start.3 = (f32[104,256]{1,0:T(8,128)S(1)}, f32[104,256]{1,0:T(8,128)S(1)}, u32[]{:S(2)}, u32[]{:S(2)}) collective-permute-start(f32[104,256]{1,0:T(8,128)S(1)} %add.30), channel_id=1, source_target_pairs={{0,6},{1,25},{2,26},{3,5},{4,28},{5,3},{6,0},{7,31},{8,16},{9,15},... | collective-permute-start | bytes 319496 | tf_op jit(solution)/shard_map/ppermute | solution.py:247
  9.2 4.1 %collective-permute-start.2 = (f32[104,256]{1,0:T(8,128)S(1)}, f32[104,256]{1,0:T(8,128)S(1)}, u32[]{:S(2)}, u32[]{:S(2)}) collective-permute-start(f32[104,256]{1,0:T(8,128)S(1)} %add.30), channel_id=1, source_target_pairs={{0,5},{1,16},{2,19},{3,6},{4,21},{5,0},{6,3},{7,22},{8,25},{9,12},... | collective-permute-start | bytes 319496 | tf_op jit(solution)/shard_map/ppermute | solution.py:247
  9.2 4.1 %collective-permute-start.1 = (f32[104,256]{1,0:T(8,128)S(1)}, f32[104,256]{1,0:T(8,128)S(1)}, u32[]{:S(2)}, u32[]{:S(2)}) collective-permute-start(f32[104,256]{1,0:T(8,128)S(1)} %add.30), channel_id=1, source_target_pairs={{0,3},{1,8},{2,11},{3,0},{4,13},{5,6},{6,5},{7,14},{8,1},{9,10},{1... | collective-permute-start | bytes 319496 | tf_op jit(solution)/shard_map/ppermute | solution.py:247
  13.3 9.9 %copy-start.1 = (f32[512]{0:T(512)S(1)}, f32[512]{0:T(512)}, u32[]{:S(2)}) copy-start(f32[512]{0:T(512)} %volumes_ref.1) | copy-start | bytes 6148
  13.3 6.7 %collective-permute-start.6 = (f32[104,256]{1,0:T(8,128)S(1)}, f32[104,256]{1,0:T(8,128)S(1)}, u32[]{:S(2)}, u32[]{:S(2)}) collective-permute-start(f32[104,256]{1,0:T(8,128)S(1)} %add_add_fusion.1), channel_id=1, source_target_pairs={{0,24},{1,7},{2,4},{3,27},{4,2},{5,29},{6,30},{7,1},{8,14},{9,17},... | collective-permute-start | bytes 319496 | tf_op jit(solution)/shard_map/ppermute | solution.py:247
  17.2 5.8 %collective-permute-start.5 = (f32[104,256]{1,0:T(8,128)S(1)}, f32[104,256]{1,0:T(8,128)S(1)}, u32[]{:S(2)}, u32[]{:S(2)}) collective-permute-start(f32[104,256]{1,0:T(8,128)S(1)} %add_add_fusion.1), channel_id=1, source_target_pairs={{0,17},{1,4},{2,7},{3,18},{4,1},{5,20},{6,23},{7,2},{8,13},{9,24},... | collective-permute-start | bytes 319496 | tf_op jit(solution)/shard_map/ppermute | solution.py:247
  17.2 5.8 %collective-permute-start.4 = (f32[104,256]{1,0:T(8,128)S(1)}, f32[104,256]{1,0:T(8,128)S(1)}, u32[]{:S(2)}, u32[]{:S(2)}) collective-permute-start(f32[104,256]{1,0:T(8,128)S(1)} %add_add_fusion.1), channel_id=1, source_target_pairs={{0,9},{1,2},{2,1},{3,10},{4,7},{5,12},{6,15},{7,4},{8,11},{9,0},{1... | collective-permute-start | bytes 319496 | tf_op jit(solution)/shard_map/ppermute | solution.py:247
  23.0 1.4 %collective-permute-start.7 = (f32[104,256]{1,0:T(8,128)S(1)}, f32[104,256]{1,0:T(8,128)S(1)}, u32[]{:S(2)}, u32[]{:S(2)}) collective-permute-start(f32[104,256]{1,0:T(8,128)S(1)} %add_add_fusion.mine_ref), channel_id=1, source_target_pairs={{0,1},{1,0},{2,3},{3,2},{4,5},{5,4},{6,7},{7,6},{8,9},{9,8},{10,11... | collective-permute-start | bytes 319496 | tf_op jit(solution)/shard_map/ppermute | solution.py:247

commit v8 on v7

--- a/solution.py
+++ b/solution.py
@@ -46,7 +46,8 @@
         offset = block * BLOCK
         in_block = (lane_ids >= offset) & (lane_ids < offset + BLOCK)
         columns = following
-        own = jnp.where(in_block, jnp.where(spread_ids == offset, 1.0, 0.0), tiles[block])
+        before = tiles[block]
+        own = jnp.where(in_block, jnp.where(spread_ids == offset, 1.0, 0.0), before)
         rows = [row_of(own, r) for r in range(BLOCK)]
         near = range(block + 1, min(block + 1 + AHEAD, count))
         weights = {k: [lanes_of(tiles[k], offset + c) for c in range(BLOCK)] for k in near}
@@ -84,11 +85,9 @@
                 solved[r] = rows[r] * inverse[r]
                 for c in range(r + 1, BLOCK):
                     solved[r] = solved[r] - scaled[c, r] * solved[c]
+            update = product(before, gather(solved), ((0,), (0,)))
             for k in range(block + 1 + AHEAD, count):
-                terms = [lanes_of(tiles[k], offset + c) * solved[c] for c in range(BLOCK)]
-                while len(terms) > 1:
-                    terms = [terms[t] + terms[t + 1] for t in range(0, len(terms), 2)]
-                tiles[k] = jnp.where(in_block, 0.0, tiles[k]) - terms[0]
+                tiles[k] = jnp.where(in_block, 0.0, tiles[k]) - update[k * BLOCK : (k + 1) * BLOCK, :]
     return jnp.concatenate(lower_rows, axis=0)
 
 
@@ -102,7 +101,7 @@
     return jnp.where(ids < live_ref[0], part, 0.0)
 
 
-def sums_kernel(total_rows, snapshots_hbm, volumes_hbm, live_ref, probes_hbm, part_ref, keep_ref, send_ref, snapshots_ref, volumes_ref, probes_ref, packed, sems):
+def sums_kernel(total_rows, snapshots_hbm, volumes_hbm, live_ref, probes_hbm, part_ref, keep_ref, send_ref, scale_ref, snapshots_ref, volumes_ref, probes_ref, packed, sems):
     copies = [
         pltpu.make_async_copy(source, target, sems.at[i])
         for i, (source, target) in enumerate(
@@ -116,6 +115,7 @@
     half = order // 2
     copies[0].wait()
     volume = jnp.concatenate([live_volumes(volumes_ref, live_ref, b) for b in range(0, row_count, LANES)], axis=1)
+    scale_ref[...] = jnp.sqrt(volume)
     copies[1].wait()
     snapshots = snapshots_ref[...]
     scaled = snapshots.T * (volume * (1.0 / total_rows))
@@ -144,6 +144,10 @@
         send_ref[...] = packed[:middle, :]
 
 
+def hold(array):
+    return pltpu.with_memory_space_constraint(array, pltpu.HBM)
+
+
 def local_sums(total_rows, snapshots, volumes, live_rows, probes, part):
     order = snapshots.shape[1]
     size = packed_rows(order, probes.shape[0])
@@ -152,9 +156,9 @@
     scalar = pl.BlockSpec(memory_space=pltpu.SMEM)
     return pl.pallas_call(
         functools.partial(sums_kernel, total_rows),
-        out_shape=(jax.ShapeDtypeStruct((size // 2, order), F32),) * 2,
+        out_shape=(jax.ShapeDtypeStruct((size // 2, order), F32),) * 2 + (jax.ShapeDtypeStruct((1, volumes.shape[0]), F32),),
         in_specs=[hbm, hbm, scalar, hbm, scalar],
-        out_specs=(whole, whole),
+        out_specs=(whole, whole, whole),
         scratch_shapes=[
             pltpu.VMEM(snapshots.shape, F32),
             pltpu.VMEM(volumes.shape, F32),
@@ -163,29 +167,27 @@
             pltpu.SemaphoreType.DMA((3,)),
         ],
         compiler_params=pltpu.CompilerParams(vmem_limit_bytes=24 * 1024 * 1024),
-    )(*(pltpu.with_memory_space_constraint(x, pltpu.HBM) for x in (snapshots, volumes)), live_rows, pltpu.with_memory_space_constraint(probes, pltpu.HBM), part)
-
-
-def weigh_kernel(snapshots_ref, volumes_ref, live_ref, weighted_ref):
+    )(hold(snapshots), hold(volumes), live_rows, hold(probes), part)
+
+
+def weigh_kernel(snapshots_ref, scale_ref, weighted_ref):
     row_count, order = snapshots_ref.shape
     for begin in range(0, row_count, LANES):
-        scale = jnp.sqrt(live_volumes(volumes_ref, live_ref, begin))
-        scale = jnp.broadcast_to(scale, (LANES, LANES)).T
         rows = pl.ds(begin, LANES)
+        scale = jnp.broadcast_to(scale_ref[:, rows], (LANES, LANES)).T
         weighted_ref[rows, :] = snapshots_ref[rows, :] * jnp.concatenate([scale] * (order // LANES), axis=1)
 
 
-def weigh(snapshots, volumes, live_rows):
+def weigh(snapshots, scale):
     whole = pl.BlockSpec(memory_space=pltpu.VMEM)
-    scalar = pl.BlockSpec(memory_space=pltpu.SMEM)
     return pl.pallas_call(
         weigh_kernel,
         out_shape=jax.ShapeDtypeStruct(snapshots.shape, F32),
-        in_specs=[whole, whole, scalar],
+        in_specs=[whole, whole],
         out_specs=whole,
         compiler_params=pltpu.CompilerParams(vmem_limit_bytes=24 * 1024 * 1024),
         cost_estimate=pl.CostEstimate(flops=snapshots.size, bytes_accessed=8 * snapshots.size, transcendentals=0),
-    )(snapshots, volumes, live_rows)
+    )(snapshots, scale)
 
 
 def finish_kernel(mine_ref, other_ref, weighted_ref, part_ref, basis_ref, factor_ref, coef_ref):
@@ -267,9 +269,9 @@
     count = lax.axis_size("cells") * lax.axis_size("sub")
     index = lax.axis_index("cells") * lax.axis_size("sub") + lax.axis_index("sub")
     part = (lax.population_count(index.astype(jnp.int32)) % 2).reshape(1)
-    keep, send = local_sums(snapshots.shape[0] * count, snapshots, volumes, live_rows, probes, part)
+    keep, send, scale = local_sums(snapshots.shape[0] * count, snapshots, volumes, live_rows, probes, part)
     mine, other = reduce_halves(keep, send)
-    return finish(mine, other, weigh(snapshots, volumes, live_rows), part, probes.shape[0])
+    return finish(mine, other, weigh(snapshots, scale), part, probes.shape[0])
 
 
 def solution(mesh):

time: 32.2 us -> 34.5 us (1.071)
  Pallas kernels: 10.3 us -> 12.6 us
    pallas_call x1, Pallas kernels: 7.67 us -> 10 us  [finish(): pl.pallas_call(finish_kernel, out_shape=(jax.ShapeDtypeStruct((row_count,...]
where the time goes in v8:
time: 34.5 us; the launch traced here: 34.4 us
  Pallas kernels  12.6 us (37%)
  waiting for transfers between devices  11.2 us (32%)
  starting transfers between devices  9.11 us (26%)
  between operations  1.34 us (4%)
    ppermute x8, waiting for transfers between devices, exchange(): return lax.ppermute(value, ('cells', 'sub'), pairs)  11.2 us
    pallas_call x1, Pallas kernels, finish(): pl.pallas_call(finish_kernel, out_shape=(jax.ShapeDtypeStruct((row_count,...  10 us
    ppermute x8, starting transfers between devices, exchange(): return lax.ppermute(value, ('cells', 'sub'), pairs)  9.11 us
    pallas_call x1, Pallas kernels, local_sums(): pl.pallas_call(functools.partial(sums_kernel, total_rows), out_shape=(jax...  2.48 us
  transfers between devices with their start and end apart: 8, of which 6 were waited for; matrix products, arithmetic and copies ran while one was open for 0% of the time, Pallas kernels for 0%

profile of v8, /device:TPU:0, one launch (start us, length us, event | category | flops | bytes accessed | tf_op | source)
XLA Modules:
  0.0 34.4 jit_solution(12724271435051552428)
XLA Ops:
  1.3 2.5 %shard_map.67 = (f32[104,256]{1,0:T(8,128)S(1)}, f32[104,256]{1,0:T(8,128)S(1)}, f32[1,512]{1,0:T(1,128)S(1)}) custom-call(f32[512,256]{1,0:T(8,128)} %snapshots_ref.1, f32[512]{0:T(512)} %volumes_hbm.1, s32[1]{0:T(128)S(6)} %copy.7.live_ref, f32[64,512]{1,0:T(8,128)} %probes_hbm.1, s32[1]{0:T(128)} %bitcast.part_ref), custom_call_target="tpu_custom_call" | custom-call | tf_op jit(solution)/shard_map/pallas_call | solution.py:157
  3.8 0.5 %collective-permute-start = (f32[104,256]{1,0:T(8,128)S(1)}, f32[104,256]{1,0:T(8,128)S(1)}, u32[]{:S(2)}, u32[]{:S(2)}) collective-permute-start(f32[104,256]{1,0:T(8,128)S(1)} %get-tuple-element.7), channel_id=1, source_target_pairs={{0,1},{1,0},{2,3},{3,2},{4,5},{5,4},{6,7},{7,6},{8,9},{9,8},{10,11... | collective-permute-start | bytes 319496 | tf_op jit(solution)/shard_map/ppermute | solution.py:249
  4.3 1.0 %collective-permute-done = f32[104,256]{1,0:T(8,128)S(1)} collective-permute-done((f32[104,256]{1,0:T(8,128)S(1)}, f32[104,256]{1,0:T(8,128)S(1)}, u32[]{:S(2)}, u32[]{:S(2)}) %collective-permute-start) | collective-permute-done | bytes 106528 | tf_op jit(solution)/shard_map/ppermute | solution.py:249
  5.3 0.0 copy-start
  5.3 3.9 %collective-permute-start.3 = (f32[104,256]{1,0:T(8,128)S(1)}, f32[104,256]{1,0:T(8,128)S(1)}, u32[]{:S(2)}, u32[]{:S(2)}) collective-permute-start(f32[104,256]{1,0:T(8,128)S(1)} %add.30), channel_id=1, source_target_pairs={{0,6},{1,25},{2,26},{3,5},{4,28},{5,3},{6,0},{7,31},{8,16},{9,15},... | collective-permute-start | bytes 319496 | tf_op jit(solution)/shard_map/ppermute | solution.py:249
  9.1 0.0 collective-permute-start.2
  9.2 0.4 %collective-permute-start.1 = (f32[104,256]{1,0:T(8,128)S(1)}, f32[104,256]{1,0:T(8,128)S(1)}, u32[]{:S(2)}, u32[]{:S(2)}) collective-permute-start(f32[104,256]{1,0:T(8,128)S(1)} %add.30), channel_id=1, source_target_pairs={{0,3},{1,8},{2,11},{3,0},{4,13},{5,6},{6,5},{7,14},{8,1},{9,10},{1... | collective-permute-start | bytes 319496 | tf_op jit(solution)/shard_map/ppermute | solution.py:249
  9.5 2.3 %collective-permute-done.3 = f32[104,256]{1,0:T(8,128)S(1)} collective-permute-done((f32[104,256]{1,0:T(8,128)S(1)}, f32[104,256]{1,0:T(8,128)S(1)}, u32[]{:S(2)}, u32[]{:S(2)}) %collective-permute-start.3) | collective-permute-done | bytes 106528 | tf_op jit(solution)/shard_map/ppermute | solution.py:249
  11.8 1.4 %collective-permute-done.2 = f32[104,256]{1,0:T(8,128)S(1)} collective-permute-done((f32[104,256]{1,0:T(8,128)S(1)}, f32[104,256]{1,0:T(8,128)S(1)}, u32[]{:S(2)}, u32[]{:S(2)}) %collective-permute-start.2) | collective-permute-done | bytes 106528 | tf_op jit(solution)/shard_map/ppermute | solution.py:249
  13.3 0.0 collective-permute-done.1
  13.3 3.8 %collective-permute-start.6 = (f32[104,256]{1,0:T(8,128)S(1)}, f32[104,256]{1,0:T(8,128)S(1)}, u32[]{:S(2)}, u32[]{:S(2)}) collective-permute-start(f32[104,256]{1,0:T(8,128)S(1)} %add_add_fusion.1), channel_id=1, source_target_pairs={{0,24},{1,7},{2,4},{3,27},{4,2},{5,29},{6,30},{7,1},{8,14},{9,17},... | collective-permute-start | bytes 319496 | tf_op jit(solution)/shard_map/ppermute | solution.py:249
  17.1 0.0 collective-permute-start.5
  17.1 0.4 %collective-permute-start.4 = (f32[104,256]{1,0:T(8,128)S(1)}, f32[104,256]{1,0:T(8,128)S(1)}, u32[]{:S(2)}, u32[]{:S(2)}) collective-permute-start(f32[104,256]{1,0:T(8,128)S(1)} %add_add_fusion.1), channel_id=1, source_target_pairs={{0,9},{1,2},{2,1},{3,10},{4,7},{5,12},{6,15},{7,4},{8,11},{9,0},{1... | collective-permute-start | bytes 319496 | tf_op jit(solution)/shard_map/ppermute | solution.py:249
  17.5 2.5 %collective-permute-done.6 = f32[104,256]{1,0:T(8,128)S(1)} collective-permute-done((f32[104,256]{1,0:T(8,128)S(1)}, f32[104,256]{1,0:T(8,128)S(1)}, u32[]{:S(2)}, u32[]{:S(2)}) %collective-permute-start.6) | collective-permute-done | bytes 106528 | tf_op jit(solution)/shard_map/ppermute | solution.py:249
  20.0 3.0 %collective-permute-done.5 = f32[104,256]{1,0:T(8,128)S(1)} collective-permute-done((f32[104,256]{1,0:T(8,128)S(1)}, f32[104,256]{1,0:T(8,128)S(1)}, u32[]{:S(2)}, u32[]{:S(2)}) %collective-permute-start.5) | collective-permute-done | bytes 106528 | tf_op jit(solution)/shard_map/ppermute | solution.py:249
  23.0 0.0 collective-permute-done.4
  23.0 0.2 collective-permute-start.7
  23.2 0.0 copy-done
  23.2 0.1 shard_map.68.weighted_ref
  23.3 1.1 %collective-permute-done.7.other_ref = f32[104,256]{1,0:T(8,128)S(1)} collective-permute-done((f32[104,256]{1,0:T(8,128)S(1)}, f32[104,256]{1,0:T(8,128)S(1)}, u32[]{:S(2)}, u32[]{:S(2)}) %collective-permute-start.7) | collective-permute-done | bytes 106528 | tf_op jit(solution)/shard_map/ppermute | solution.py:249
  24.4 10.0 %shard_map.69 = (f32[512,256]{1,0:T(8,128)}, f32[256,256]{1,0:T(8,128)}, f32[64,256]{1,0:T(8,128)}) custom-call(f32[104,256]{1,0:T(8,128)S(1)} %add_add_fusion.mine_ref, f32[104,256]{1,0:T(8,128)S(1)} %collective-permute-done.7.other_ref, f32[512,256]{1,0:T(8,128)S(1)} %shard_map.68.weighted_ref, s32[1]{0:T(128)} %bitcast.part_ref), custom_call_target="tpu_custom_call" | custom-call | tf_op jit(solution)/shard_map/pallas_call | solution.py:233
  (3 shorter events, 0.1 us)
Async XLA Ops:
  3.8 1.5 %collective-permute-start = (f32[104,256]{1,0:T(8,128)S(1)}, f32[104,256]{1,0:T(8,128)S(1)}, u32[]{:S(2)}, u32[]{:S(2)}) collective-permute-start(f32[104,256]{1,0:T(8,128)S(1)} %get-tuple-element.7), channel_id=1, source_target_pairs={{0,1},{1,0},{2,3},{3,2},{4,5},{5,4},{6,7},{7,6},{8,9},{9,8},{10,11... | collective-permute-start | bytes 319496 | tf_op jit(solution)/shard_map/ppermute | solution.py:249
  5.3 17.9 %copy-start = (f32[512,256]{1,0:T(8,128)S(1)}, f32[512,256]{1,0:T(8,128)}, u32[]{:S(2)}) copy-start(f32[512,256]{1,0:T(8,128)} %snapshots_ref.1) | copy-start | bytes 1572868
  5.3 6.5 %collective-permute-start.3 = (f32[104,256]{1,0:T(8,128)S(1)}, f32[104,256]{1,0:T(8,128)S(1)}, u32[]{:S(2)}, u32[]{:S(2)}) collective-permute-start(f32[104,256]{1,0:T(8,128)S(1)} %add.30), channel_id=1, source_target_pairs={{0,6},{1,25},{2,26},{3,5},{4,28},{5,3},{6,0},{7,31},{8,16},{9,15},... | collective-permute-start | bytes 319496 | tf_op jit(solution)/shard_map/ppermute | solution.py:249
  9.1 4.1 %collective-permute-start.2 = (f32[104,256]{1,0:T(8,128)S(1)}, f32[104,256]{1,0:T(8,128)S(1)}, u32[]{:S(2)}, u32[]{:S(2)}) collective-permute-start(f32[104,256]{1,0:T(8,128)S(1)} %add.30), channel_id=1, source_target_pairs={{0,5},{1,16},{2,19},{3,6},{4,21},{5,0},{6,3},{7,22},{8,25},{9,12},... | collective-permute-start | bytes 319496 | tf_op jit(solution)/shard_map/ppermute | solution.py:249
  9.2 4.1 %collective-permute-start.1 = (f32[104,256]{1,0:T(8,128)S(1)}, f32[104,256]{1,0:T(8,128)S(1)}, u32[]{:S(2)}, u32[]{:S(2)}) collective-permute-start(f32[104,256]{1,0:T(8,128)S(1)} %add.30), channel_id=1, source_target_pairs={{0,3},{1,8},{2,11},{3,0},{4,13},{5,6},{6,5},{7,14},{8,1},{9,10},{1... | collective-permute-start | bytes 319496 | tf_op jit(solution)/shard_map/ppermute | solution.py:249
  13.3 6.7 %collective-permute-start.6 = (f32[104,256]{1,0:T(8,128)S(1)}, f32[104,256]{1,0:T(8,128)S(1)}, u32[]{:S(2)}, u32[]{:S(2)}) collective-permute-start(f32[104,256]{1,0:T(8,128)S(1)} %add_add_fusion.1), channel_id=1, source_target_pairs={{0,24},{1,7},{2,4},{3,27},{4,2},{5,29},{6,30},{7,1},{8,14},{9,17},... | collective-permute-start | bytes 319496 | tf_op jit(solution)/shard_map/ppermute | solution.py:249
  17.1 5.8 %collective-permute-start.5 = (f32[104,256]{1,0:T(8,128)S(1)}, f32[104,256]{1,0:T(8,128)S(1)}, u32[]{:S(2)}, u32[]{:S(2)}) collective-permute-start(f32[104,256]{1,0:T(8,128)S(1)} %add_add_fusion.1), channel_id=1, source_target_pairs={{0,17},{1,4},{2,7},{3,18},{4,1},{5,20},{6,23},{7,2},{8,13},{9,24},... | collective-permute-start | bytes 319496 | tf_op jit(solution)/shard_map/ppermute | solution.py:249
  17.1 5.8 %collective-permute-start.4 = (f32[104,256]{1,0:T(8,128)S(1)}, f32[104,256]{1,0:T(8,128)S(1)}, u32[]{:S(2)}, u32[]{:S(2)}) collective-permute-start(f32[104,256]{1,0:T(8,128)S(1)} %add_add_fusion.1), channel_id=1, source_target_pairs={{0,9},{1,2},{2,1},{3,10},{4,7},{5,12},{6,15},{7,4},{8,11},{9,0},{1... | collective-permute-start | bytes 319496 | tf_op jit(solution)/shard_map/ppermute | solution.py:249
  23.0 1.4 %collective-permute-start.7 = (f32[104,256]{1,0:T(8,128)S(1)}, f32[104,256]{1,0:T(8,128)S(1)}, u32[]{:S(2)}, u32[]{:S(2)}) collective-permute-start(f32[104,256]{1,0:T(8,128)S(1)} %add_add_fusion.mine_ref), channel_id=1, source_target_pairs={{0,1},{1,0},{2,3},{3,2},{4,5},{5,4},{6,7},{7,6},{8,9},{9,8},{10,11... | collective-permute-start | bytes 319496 | tf_op jit(solution)/shard_map/ppermute | solution.py:249

commit v9 on v8

--- a/solution.py
+++ b/solution.py
@@ -25,7 +25,7 @@
     return lax.dot_general(left, right, (dims, ((), ())), precision=HIGHEST, preferred_element_type=F32)
 
 
-def eliminate(matrix):
+def eliminate(matrix, tasks=()):
     width = matrix.shape[1]
     count = width // BLOCK
     shape = (BLOCK, width)
@@ -40,14 +40,14 @@
             total = jnp.where(sub_ids == r, parts[r], total)
         return total
 
+    tasks = iter(tasks)
     lower_rows = []
     following = [lanes_of(tiles[0], c) for c in range(BLOCK)]
     for block in range(count):
         offset = block * BLOCK
         in_block = (lane_ids >= offset) & (lane_ids < offset + BLOCK)
         columns = following
-        before = tiles[block]
-        own = jnp.where(in_block, jnp.where(spread_ids == offset, 1.0, 0.0), before)
+        own = jnp.where(in_block, jnp.where(spread_ids == offset, 1.0, 0.0), tiles[block])
         rows = [row_of(own, r) for r in range(BLOCK)]
         near = range(block + 1, min(block + 1 + AHEAD, count))
         weights = {k: [lanes_of(tiles[k], offset + c) for c in range(BLOCK)] for k in near}
@@ -85,9 +85,16 @@
                 solved[r] = rows[r] * inverse[r]
                 for c in range(r + 1, BLOCK):
                     solved[r] = solved[r] - scaled[c, r] * solved[c]
-            update = product(before, gather(solved), ((0,), (0,)))
             for k in range(block + 1 + AHEAD, count):
-                tiles[k] = jnp.where(in_block, 0.0, tiles[k]) - update[k * BLOCK : (k + 1) * BLOCK, :]
+                terms = [lanes_of(tiles[k], offset + c) * solved[c] for c in range(BLOCK)]
+                while len(terms) > 1:
+                    terms = [terms[t] + terms[t + 1] for t in range(0, len(terms), 2)]
+                tiles[k] = jnp.where(in_block, 0.0, tiles[k]) - terms[0]
+        for task in tasks:
+            task()
+            break
+    for task in tasks:
+        task()
     return jnp.concatenate(lower_rows, axis=0)
 
 
@@ -190,10 +197,19 @@
     )(snapshots, scale)
 
 
-def finish_kernel(mine_ref, other_ref, weighted_ref, part_ref, basis_ref, factor_ref, coef_ref):
-    order = weighted_ref.shape[1]
+def finish_kernel(mine_ref, other_ref, weighted_ref, part_ref, basis_hbm, factor_hbm, coef_hbm, basis_ref, factor_ref, coef_ref, rest_ref, sems):
+    row_count, order = weighted_ref.shape
     probes = coef_ref.shape[0]
     half = order // 2
+    chunks = [pl.ds(begin, LANES) for begin in range(0, row_count, LANES)]
+    left, right = pl.ds(0, half), pl.ds(half, half)
+    copies = []
+
+    def write(source, target, place):
+        copy = pltpu.make_async_copy(source.at[place], target.at[place], sems.at[len(copies)])
+        copy.start()
+        copies.append(copy)
+
     low = part_ref[0] == 0
     mine, other = mine_ref[...], other_ref[...]
     packed = jnp.concatenate([jnp.where(low, mine, other), jnp.where(low, other, mine)], axis=0)
@@ -210,35 +226,61 @@
     beside = product(inverse, packed[:half, half:], ((1,), (0,)))
     second = jnp.where(row_ids > column_ids, square, turned)
     second = jnp.where(row_ids == column_ids, diagonal, second) - product(beside, beside, ((0,), (0,)))
-    factor_ref[:half, :half] = jnp.where(in_upper, product(inverse, first, ((1,), (0,))), 0.0)
-    factor_ref[:half, half:] = beside
-    factor_ref[half:, :half] = jnp.zeros((half, half), F32)
-
-    left = product(cross[:, :half], inverse, ((1,), (1,)))
-    coef_ref[:, :half] = left
-    cross_rest = cross[:, half:] - product(left, beside, ((1,), (0,)))
-    left = product(weighted_ref[:, :half], inverse, ((1,), (1,)))
-    basis_ref[:, :half] = left
-    rest = weighted_ref[:, half:] - product(left, beside, ((1,), (0,)))
-
-    inverse_second = eliminate(second)
-    coef_ref[:, half:] = product(cross_rest, inverse_second, ((1,), (1,)))
-    basis_ref[:, half:] = product(rest, inverse_second, ((1,), (1,)))
-    factor_ref[half:, half:] = jnp.where(in_upper, product(inverse_second, second, ((1,), (0,))), 0.0)
+
+    def basis_left(rows):
+        def task():
+            basis_ref[rows, left] = product(weighted_ref[rows, left], inverse, ((1,), (1,)))
+            write(basis_ref, basis_hbm, (rows, left))
+
+        return task
+
+    def basis_rest(rows):
+        def task():
+            rest_ref[rows, :] = weighted_ref[rows, right] - product(basis_ref[rows, left], beside, ((1,), (0,)))
+
+        return task
+
+    def coef_left():
+        coef_ref[:, left] = product(cross[:, :half], inverse, ((1,), (1,)))
+
+    def coef_rest():
+        coef_ref[:, right] = cross[:, half:] - product(coef_ref[:, left], beside, ((1,), (0,)))
+
+    def factor_top():
+        top = pl.ds(0, half)
+        factor_ref[top, left] = jnp.where(in_upper, product(inverse, first, ((1,), (0,))), 0.0)
+        factor_ref[top, right] = beside
+        write(factor_ref, factor_hbm, (top, pl.ds(0, order)))
+
+    tasks = [task(rows) for task in (basis_left, basis_rest) for rows in chunks]
+    inverse_second = eliminate(second, tasks + [coef_left, coef_rest, factor_top])
+    for rows in chunks:
+        basis_ref[rows, right] = product(rest_ref[rows, :], inverse_second, ((1,), (1,)))
+        write(basis_ref, basis_hbm, (rows, right))
+    bottom = pl.ds(half, half)
+    factor_ref[bottom, left] = jnp.zeros((half, half), F32)
+    factor_ref[bottom, right] = jnp.where(in_upper, product(inverse_second, second, ((1,), (0,))), 0.0)
+    write(factor_ref, factor_hbm, (bottom, pl.ds(0, order)))
+    coef_ref[:, right] = product(coef_ref[:, right], inverse_second, ((1,), (1,)))
+    write(coef_ref, coef_hbm, (pl.ds(0, probes), pl.ds(0, order)))
+    for copy in copies:
+        copy.wait()
 
 
 def finish(mine, other, weighted, part, probes):
     row_count, order = weighted.shape
     whole = pl.BlockSpec(memory_space=pltpu.VMEM)
+    shapes = (row_count, order), (order, order), (probes, order)
     return pl.pallas_call(
         finish_kernel,
-        out_shape=(
-            jax.ShapeDtypeStruct((row_count, order), F32),
-            jax.ShapeDtypeStruct((order, order), F32),
-            jax.ShapeDtypeStruct((probes, order), F32),
-        ),
+        out_shape=tuple(jax.ShapeDtypeStruct(shape, F32) for shape in shapes),
         in_specs=[whole] * 3 + [pl.BlockSpec(memory_space=pltpu.SMEM)],
-        out_specs=(whole,) * 3,
+        out_specs=(pl.BlockSpec(memory_space=pltpu.HBM),) * 3,
+        scratch_shapes=[
+            *(pltpu.VMEM(shape, F32) for shape in shapes),
+            pltpu.VMEM((row_count, order // 2), F32),
+            pltpu.SemaphoreType.DMA((2 * (row_count // LANES) + 3,)),
+        ],
         compiler_params=pltpu.CompilerParams(vmem_limit_bytes=32 * 1024 * 1024),
     )(mine, other, weighted, part)
 

time: 34.5 us -> 32.4 us (0.939)
  Pallas kernels: 12.6 us -> 10.4 us
    pallas_call x1, Pallas kernels: 10 us -> 7.81 us  [finish(): pl.pallas_call(finish_kernel, out_shape=tuple((jax.ShapeDtypeStruct(shape...]
where the time goes in v9:
time: 32.4 us; the launch traced here: 32.2 us
  waiting for transfers between devices  11.2 us (35%)
  Pallas kernels  10.4 us (32%)
  starting transfers between devices  9.11 us (28%)
  between operations  1.34 us (4%)
    ppermute x8, waiting for transfers between devices, exchange(): return lax.ppermute(value, ('cells', 'sub'), pairs)  11.2 us
    ppermute x8, starting transfers between devices, exchange(): return lax.ppermute(value, ('cells', 'sub'), pairs)  9.11 us
    pallas_call x1, Pallas kernels, finish(): pl.pallas_call(finish_kernel, out_shape=tuple((jax.ShapeDtypeStruct(shape...  7.81 us
    pallas_call x1, Pallas kernels, local_sums(): pl.pallas_call(functools.partial(sums_kernel, total_rows), out_shape=(jax...  2.48 us
  transfers between devices with their start and end apart: 8, of which 6 were waited for; matrix products, arithmetic and copies ran while one was open for 0% of the time, Pallas kernels for 0%

profile of v9, /device:TPU:0, one launch (start us, length us, event | category | flops | bytes accessed | tf_op | source)
XLA Modules:
  0.0 32.2 jit_solution(10430472724017543467)
XLA Ops:
  1.3 2.5 %shard_map.67 = (f32[104,256]{1,0:T(8,128)S(1)}, f32[104,256]{1,0:T(8,128)S(1)}, f32[1,512]{1,0:T(1,128)S(1)}) custom-call(f32[512,256]{1,0:T(8,128)} %snapshots_ref.1, f32[512]{0:T(512)} %volumes_hbm.1, s32[1]{0:T(128)S(6)} %copy.7.live_ref, f32[64,512]{1,0:T(8,128)} %probes_hbm.1, s32[1]{0:T(128)} %bitcast.part_ref), custom_call_target="tpu_custom_call" | custom-call | tf_op jit(solution)/shard_map/pallas_call | solution.py:164
  3.8 0.5 %collective-permute-start = (f32[104,256]{1,0:T(8,128)S(1)}, f32[104,256]{1,0:T(8,128)S(1)}, u32[]{:S(2)}, u32[]{:S(2)}) collective-permute-start(f32[104,256]{1,0:T(8,128)S(1)} %get-tuple-element.7), channel_id=1, source_target_pairs={{0,1},{1,0},{2,3},{3,2},{4,5},{5,4},{6,7},{7,6},{8,9},{9,8},{10,11... | collective-permute-start | bytes 319496 | tf_op jit(solution)/shard_map/ppermute | solution.py:291
  4.3 1.0 %collective-permute-done = f32[104,256]{1,0:T(8,128)S(1)} collective-permute-done((f32[104,256]{1,0:T(8,128)S(1)}, f32[104,256]{1,0:T(8,128)S(1)}, u32[]{:S(2)}, u32[]{:S(2)}) %collective-permute-start) | collective-permute-done | bytes 106528 | tf_op jit(solution)/shard_map/ppermute | solution.py:291
  5.3 0.0 copy-start
  5.3 3.9 %collective-permute-start.3 = (f32[104,256]{1,0:T(8,128)S(1)}, f32[104,256]{1,0:T(8,128)S(1)}, u32[]{:S(2)}, u32[]{:S(2)}) collective-permute-start(f32[104,256]{1,0:T(8,128)S(1)} %add.30), channel_id=1, source_target_pairs={{0,6},{1,25},{2,26},{3,5},{4,28},{5,3},{6,0},{7,31},{8,16},{9,15},... | collective-permute-start | bytes 319496 | tf_op jit(solution)/shard_map/ppermute | solution.py:291
  9.1 0.0 collective-permute-start.2
  9.2 0.4 %collective-permute-start.1 = (f32[104,256]{1,0:T(8,128)S(1)}, f32[104,256]{1,0:T(8,128)S(1)}, u32[]{:S(2)}, u32[]{:S(2)}) collective-permute-start(f32[104,256]{1,0:T(8,128)S(1)} %add.30), channel_id=1, source_target_pairs={{0,3},{1,8},{2,11},{3,0},{4,13},{5,6},{6,5},{7,14},{8,1},{9,10},{1... | collective-permute-start | bytes 319496 | tf_op jit(solution)/shard_map/ppermute | solution.py:291
  9.5 2.3 %collective-permute-done.3 = f32[104,256]{1,0:T(8,128)S(1)} collective-permute-done((f32[104,256]{1,0:T(8,128)S(1)}, f32[104,256]{1,0:T(8,128)S(1)}, u32[]{:S(2)}, u32[]{:S(2)}) %collective-permute-start.3) | collective-permute-done | bytes 106528 | tf_op jit(solution)/shard_map/ppermute | solution.py:291
  11.8 1.4 %collective-permute-done.2 = f32[104,256]{1,0:T(8,128)S(1)} collective-permute-done((f32[104,256]{1,0:T(8,128)S(1)}, f32[104,256]{1,0:T(8,128)S(1)}, u32[]{:S(2)}, u32[]{:S(2)}) %collective-permute-start.2) | collective-permute-done | bytes 106528 | tf_op jit(solution)/shard_map/ppermute | solution.py:291
  13.3 0.0 collective-permute-done.1
  13.3 3.8 %collective-permute-start.6 = (f32[104,256]{1,0:T(8,128)S(1)}, f32[104,256]{1,0:T(8,128)S(1)}, u32[]{:S(2)}, u32[]{:S(2)}) collective-permute-start(f32[104,256]{1,0:T(8,128)S(1)} %add_add_fusion.1), channel_id=1, source_target_pairs={{0,24},{1,7},{2,4},{3,27},{4,2},{5,29},{6,30},{7,1},{8,14},{9,17},... | collective-permute-start | bytes 319496 | tf_op jit(solution)/shard_map/ppermute | solution.py:291
  17.1 0.0 collective-permute-start.5
  17.1 0.4 %collective-permute-start.4 = (f32[104,256]{1,0:T(8,128)S(1)}, f32[104,256]{1,0:T(8,128)S(1)}, u32[]{:S(2)}, u32[]{:S(2)}) collective-permute-start(f32[104,256]{1,0:T(8,128)S(1)} %add_add_fusion.1), channel_id=1, source_target_pairs={{0,9},{1,2},{2,1},{3,10},{4,7},{5,12},{6,15},{7,4},{8,11},{9,0},{1... | collective-permute-start | bytes 319496 | tf_op jit(solution)/shard_map/ppermute | solution.py:291
  17.5 2.5 %collective-permute-done.6 = f32[104,256]{1,0:T(8,128)S(1)} collective-permute-done((f32[104,256]{1,0:T(8,128)S(1)}, f32[104,256]{1,0:T(8,128)S(1)}, u32[]{:S(2)}, u32[]{:S(2)}) %collective-permute-start.6) | collective-permute-done | bytes 106528 | tf_op jit(solution)/shard_map/ppermute | solution.py:291
  20.0 3.0 %collective-permute-done.5 = f32[104,256]{1,0:T(8,128)S(1)} collective-permute-done((f32[104,256]{1,0:T(8,128)S(1)}, f32[104,256]{1,0:T(8,128)S(1)}, u32[]{:S(2)}, u32[]{:S(2)}) %collective-permute-start.5) | collective-permute-done | bytes 106528 | tf_op jit(solution)/shard_map/ppermute | solution.py:291
  23.0 0.0 collective-permute-done.4
  23.0 0.2 collective-permute-start.7
  23.2 0.0 copy-done
  23.2 0.1 shard_map.68.weighted_ref
  23.3 1.1 %collective-permute-done.7.other_ref = f32[104,256]{1,0:T(8,128)S(1)} collective-permute-done((f32[104,256]{1,0:T(8,128)S(1)}, f32[104,256]{1,0:T(8,128)S(1)}, u32[]{:S(2)}, u32[]{:S(2)}) %collective-permute-start.7) | collective-permute-done | bytes 106528 | tf_op jit(solution)/shard_map/ppermute | solution.py:291
  24.4 7.8 %shard_map.69 = (f32[512,256]{1,0:T(8,128)}, f32[256,256]{1,0:T(8,128)}, f32[64,256]{1,0:T(8,128)}) custom-call(f32[104,256]{1,0:T(8,128)S(1)} %add_add_fusion.mine_ref, f32[104,256]{1,0:T(8,128)S(1)} %collective-permute-done.7.other_ref, f32[512,256]{1,0:T(8,128)S(1)} %shard_map.68.weighted_ref, s32[1]{0:T(128)} %bitcast.part_ref), custom_call_target="tpu_custom_call" | custom-call | tf_op jit(solution)/shard_map/pallas_call | solution.py:274
  (3 shorter events, 0.1 us)
Async XLA Ops:
  3.8 1.5 %collective-permute-start = (f32[104,256]{1,0:T(8,128)S(1)}, f32[104,256]{1,0:T(8,128)S(1)}, u32[]{:S(2)}, u32[]{:S(2)}) collective-permute-start(f32[104,256]{1,0:T(8,128)S(1)} %get-tuple-element.7), channel_id=1, source_target_pairs={{0,1},{1,0},{2,3},{3,2},{4,5},{5,4},{6,7},{7,6},{8,9},{9,8},{10,11... | collective-permute-start | bytes 319496 | tf_op jit(solution)/shard_map/ppermute | solution.py:291
  5.3 17.9 %copy-start = (f32[512,256]{1,0:T(8,128)S(1)}, f32[512,256]{1,0:T(8,128)}, u32[]{:S(2)}) copy-start(f32[512,256]{1,0:T(8,128)} %snapshots_ref.1) | copy-start | bytes 1572868
  5.3 6.5 %collective-permute-start.3 = (f32[104,256]{1,0:T(8,128)S(1)}, f32[104,256]{1,0:T(8,128)S(1)}, u32[]{:S(2)}, u32[]{:S(2)}) collective-permute-start(f32[104,256]{1,0:T(8,128)S(1)} %add.30), channel_id=1, source_target_pairs={{0,6},{1,25},{2,26},{3,5},{4,28},{5,3},{6,0},{7,31},{8,16},{9,15},... | collective-permute-start | bytes 319496 | tf_op jit(solution)/shard_map/ppermute | solution.py:291
  9.1 4.1 %collective-permute-start.2 = (f32[104,256]{1,0:T(8,128)S(1)}, f32[104,256]{1,0:T(8,128)S(1)}, u32[]{:S(2)}, u32[]{:S(2)}) collective-permute-start(f32[104,256]{1,0:T(8,128)S(1)} %add.30), channel_id=1, source_target_pairs={{0,5},{1,16},{2,19},{3,6},{4,21},{5,0},{6,3},{7,22},{8,25},{9,12},... | collective-permute-start | bytes 319496 | tf_op jit(solution)/shard_map/ppermute | solution.py:291
  9.2 4.1 %collective-permute-start.1 = (f32[104,256]{1,0:T(8,128)S(1)}, f32[104,256]{1,0:T(8,128)S(1)}, u32[]{:S(2)}, u32[]{:S(2)}) collective-permute-start(f32[104,256]{1,0:T(8,128)S(1)} %add.30), channel_id=1, source_target_pairs={{0,3},{1,8},{2,11},{3,0},{4,13},{5,6},{6,5},{7,14},{8,1},{9,10},{1... | collective-permute-start | bytes 319496 | tf_op jit(solution)/shard_map/ppermute | solution.py:291
  13.3 6.7 %collective-permute-start.6 = (f32[104,256]{1,0:T(8,128)S(1)}, f32[104,256]{1,0:T(8,128)S(1)}, u32[]{:S(2)}, u32[]{:S(2)}) collective-permute-start(f32[104,256]{1,0:T(8,128)S(1)} %add_add_fusion.1), channel_id=1, source_target_pairs={{0,24},{1,7},{2,4},{3,27},{4,2},{5,29},{6,30},{7,1},{8,14},{9,17},... | collective-permute-start | bytes 319496 | tf_op jit(solution)/shard_map/ppermute | solution.py:291
  17.1 5.8 %collective-permute-start.5 = (f32[104,256]{1,0:T(8,128)S(1)}, f32[104,256]{1,0:T(8,128)S(1)}, u32[]{:S(2)}, u32[]{:S(2)}) collective-permute-start(f32[104,256]{1,0:T(8,128)S(1)} %add_add_fusion.1), channel_id=1, source_target_pairs={{0,17},{1,4},{2,7},{3,18},{4,1},{5,20},{6,23},{7,2},{8,13},{9,24},... | collective-permute-start | bytes 319496 | tf_op jit(solution)/shard_map/ppermute | solution.py:291
  17.1 5.8 %collective-permute-start.4 = (f32[104,256]{1,0:T(8,128)S(1)}, f32[104,256]{1,0:T(8,128)S(1)}, u32[]{:S(2)}, u32[]{:S(2)}) collective-permute-start(f32[104,256]{1,0:T(8,128)S(1)} %add_add_fusion.1), channel_id=1, source_target_pairs={{0,9},{1,2},{2,1},{3,10},{4,7},{5,12},{6,15},{7,4},{8,11},{9,0},{1... | collective-permute-start | bytes 319496 | tf_op jit(solution)/shard_map/ppermute | solution.py:291
  23.0 1.4 %collective-permute-start.7 = (f32[104,256]{1,0:T(8,128)S(1)}, f32[104,256]{1,0:T(8,128)S(1)}, u32[]{:S(2)}, u32[]{:S(2)}) collective-permute-start(f32[104,256]{1,0:T(8,128)S(1)} %add_add_fusion.mine_ref), channel_id=1, source_target_pairs={{0,1},{1,0},{2,3},{3,2},{4,5},{5,4},{6,7},{7,6},{8,9},{9,8},{10,11... | collective-permute-start | bytes 319496 | tf_op jit(solution)/shard_map/ppermute | solution.py:291

commit v10 on v8

--- a/solution.py
+++ b/solution.py
@@ -42,17 +42,18 @@
 
     lower_rows = []
     following = [lanes_of(tiles[0], c) for c in range(BLOCK)]
+    carried = [lanes_of(tiles[1], c) for c in range(BLOCK)]
     for block in range(count):
         offset = block * BLOCK
         in_block = (lane_ids >= offset) & (lane_ids < offset + BLOCK)
         columns = following
-        before = tiles[block]
-        own = jnp.where(in_block, jnp.where(spread_ids == offset, 1.0, 0.0), before)
+        own = jnp.where(in_block, jnp.where(spread_ids == offset, 1.0, 0.0), tiles[block])
         rows = [row_of(own, r) for r in range(BLOCK)]
         near = range(block + 1, min(block + 1 + AHEAD, count))
-        weights = {k: [lanes_of(tiles[k], offset + c) for c in range(BLOCK)] for k in near}
-        if block + 1 < count:
-            following = [lanes_of(tiles[block + 1], offset + BLOCK + c) for c in range(BLOCK)]
+        weights = {k: [lanes_of(tiles[k], offset + c) for c in range(BLOCK)] for k in near if k > block + 1}
+        weights[block + 1] = carried
+        bases = {k: [lanes_of(tiles[k], offset + BLOCK + c) for c in range(BLOCK)] for k in near if k <= block + 2}
+        changes = {k: [None] * BLOCK for k in bases}
         for k in near:
             tiles[k] = jnp.where(in_block, 0.0, tiles[k])
         pivots, inverse, scaled = [row_of(columns[0], 0)], [], {}
@@ -70,13 +71,18 @@
                 here = weights[k][i]
                 weight = here * inv
                 if k == block + 1:
+                    splats = [row_of(here, c) for c in range(BLOCK)]
+                if k in changes:
                     for c in range(BLOCK):
-                        following[c] = following[c] - weight * row_of(here, c)
+                        change = weight * splats[c]
+                        changes[k][c] = change if i == 0 else changes[k][c] + change
                 for c in range(i + 1, BLOCK):
                     weights[k][c] = weights[k][c] - here * scaled[c, i]
                 tiles[k] = tiles[k] - weight * rows[i]
             for r in range(i + 1, BLOCK):
                 rows[r] = rows[r] - scaled[r, i] * rows[i]
+        updated = {k: [base - change for base, change in zip(bases[k], changes[k])] for k in bases}
+        following, carried = updated.get(block + 1), updated.get(block + 2)
         merged = gather(rows) * lax.rsqrt(gather(pivots))
         lower_rows.append(jnp.where(spread_ids <= offset, merged, 0.0))
         if block + 1 + AHEAD < count:
@@ -85,9 +91,11 @@
                 solved[r] = rows[r] * inverse[r]
                 for c in range(r + 1, BLOCK):
                     solved[r] = solved[r] - scaled[c, r] * solved[c]
-            update = product(before, gather(solved), ((0,), (0,)))
             for k in range(block + 1 + AHEAD, count):
-                tiles[k] = jnp.where(in_block, 0.0, tiles[k]) - update[k * BLOCK : (k + 1) * BLOCK, :]
+                terms = [lanes_of(tiles[k], offset + c) * solved[c] for c in range(BLOCK)]
+                while len(terms) > 1:
+                    terms = [terms[t] + terms[t + 1] for t in range(0, len(terms), 2)]
+                tiles[k] = jnp.where(in_block, 0.0, tiles[k]) - terms[0]
     return jnp.concatenate(lower_rows, axis=0)
 
 

time: 34.5 us -> 32 us (0.928)
  Pallas kernels: 12.6 us -> 10.1 us
    pallas_call x1, Pallas kernels: 10 us -> 7.45 us  [finish(): pl.pallas_call(finish_kernel, out_shape=(jax.ShapeDtypeStruct((row_count,...]
where the time goes in v10:
time: 32 us; the launch traced here: 31.8 us
  waiting for transfers between devices  11.2 us (35%)
  Pallas kernels  10.1 us (32%)
  starting transfers between devices  9.11 us (28%)
  between operations  1.34 us (4%)
    ppermute x8, waiting for transfers between devices, exchange(): return lax.ppermute(value, ('cells', 'sub'), pairs)  11.2 us
    ppermute x8, starting transfers between devices, exchange(): return lax.ppermute(value, ('cells', 'sub'), pairs)  9.11 us
    pallas_call x1, Pallas kernels, finish(): pl.pallas_call(finish_kernel, out_shape=(jax.ShapeDtypeStruct((row_count,...  7.45 us
    pallas_call x1, Pallas kernels, local_sums(): pl.pallas_call(functools.partial(sums_kernel, total_rows), out_shape=(jax...  2.48 us
  transfers between devices with their start and end apart: 8, of which 6 were waited for; matrix products, arithmetic and copies ran while one was open for 0% of the time, Pallas kernels for 0%

profile of v10, /device:TPU:0, one launch (start us, length us, event | category | flops | bytes accessed | tf_op | source)
XLA Modules:
  0.0 31.8 jit_solution(10952571944321852479)
XLA Ops:
  1.3 2.5 %shard_map.67 = (f32[104,256]{1,0:T(8,128)S(1)}, f32[104,256]{1,0:T(8,128)S(1)}, f32[1,512]{1,0:T(1,128)S(1)}) custom-call(f32[512,256]{1,0:T(8,128)} %snapshots_ref.1, f32[512]{0:T(512)} %volumes_hbm.1, s32[1]{0:T(128)S(6)} %copy.7.live_ref, f32[64,512]{1,0:T(8,128)} %probes_hbm.1, s32[1]{0:T(128)} %bitcast.part_ref), custom_call_target="tpu_custom_call" | custom-call | tf_op jit(solution)/shard_map/pallas_call | solution.py:165
  3.8 0.5 %collective-permute-start = (f32[104,256]{1,0:T(8,128)S(1)}, f32[104,256]{1,0:T(8,128)S(1)}, u32[]{:S(2)}, u32[]{:S(2)}) collective-permute-start(f32[104,256]{1,0:T(8,128)S(1)} %get-tuple-element.7), channel_id=1, source_target_pairs={{0,1},{1,0},{2,3},{3,2},{4,5},{5,4},{6,7},{7,6},{8,9},{9,8},{10,11... | collective-permute-start | bytes 319496 | tf_op jit(solution)/shard_map/ppermute | solution.py:257
  4.3 1.0 %collective-permute-done = f32[104,256]{1,0:T(8,128)S(1)} collective-permute-done((f32[104,256]{1,0:T(8,128)S(1)}, f32[104,256]{1,0:T(8,128)S(1)}, u32[]{:S(2)}, u32[]{:S(2)}) %collective-permute-start) | collective-permute-done | bytes 106528 | tf_op jit(solution)/shard_map/ppermute | solution.py:257
  5.3 0.0 copy-start
  5.3 3.9 %collective-permute-start.3 = (f32[104,256]{1,0:T(8,128)S(1)}, f32[104,256]{1,0:T(8,128)S(1)}, u32[]{:S(2)}, u32[]{:S(2)}) collective-permute-start(f32[104,256]{1,0:T(8,128)S(1)} %add.30), channel_id=1, source_target_pairs={{0,6},{1,25},{2,26},{3,5},{4,28},{5,3},{6,0},{7,31},{8,16},{9,15},... | collective-permute-start | bytes 319496 | tf_op jit(solution)/shard_map/ppermute | solution.py:257
  9.1 0.0 collective-permute-start.2
  9.2 0.4 %collective-permute-start.1 = (f32[104,256]{1,0:T(8,128)S(1)}, f32[104,256]{1,0:T(8,128)S(1)}, u32[]{:S(2)}, u32[]{:S(2)}) collective-permute-start(f32[104,256]{1,0:T(8,128)S(1)} %add.30), channel_id=1, source_target_pairs={{0,3},{1,8},{2,11},{3,0},{4,13},{5,6},{6,5},{7,14},{8,1},{9,10},{1... | collective-permute-start | bytes 319496 | tf_op jit(solution)/shard_map/ppermute | solution.py:257
  9.5 2.3 %collective-permute-done.3 = f32[104,256]{1,0:T(8,128)S(1)} collective-permute-done((f32[104,256]{1,0:T(8,128)S(1)}, f32[104,256]{1,0:T(8,128)S(1)}, u32[]{:S(2)}, u32[]{:S(2)}) %collective-permute-start.3) | collective-permute-done | bytes 106528 | tf_op jit(solution)/shard_map/ppermute | solution.py:257
  11.8 1.4 %collective-permute-done.2 = f32[104,256]{1,0:T(8,128)S(1)} collective-permute-done((f32[104,256]{1,0:T(8,128)S(1)}, f32[104,256]{1,0:T(8,128)S(1)}, u32[]{:S(2)}, u32[]{:S(2)}) %collective-permute-start.2) | collective-permute-done | bytes 106528 | tf_op jit(solution)/shard_map/ppermute | solution.py:257
  13.3 0.0 collective-permute-done.1
  13.3 3.8 %collective-permute-start.6 = (f32[104,256]{1,0:T(8,128)S(1)}, f32[104,256]{1,0:T(8,128)S(1)}, u32[]{:S(2)}, u32[]{:S(2)}) collective-permute-start(f32[104,256]{1,0:T(8,128)S(1)} %add_add_fusion.1), channel_id=1, source_target_pairs={{0,24},{1,7},{2,4},{3,27},{4,2},{5,29},{6,30},{7,1},{8,14},{9,17},... | collective-permute-start | bytes 319496 | tf_op jit(solution)/shard_map/ppermute | solution.py:257
  17.1 0.0 collective-permute-start.5
  17.1 0.4 %collective-permute-start.4 = (f32[104,256]{1,0:T(8,128)S(1)}, f32[104,256]{1,0:T(8,128)S(1)}, u32[]{:S(2)}, u32[]{:S(2)}) collective-permute-start(f32[104,256]{1,0:T(8,128)S(1)} %add_add_fusion.1), channel_id=1, source_target_pairs={{0,9},{1,2},{2,1},{3,10},{4,7},{5,12},{6,15},{7,4},{8,11},{9,0},{1... | collective-permute-start | bytes 319496 | tf_op jit(solution)/shard_map/ppermute | solution.py:257
  17.5 2.5 %collective-permute-done.6 = f32[104,256]{1,0:T(8,128)S(1)} collective-permute-done((f32[104,256]{1,0:T(8,128)S(1)}, f32[104,256]{1,0:T(8,128)S(1)}, u32[]{:S(2)}, u32[]{:S(2)}) %collective-permute-start.6) | collective-permute-done | bytes 106528 | tf_op jit(solution)/shard_map/ppermute | solution.py:257
  20.0 3.0 %collective-permute-done.5 = f32[104,256]{1,0:T(8,128)S(1)} collective-permute-done((f32[104,256]{1,0:T(8,128)S(1)}, f32[104,256]{1,0:T(8,128)S(1)}, u32[]{:S(2)}, u32[]{:S(2)}) %collective-permute-start.5) | collective-permute-done | bytes 106528 | tf_op jit(solution)/shard_map/ppermute | solution.py:257
  23.0 0.0 collective-permute-done.4
  23.0 0.2 collective-permute-start.7
  23.2 0.0 copy-done
  23.2 0.1 shard_map.68.weighted_ref
  23.3 1.1 %collective-permute-done.7.other_ref = f32[104,256]{1,0:T(8,128)S(1)} collective-permute-done((f32[104,256]{1,0:T(8,128)S(1)}, f32[104,256]{1,0:T(8,128)S(1)}, u32[]{:S(2)}, u32[]{:S(2)}) %collective-permute-start.7) | collective-permute-done | bytes 106528 | tf_op jit(solution)/shard_map/ppermute | solution.py:257
  24.4 7.5 %shard_map.69 = (f32[512,256]{1,0:T(8,128)}, f32[256,256]{1,0:T(8,128)}, f32[64,256]{1,0:T(8,128)}) custom-call(f32[104,256]{1,0:T(8,128)S(1)} %add_add_fusion.mine_ref, f32[104,256]{1,0:T(8,128)S(1)} %collective-permute-done.7.other_ref, f32[512,256]{1,0:T(8,128)S(1)} %shard_map.68.weighted_ref, s32[1]{0:T(128)} %bitcast.part_ref), custom_call_target="tpu_custom_call" | custom-call | tf_op jit(solution)/shard_map/pallas_call | solution.py:241
  (3 shorter events, 0.1 us)
Async XLA Ops:
  3.8 1.5 %collective-permute-start = (f32[104,256]{1,0:T(8,128)S(1)}, f32[104,256]{1,0:T(8,128)S(1)}, u32[]{:S(2)}, u32[]{:S(2)}) collective-permute-start(f32[104,256]{1,0:T(8,128)S(1)} %get-tuple-element.7), channel_id=1, source_target_pairs={{0,1},{1,0},{2,3},{3,2},{4,5},{5,4},{6,7},{7,6},{8,9},{9,8},{10,11... | collective-permute-start | bytes 319496 | tf_op jit(solution)/shard_map/ppermute | solution.py:257
  5.3 17.9 %copy-start = (f32[512,256]{1,0:T(8,128)S(1)}, f32[512,256]{1,0:T(8,128)}, u32[]{:S(2)}) copy-start(f32[512,256]{1,0:T(8,128)} %snapshots_ref.1) | copy-start | bytes 1572868
  5.3 6.5 %collective-permute-start.3 = (f32[104,256]{1,0:T(8,128)S(1)}, f32[104,256]{1,0:T(8,128)S(1)}, u32[]{:S(2)}, u32[]{:S(2)}) collective-permute-start(f32[104,256]{1,0:T(8,128)S(1)} %add.30), channel_id=1, source_target_pairs={{0,6},{1,25},{2,26},{3,5},{4,28},{5,3},{6,0},{7,31},{8,16},{9,15},... | collective-permute-start | bytes 319496 | tf_op jit(solution)/shard_map/ppermute | solution.py:257
  9.1 4.1 %collective-permute-start.2 = (f32[104,256]{1,0:T(8,128)S(1)}, f32[104,256]{1,0:T(8,128)S(1)}, u32[]{:S(2)}, u32[]{:S(2)}) collective-permute-start(f32[104,256]{1,0:T(8,128)S(1)} %add.30), channel_id=1, source_target_pairs={{0,5},{1,16},{2,19},{3,6},{4,21},{5,0},{6,3},{7,22},{8,25},{9,12},... | collective-permute-start | bytes 319496 | tf_op jit(solution)/shard_map/ppermute | solution.py:257
  9.2 4.1 %collective-permute-start.1 = (f32[104,256]{1,0:T(8,128)S(1)}, f32[104,256]{1,0:T(8,128)S(1)}, u32[]{:S(2)}, u32[]{:S(2)}) collective-permute-start(f32[104,256]{1,0:T(8,128)S(1)} %add.30), channel_id=1, source_target_pairs={{0,3},{1,8},{2,11},{3,0},{4,13},{5,6},{6,5},{7,14},{8,1},{9,10},{1... | collective-permute-start | bytes 319496 | tf_op jit(solution)/shard_map/ppermute | solution.py:257
  13.3 6.7 %collective-permute-start.6 = (f32[104,256]{1,0:T(8,128)S(1)}, f32[104,256]{1,0:T(8,128)S(1)}, u32[]{:S(2)}, u32[]{:S(2)}) collective-permute-start(f32[104,256]{1,0:T(8,128)S(1)} %add_add_fusion.1), channel_id=1, source_target_pairs={{0,24},{1,7},{2,4},{3,27},{4,2},{5,29},{6,30},{7,1},{8,14},{9,17},... | collective-permute-start | bytes 319496 | tf_op jit(solution)/shard_map/ppermute | solution.py:257
  17.1 5.8 %collective-permute-start.5 = (f32[104,256]{1,0:T(8,128)S(1)}, f32[104,256]{1,0:T(8,128)S(1)}, u32[]{:S(2)}, u32[]{:S(2)}) collective-permute-start(f32[104,256]{1,0:T(8,128)S(1)} %add_add_fusion.1), channel_id=1, source_target_pairs={{0,17},{1,4},{2,7},{3,18},{4,1},{5,20},{6,23},{7,2},{8,13},{9,24},... | collective-permute-start | bytes 319496 | tf_op jit(solution)/shard_map/ppermute | solution.py:257
  17.1 5.8 %collective-permute-start.4 = (f32[104,256]{1,0:T(8,128)S(1)}, f32[104,256]{1,0:T(8,128)S(1)}, u32[]{:S(2)}, u32[]{:S(2)}) collective-permute-start(f32[104,256]{1,0:T(8,128)S(1)} %add_add_fusion.1), channel_id=1, source_target_pairs={{0,9},{1,2},{2,1},{3,10},{4,7},{5,12},{6,15},{7,4},{8,11},{9,0},{1... | collective-permute-start | bytes 319496 | tf_op jit(solution)/shard_map/ppermute | solution.py:257
  23.0 1.4 %collective-permute-start.7 = (f32[104,256]{1,0:T(8,128)S(1)}, f32[104,256]{1,0:T(8,128)S(1)}, u32[]{:S(2)}, u32[]{:S(2)}) collective-permute-start(f32[104,256]{1,0:T(8,128)S(1)} %add_add_fusion.mine_ref), channel_id=1, source_target_pairs={{0,1},{1,0},{2,3},{3,2},{4,5},{5,4},{6,7},{7,6},{8,9},{9,8},{10,11... | collective-permute-start | bytes 319496 | tf_op jit(solution)/shard_map/ppermute | solution.py:257

commit v11 on v10

--- a/solution.py
+++ b/solution.py
@@ -103,13 +103,20 @@
     return -(-(order // 2 + probes + 1) // (2 * BLOCK)) * 2 * BLOCK
 
 
+def own_part():
+    bits = lax.axis_index("cells") ^ lax.axis_index("sub")
+    for shift in (16, 8, 4, 2, 1):
+        bits = bits ^ (bits >> shift)
+    return bits & 1
+
+
 def live_volumes(volumes_ref, live_ref, begin):
     ids = lax.broadcasted_iota(jnp.int32, (1, LANES), 1) + begin
     part = volumes_ref[pl.ds(begin, LANES)].reshape(1, LANES)
     return jnp.where(ids < live_ref[0], part, 0.0)
 
 
-def sums_kernel(total_rows, snapshots_hbm, volumes_hbm, live_ref, probes_hbm, part_ref, keep_ref, send_ref, scale_ref, snapshots_ref, volumes_ref, probes_ref, packed, sems):
+def sums_kernel(total_rows, snapshots_hbm, volumes_hbm, live_ref, probes_hbm, keep_ref, send_ref, scale_ref, snapshots_ref, volumes_ref, probes_ref, packed, sems):
     copies = [
         pltpu.make_async_copy(source, target, sems.at[i])
         for i, (source, target) in enumerate(
@@ -139,7 +146,7 @@
     probe_scaled = probes_ref[...] * (volume * (1.0 / total_rows**0.5))
     packed[half : half + probes, :] = product(probe_scaled, snapshots, ((1,), (0,)))
     middle = packed.shape[0] // 2
-    low = part_ref[0] == 0
+    low = own_part() == 0
 
     @pl.when(low)
     def _():
@@ -156,16 +163,15 @@
     return pltpu.with_memory_space_constraint(array, pltpu.HBM)
 
 
-def local_sums(total_rows, snapshots, volumes, live_rows, probes, part):
+def local_sums(total_rows, snapshots, volumes, live_rows, probes):
     order = snapshots.shape[1]
     size = packed_rows(order, probes.shape[0])
     hbm = pl.BlockSpec(memory_space=pltpu.HBM)
     whole = pl.BlockSpec(memory_space=pltpu.VMEM)
-    scalar = pl.BlockSpec(memory_space=pltpu.SMEM)
     return pl.pallas_call(
         functools.partial(sums_kernel, total_rows),
         out_shape=(jax.ShapeDtypeStruct((size // 2, order), F32),) * 2 + (jax.ShapeDtypeStruct((1, volumes.shape[0]), F32),),
-        in_specs=[hbm, hbm, scalar, hbm, scalar],
+        in_specs=[hbm, hbm, pl.BlockSpec(memory_space=pltpu.SMEM), hbm],
         out_specs=(whole, whole, whole),
         scratch_shapes=[
             pltpu.VMEM(snapshots.shape, F32),
@@ -175,7 +181,7 @@
             pltpu.SemaphoreType.DMA((3,)),
         ],
         compiler_params=pltpu.CompilerParams(vmem_limit_bytes=24 * 1024 * 1024),
-    )(hold(snapshots), hold(volumes), live_rows, hold(probes), part)
+    )(hold(snapshots), hold(volumes), live_rows, hold(probes))
 
 
 def weigh_kernel(snapshots_ref, scale_ref, weighted_ref):
@@ -198,11 +204,11 @@
     )(snapshots, scale)
 
 
-def finish_kernel(mine_ref, other_ref, weighted_ref, part_ref, basis_ref, factor_ref, coef_ref):
+def finish_kernel(mine_ref, other_ref, weighted_ref, basis_ref, factor_ref, coef_ref):
     order = weighted_ref.shape[1]
     probes = coef_ref.shape[0]
     half = order // 2
-    low = part_ref[0] == 0
+    low = own_part() == 0
     mine, other = mine_ref[...], other_ref[...]
     packed = jnp.concatenate([jnp.where(low, mine, other), jnp.where(low, other, mine)], axis=0)
     row_ids = lax.broadcasted_iota(jnp.int32, (half, half), 0)
@@ -235,7 +241,7 @@
     factor_ref[half:, half:] = jnp.where(in_upper, product(inverse_second, second, ((1,), (0,))), 0.0)
 
 
-def finish(mine, other, weighted, part, probes):
+def finish(mine, other, weighted, probes):
     row_count, order = weighted.shape
     whole = pl.BlockSpec(memory_space=pltpu.VMEM)
     return pl.pallas_call(
@@ -245,10 +251,10 @@
             jax.ShapeDtypeStruct((order, order), F32),
             jax.ShapeDtypeStruct((probes, order), F32),
         ),
-        in_specs=[whole] * 3 + [pl.BlockSpec(memory_space=pltpu.SMEM)],
+        in_specs=[whole] * 3,
         out_specs=(whole,) * 3,
         compiler_params=pltpu.CompilerParams(vmem_limit_bytes=32 * 1024 * 1024),
-    )(mine, other, weighted, part)
+    )(mine, other, weighted)
 
 
 def exchange(value, masks):
@@ -275,11 +281,9 @@
 
 def per_device(snapshots, volumes, live_rows, probes):
     count = lax.axis_size("cells") * lax.axis_size("sub")
-    index = lax.axis_index("cells") * lax.axis_size("sub") + lax.axis_index("sub")
-    part = (lax.population_count(index.astype(jnp.int32)) % 2).reshape(1)
-    keep, send, scale = local_sums(snapshots.shape[0] * count, snapshots, volumes, live_rows, probes, part)
+    keep, send, scale = local_sums(snapshots.shape[0] * count, snapshots, volumes, live_rows, probes)
     mine, other = reduce_halves(keep, send)
-    return finish(mine, other, weigh(snapshots, scale), part, probes.shape[0])
+    return finish(mine, other, weigh(snapshots, scale), probes.shape[0])
 
 
 def solution(mesh):

time: 32 us -> 31.9 us (level)
  no operation moved by 1% of the time
where the time goes in v11:
time: 31.9 us; the launch traced here: 31.7 us
  waiting for transfers between devices  11.2 us (35%)
  Pallas kernels  9.96 us (31%)
  starting transfers between devices  9.12 us (29%)
  between operations  1.32 us (4%)
    ppermute x8, waiting for transfers between devices, exchange(): return lax.ppermute(value, ('cells', 'sub'), pairs)  11.2 us
    ppermute x8, starting transfers between devices, exchange(): return lax.ppermute(value, ('cells', 'sub'), pairs)  9.12 us
    pallas_call x1, Pallas kernels, finish(): pl.pallas_call(finish_kernel, out_shape=(jax.ShapeDtypeStruct((row_count,...  7.36 us
    pallas_call x1, Pallas kernels, local_sums(): pl.pallas_call(functools.partial(sums_kernel, total_rows), out_shape=(jax...  2.47 us
  transfers between devices with their start and end apart: 8, of which 6 were waited for; matrix products, arithmetic and copies ran while one was open for 0% of the time, Pallas kernels for 0%

profile of v11, /device:TPU:0, one launch (start us, length us, event | category | flops | bytes accessed | tf_op | source)
XLA Modules:
  0.0 31.7 jit_solution(8091301964824035458)
XLA Ops:
  1.3 2.5 %shard_map.67 = (f32[104,256]{1,0:T(8,128)S(1)}, f32[104,256]{1,0:T(8,128)S(1)}, f32[1,512]{1,0:T(1,128)S(1)}) custom-call(f32[512,256]{1,0:T(8,128)} %snapshots_ref.1, f32[512]{0:T(512)} %volumes_hbm.1, s32[1]{0:T(128)S(6)} %copy.7.live_ref, f32[64,512]{1,0:T(8,128)} %probes_hbm.1), custom_call_target="tpu_custom_call" | custom-call | tf_op jit(solution)/shard_map/pallas_call | solution.py:171
  3.8 0.5 %collective-permute-start = (f32[104,256]{1,0:T(8,128)S(1)}, f32[104,256]{1,0:T(8,128)S(1)}, u32[]{:S(2)}, u32[]{:S(2)}) collective-permute-start(f32[104,256]{1,0:T(8,128)S(1)} %get-tuple-element.7), channel_id=1, source_target_pairs={{0,1},{1,0},{2,3},{3,2},{4,5},{5,4},{6,7},{7,6},{8,9},{9,8},{10,11... | collective-permute-start | bytes 319496 | tf_op jit(solution)/shard_map/ppermute | solution.py:263
  4.3 1.0 %collective-permute-done = f32[104,256]{1,0:T(8,128)S(1)} collective-permute-done((f32[104,256]{1,0:T(8,128)S(1)}, f32[104,256]{1,0:T(8,128)S(1)}, u32[]{:S(2)}, u32[]{:S(2)}) %collective-permute-start) | collective-permute-done | bytes 106528 | tf_op jit(solution)/shard_map/ppermute | solution.py:263
  5.3 0.0 copy-start
  5.3 3.9 %collective-permute-start.3 = (f32[104,256]{1,0:T(8,128)S(1)}, f32[104,256]{1,0:T(8,128)S(1)}, u32[]{:S(2)}, u32[]{:S(2)}) collective-permute-start(f32[104,256]{1,0:T(8,128)S(1)} %add.21), channel_id=1, source_target_pairs={{0,6},{1,25},{2,26},{3,5},{4,28},{5,3},{6,0},{7,31},{8,16},{9,15},... | collective-permute-start | bytes 319496 | tf_op jit(solution)/shard_map/ppermute | solution.py:263
  9.1 0.0 collective-permute-start.2
  9.1 0.4 %collective-permute-start.1 = (f32[104,256]{1,0:T(8,128)S(1)}, f32[104,256]{1,0:T(8,128)S(1)}, u32[]{:S(2)}, u32[]{:S(2)}) collective-permute-start(f32[104,256]{1,0:T(8,128)S(1)} %add.21), channel_id=1, source_target_pairs={{0,3},{1,8},{2,11},{3,0},{4,13},{5,6},{6,5},{7,14},{8,1},{9,10},{1... | collective-permute-start | bytes 319496 | tf_op jit(solution)/shard_map/ppermute | solution.py:263
  9.5 2.3 %collective-permute-done.3 = f32[104,256]{1,0:T(8,128)S(1)} collective-permute-done((f32[104,256]{1,0:T(8,128)S(1)}, f32[104,256]{1,0:T(8,128)S(1)}, u32[]{:S(2)}, u32[]{:S(2)}) %collective-permute-start.3) | collective-permute-done | bytes 106528 | tf_op jit(solution)/shard_map/ppermute | solution.py:263
  11.8 1.4 %collective-permute-done.2 = f32[104,256]{1,0:T(8,128)S(1)} collective-permute-done((f32[104,256]{1,0:T(8,128)S(1)}, f32[104,256]{1,0:T(8,128)S(1)}, u32[]{:S(2)}, u32[]{:S(2)}) %collective-permute-start.2) | collective-permute-done | bytes 106528 | tf_op jit(solution)/shard_map/ppermute | solution.py:263
  13.3 0.0 collective-permute-done.1
  13.3 3.8 %collective-permute-start.6 = (f32[104,256]{1,0:T(8,128)S(1)}, f32[104,256]{1,0:T(8,128)S(1)}, u32[]{:S(2)}, u32[]{:S(2)}) collective-permute-start(f32[104,256]{1,0:T(8,128)S(1)} %add_add_fusion.1), channel_id=1, source_target_pairs={{0,24},{1,7},{2,4},{3,27},{4,2},{5,29},{6,30},{7,1},{8,14},{9,17},... | collective-permute-start | bytes 319496 | tf_op jit(solution)/shard_map/ppermute | solution.py:263
  17.1 0.0 collective-permute-start.5
  17.1 0.4 %collective-permute-start.4 = (f32[104,256]{1,0:T(8,128)S(1)}, f32[104,256]{1,0:T(8,128)S(1)}, u32[]{:S(2)}, u32[]{:S(2)}) collective-permute-start(f32[104,256]{1,0:T(8,128)S(1)} %add_add_fusion.1), channel_id=1, source_target_pairs={{0,9},{1,2},{2,1},{3,10},{4,7},{5,12},{6,15},{7,4},{8,11},{9,0},{1... | collective-permute-start | bytes 319496 | tf_op jit(solution)/shard_map/ppermute | solution.py:263
  17.5 2.5 %collective-permute-done.6 = f32[104,256]{1,0:T(8,128)S(1)} collective-permute-done((f32[104,256]{1,0:T(8,128)S(1)}, f32[104,256]{1,0:T(8,128)S(1)}, u32[]{:S(2)}, u32[]{:S(2)}) %collective-permute-start.6) | collective-permute-done | bytes 106528 | tf_op jit(solution)/shard_map/ppermute | solution.py:263
  20.0 3.0 %collective-permute-done.5 = f32[104,256]{1,0:T(8,128)S(1)} collective-permute-done((f32[104,256]{1,0:T(8,128)S(1)}, f32[104,256]{1,0:T(8,128)S(1)}, u32[]{:S(2)}, u32[]{:S(2)}) %collective-permute-start.5) | collective-permute-done | bytes 106528 | tf_op jit(solution)/shard_map/ppermute | solution.py:263
  22.9 0.0 collective-permute-done.4
  23.0 0.2 collective-permute-start.7
  23.1 0.0 copy-done
  23.1 0.1 shard_map.68.weighted_ref
  23.3 1.1 %collective-permute-done.7.other_ref = f32[104,256]{1,0:T(8,128)S(1)} collective-permute-done((f32[104,256]{1,0:T(8,128)S(1)}, f32[104,256]{1,0:T(8,128)S(1)}, u32[]{:S(2)}, u32[]{:S(2)}) %collective-permute-start.7) | collective-permute-done | bytes 106528 | tf_op jit(solution)/shard_map/ppermute | solution.py:263
  24.3 7.4 %shard_map.69 = (f32[512,256]{1,0:T(8,128)}, f32[256,256]{1,0:T(8,128)}, f32[64,256]{1,0:T(8,128)}) custom-call(f32[104,256]{1,0:T(8,128)S(1)} %add_add_fusion.mine_ref, f32[104,256]{1,0:T(8,128)S(1)} %collective-permute-done.7.other_ref, f32[512,256]{1,0:T(8,128)S(1)} %shard_map.68.weighted_ref), custom_call_target="tpu_custom_call" | custom-call | tf_op jit(solution)/shard_map/pallas_call | solution.py:247
  (3 shorter events, 0.1 us)
Async XLA Ops:
  3.8 1.5 %collective-permute-start = (f32[104,256]{1,0:T(8,128)S(1)}, f32[104,256]{1,0:T(8,128)S(1)}, u32[]{:S(2)}, u32[]{:S(2)}) collective-permute-start(f32[104,256]{1,0:T(8,128)S(1)} %get-tuple-element.7), channel_id=1, source_target_pairs={{0,1},{1,0},{2,3},{3,2},{4,5},{5,4},{6,7},{7,6},{8,9},{9,8},{10,11... | collective-permute-start | bytes 319496 | tf_op jit(solution)/shard_map/ppermute | solution.py:263
  5.3 17.9 %copy-start = (f32[512,256]{1,0:T(8,128)S(1)}, f32[512,256]{1,0:T(8,128)}, u32[]{:S(2)}) copy-start(f32[512,256]{1,0:T(8,128)} %snapshots_ref.1) | copy-start | bytes 1572868
  5.3 6.5 %collective-permute-start.3 = (f32[104,256]{1,0:T(8,128)S(1)}, f32[104,256]{1,0:T(8,128)S(1)}, u32[]{:S(2)}, u32[]{:S(2)}) collective-permute-start(f32[104,256]{1,0:T(8,128)S(1)} %add.21), channel_id=1, source_target_pairs={{0,6},{1,25},{2,26},{3,5},{4,28},{5,3},{6,0},{7,31},{8,16},{9,15},... | collective-permute-start | bytes 319496 | tf_op jit(solution)/shard_map/ppermute | solution.py:263
  9.1 4.1 %collective-permute-start.2 = (f32[104,256]{1,0:T(8,128)S(1)}, f32[104,256]{1,0:T(8,128)S(1)}, u32[]{:S(2)}, u32[]{:S(2)}) collective-permute-start(f32[104,256]{1,0:T(8,128)S(1)} %add.21), channel_id=1, source_target_pairs={{0,5},{1,16},{2,19},{3,6},{4,21},{5,0},{6,3},{7,22},{8,25},{9,12},... | collective-permute-start | bytes 319496 | tf_op jit(solution)/shard_map/ppermute | solution.py:263
  9.1 4.1 %collective-permute-start.1 = (f32[104,256]{1,0:T(8,128)S(1)}, f32[104,256]{1,0:T(8,128)S(1)}, u32[]{:S(2)}, u32[]{:S(2)}) collective-permute-start(f32[104,256]{1,0:T(8,128)S(1)} %add.21), channel_id=1, source_target_pairs={{0,3},{1,8},{2,11},{3,0},{4,13},{5,6},{6,5},{7,14},{8,1},{9,10},{1... | collective-permute-start | bytes 319496 | tf_op jit(solution)/shard_map/ppermute | solution.py:263
  13.3 6.7 %collective-permute-start.6 = (f32[104,256]{1,0:T(8,128)S(1)}, f32[104,256]{1,0:T(8,128)S(1)}, u32[]{:S(2)}, u32[]{:S(2)}) collective-permute-start(f32[104,256]{1,0:T(8,128)S(1)} %add_add_fusion.1), channel_id=1, source_target_pairs={{0,24},{1,7},{2,4},{3,27},{4,2},{5,29},{6,30},{7,1},{8,14},{9,17},... | collective-permute-start | bytes 319496 | tf_op jit(solution)/shard_map/ppermute | solution.py:263
  17.1 5.8 %collective-permute-start.5 = (f32[104,256]{1,0:T(8,128)S(1)}, f32[104,256]{1,0:T(8,128)S(1)}, u32[]{:S(2)}, u32[]{:S(2)}) collective-permute-start(f32[104,256]{1,0:T(8,128)S(1)} %add_add_fusion.1), channel_id=1, source_target_pairs={{0,17},{1,4},{2,7},{3,18},{4,1},{5,20},{6,23},{7,2},{8,13},{9,24},... | collective-permute-start | bytes 319496 | tf_op jit(solution)/shard_map/ppermute | solution.py:263
  17.1 5.8 %collective-permute-start.4 = (f32[104,256]{1,0:T(8,128)S(1)}, f32[104,256]{1,0:T(8,128)S(1)}, u32[]{:S(2)}, u32[]{:S(2)}) collective-permute-start(f32[104,256]{1,0:T(8,128)S(1)} %add_add_fusion.1), channel_id=1, source_target_pairs={{0,9},{1,2},{2,1},{3,10},{4,7},{5,12},{6,15},{7,4},{8,11},{9,0},{1... | collective-permute-start | bytes 319496 | tf_op jit(solution)/shard_map/ppermute | solution.py:263
  23.0 1.4 %collective-permute-start.7 = (f32[104,256]{1,0:T(8,128)S(1)}, f32[104,256]{1,0:T(8,128)S(1)}, u32[]{:S(2)}, u32[]{:S(2)}) collective-permute-start(f32[104,256]{1,0:T(8,128)S(1)} %add_add_fusion.mine_ref), channel_id=1, source_target_pairs={{0,1},{1,0},{2,3},{3,2},{4,5},{5,4},{6,7},{7,6},{8,9},{9,8},{10,11... | collective-permute-start | bytes 319496 | tf_op jit(solution)/shard_map/ppermute | solution.py:263

commit v12 on v11

--- a/solution.py
+++ b/solution.py
@@ -117,24 +117,27 @@
 
 
 def sums_kernel(total_rows, snapshots_hbm, volumes_hbm, live_ref, probes_hbm, keep_ref, send_ref, scale_ref, snapshots_ref, volumes_ref, probes_ref, packed, sems):
-    copies = [
-        pltpu.make_async_copy(source, target, sems.at[i])
-        for i, (source, target) in enumerate(
-            ((volumes_hbm, volumes_ref), (snapshots_hbm, snapshots_ref), (probes_hbm, probes_ref))
-        )
-    ]
+    row_count, order = snapshots_ref.shape
+    parts = [pl.ds(begin, LANES) for begin in range(0, row_count, LANES)]
+    transfers = [(volumes_hbm, volumes_ref), *((snapshots_hbm.at[rows], snapshots_ref.at[rows]) for rows in parts)]
+    transfers.append((probes_hbm, probes_ref))
+    copies = [pltpu.make_async_copy(source, target, sems.at[i]) for i, (source, target) in enumerate(transfers)]
     for copy in copies:
         copy.start()
-    row_count, order = snapshots_ref.shape
     probes = probes_ref.shape[0]
     half = order // 2
     copies[0].wait()
     volume = jnp.concatenate([live_volumes(volumes_ref, live_ref, b) for b in range(0, row_count, LANES)], axis=1)
     scale_ref[...] = jnp.sqrt(volume)
-    copies[1].wait()
-    snapshots = snapshots_ref[...]
-    scaled = snapshots.T * (volume * (1.0 / total_rows))
-    gram = product(scaled, snapshots, ((1,), (0,)))
+    weight = volume * (1.0 / total_rows)
+    gram = jnp.zeros((order, order), F32)
+    group = 2
+    for begin in range(0, len(parts), group):
+        for copy in copies[1 + begin : 1 + min(begin + group, len(parts))]:
+            copy.wait()
+        rows = slice(begin * LANES, min((begin + group) * LANES, row_count))
+        block = snapshots_ref[rows, :]
+        gram = gram + product(block.T * weight[:, rows], block, ((1,), (0,)))
     row_ids = lax.broadcasted_iota(jnp.int32, (half, half), 0)
     column_ids = lax.broadcasted_iota(jnp.int32, (half, half), 1)
     packed[:half, :half] = jnp.where(row_ids <= column_ids, gram[:half, :half], gram[half:, half:])
@@ -142,9 +145,9 @@
     rest = packed.shape[0] - half - probes
     diagonal = jnp.sum(jnp.where(row_ids == column_ids, gram[half:, half:], 0.0), axis=0, keepdims=True)
     packed[half + probes :, :] = jnp.concatenate([jnp.broadcast_to(diagonal, (rest, half))] * 2, axis=1)
-    copies[2].wait()
+    copies[-1].wait()
     probe_scaled = probes_ref[...] * (volume * (1.0 / total_rows**0.5))
-    packed[half : half + probes, :] = product(probe_scaled, snapshots, ((1,), (0,)))
+    packed[half : half + probes, :] = product(probe_scaled, snapshots_ref[...], ((1,), (0,)))
     middle = packed.shape[0] // 2
     low = own_part() == 0
 
@@ -178,7 +181,7 @@
             pltpu.VMEM(volumes.shape, F32),
             pltpu.VMEM(probes.shape, F32),
             pltpu.VMEM((size, order), F32),
-            pltpu.SemaphoreType.DMA((3,)),
+            pltpu.SemaphoreType.DMA((2 + snapshots.shape[0] // LANES,)),
         ],
         compiler_params=pltpu.CompilerParams(vmem_limit_bytes=24 * 1024 * 1024),
     )(hold(snapshots), hold(volumes), live_rows, hold(probes))
@@ -204,10 +207,17 @@
     )(snapshots, scale)
 
 
-def finish_kernel(mine_ref, other_ref, weighted_ref, basis_ref, factor_ref, coef_ref):
-    order = weighted_ref.shape[1]
+def finish_kernel(mine_ref, other_ref, weighted_ref, basis_hbm, factor_hbm, coef_hbm, basis_ref, factor_ref, coef_ref, sems):
+    row_count, order = weighted_ref.shape
     probes = coef_ref.shape[0]
     half = order // 2
+    copies = []
+
+    def write(source, target, rows, columns):
+        copy = pltpu.make_async_copy(source.at[rows, columns], target.at[rows, columns], sems.at[len(copies)])
+        copy.start()
+        copies.append(copy)
+
     low = own_part() == 0
     mine, other = mine_ref[...], other_ref[...]
     packed = jnp.concatenate([jnp.where(low, mine, other), jnp.where(low, other, mine)], axis=0)
@@ -227,32 +237,41 @@
     factor_ref[:half, :half] = jnp.where(in_upper, product(inverse, first, ((1,), (0,))), 0.0)
     factor_ref[:half, half:] = beside
     factor_ref[half:, :half] = jnp.zeros((half, half), F32)
-
+    left = product(weighted_ref[:, :half], inverse, ((1,), (1,)))
+    basis_ref[:, :half] = left
+    write(basis_ref, basis_hbm, pl.ds(0, row_count), pl.ds(0, half))
+    write(factor_ref, factor_hbm, pl.ds(0, half), pl.ds(0, order))
+    rest = weighted_ref[:, half:] - product(left, beside, ((1,), (0,)))
     left = product(cross[:, :half], inverse, ((1,), (1,)))
     coef_ref[:, :half] = left
     cross_rest = cross[:, half:] - product(left, beside, ((1,), (0,)))
-    left = product(weighted_ref[:, :half], inverse, ((1,), (1,)))
-    basis_ref[:, :half] = left
-    rest = weighted_ref[:, half:] - product(left, beside, ((1,), (0,)))
 
     inverse_second = eliminate(second)
+    for begin in range(0, row_count, LANES):
+        rows = pl.ds(begin, LANES)
+        basis_ref[rows, half:] = product(rest[begin : begin + LANES, :], inverse_second, ((1,), (1,)))
+        write(basis_ref, basis_hbm, rows, pl.ds(half, half))
+    factor_ref[half:, half:] = jnp.where(in_upper, product(inverse_second, second, ((1,), (0,))), 0.0)
+    write(factor_ref, factor_hbm, pl.ds(half, half), pl.ds(0, order))
     coef_ref[:, half:] = product(cross_rest, inverse_second, ((1,), (1,)))
-    basis_ref[:, half:] = product(rest, inverse_second, ((1,), (1,)))
-    factor_ref[half:, half:] = jnp.where(in_upper, product(inverse_second, second, ((1,), (0,))), 0.0)
+    write(coef_ref, coef_hbm, pl.ds(0, probes), pl.ds(0, order))
+    for copy in copies:
+        copy.wait()
 
 
 def finish(mine, other, weighted, probes):
     row_count, order = weighted.shape
     whole = pl.BlockSpec(memory_space=pltpu.VMEM)
+    shapes = (row_count, order), (order, order), (probes, order)
     return pl.pallas_call(
         finish_kernel,
-        out_shape=(
-            jax.ShapeDtypeStruct((row_count, order), F32),
-            jax.ShapeDtypeStruct((order, order), F32),
-            jax.ShapeDtypeStruct((probes, order), F32),
-        ),
+        out_shape=tuple(jax.ShapeDtypeStruct(shape, F32) for shape in shapes),
         in_specs=[whole] * 3,
-        out_specs=(whole,) * 3,
+        out_specs=(pl.BlockSpec(memory_space=pltpu.HBM),) * 3,
+        scratch_shapes=[
+            *(pltpu.VMEM(shape, F32) for shape in shapes),
+            pltpu.SemaphoreType.DMA((row_count // LANES + 4,)),
+        ],
         compiler_params=pltpu.CompilerParams(vmem_limit_bytes=32 * 1024 * 1024),
     )(mine, other, weighted)
 

time: 31.9 us -> 32.2 us (level)
  Pallas kernels: 9.96 us -> 10.3 us
where the time goes in v12:
time: 32.2 us; the launch traced here: 32 us
  waiting for transfers between devices  11.2 us (35%)
  Pallas kernels  10.3 us (32%)
  starting transfers between devices  9.12 us (28%)
  between operations  1.32 us (4%)
    ppermute x8, waiting for transfers between devices, exchange(): return lax.ppermute(value, ('cells', 'sub'), pairs)  11.2 us
    ppermute x8, starting transfers between devices, exchange(): return lax.ppermute(value, ('cells', 'sub'), pairs)  9.12 us
    pallas_call x1, Pallas kernels, finish(): pl.pallas_call(finish_kernel, out_shape=tuple((jax.ShapeDtypeStruct(shape...  7.57 us
    pallas_call x1, Pallas kernels, local_sums(): pl.pallas_call(functools.partial(sums_kernel, total_rows), out_shape=(jax...  2.58 us
  transfers between devices with their start and end apart: 8, of which 6 were waited for; matrix products, arithmetic and copies ran while one was open for 0% of the time, Pallas kernels for 0%

profile of v12, /device:TPU:0, one launch (start us, length us, event | category | flops | bytes accessed | tf_op | source)
XLA Modules:
  0.0 32.0 jit_solution(12076377498966791291)
XLA Ops:
  1.3 2.6 %shard_map.67 = (f32[104,256]{1,0:T(8,128)S(1)}, f32[104,256]{1,0:T(8,128)S(1)}, f32[1,512]{1,0:T(1,128)S(1)}) custom-call(f32[512,256]{1,0:T(8,128)} %snapshots_ref.1, f32[512]{0:T(512)} %volumes_hbm.1, s32[1]{0:T(128)S(6)} %copy.7.live_ref, f32[64,512]{1,0:T(8,128)} %probes_hbm.1), custom_call_target="tpu_custom_call" | custom-call | tf_op jit(solution)/shard_map/pallas_call | solution.py:174
  3.9 0.5 %collective-permute-start = (f32[104,256]{1,0:T(8,128)S(1)}, f32[104,256]{1,0:T(8,128)S(1)}, u32[]{:S(2)}, u32[]{:S(2)}) collective-permute-start(f32[104,256]{1,0:T(8,128)S(1)} %get-tuple-element.7), channel_id=1, source_target_pairs={{0,1},{1,0},{2,3},{3,2},{4,5},{5,4},{6,7},{7,6},{8,9},{9,8},{10,11... | collective-permute-start | bytes 319496 | tf_op jit(solution)/shard_map/ppermute | solution.py:282
  4.4 1.0 %collective-permute-done = f32[104,256]{1,0:T(8,128)S(1)} collective-permute-done((f32[104,256]{1,0:T(8,128)S(1)}, f32[104,256]{1,0:T(8,128)S(1)}, u32[]{:S(2)}, u32[]{:S(2)}) %collective-permute-start) | collective-permute-done | bytes 106528 | tf_op jit(solution)/shard_map/ppermute | solution.py:282
  5.4 0.0 copy-start
  5.4 3.9 %collective-permute-start.3 = (f32[104,256]{1,0:T(8,128)S(1)}, f32[104,256]{1,0:T(8,128)S(1)}, u32[]{:S(2)}, u32[]{:S(2)}) collective-permute-start(f32[104,256]{1,0:T(8,128)S(1)} %add.21), channel_id=1, source_target_pairs={{0,6},{1,25},{2,26},{3,5},{4,28},{5,3},{6,0},{7,31},{8,16},{9,15},... | collective-permute-start | bytes 319496 | tf_op jit(solution)/shard_map/ppermute | solution.py:282
  9.2 0.0 collective-permute-start.2
  9.2 0.4 %collective-permute-start.1 = (f32[104,256]{1,0:T(8,128)S(1)}, f32[104,256]{1,0:T(8,128)S(1)}, u32[]{:S(2)}, u32[]{:S(2)}) collective-permute-start(f32[104,256]{1,0:T(8,128)S(1)} %add.21), channel_id=1, source_target_pairs={{0,3},{1,8},{2,11},{3,0},{4,13},{5,6},{6,5},{7,14},{8,1},{9,10},{1... | collective-permute-start | bytes 319496 | tf_op jit(solution)/shard_map/ppermute | solution.py:282
  9.6 2.3 %collective-permute-done.3 = f32[104,256]{1,0:T(8,128)S(1)} collective-permute-done((f32[104,256]{1,0:T(8,128)S(1)}, f32[104,256]{1,0:T(8,128)S(1)}, u32[]{:S(2)}, u32[]{:S(2)}) %collective-permute-start.3) | collective-permute-done | bytes 106528 | tf_op jit(solution)/shard_map/ppermute | solution.py:282
  11.9 1.4 %collective-permute-done.2 = f32[104,256]{1,0:T(8,128)S(1)} collective-permute-done((f32[104,256]{1,0:T(8,128)S(1)}, f32[104,256]{1,0:T(8,128)S(1)}, u32[]{:S(2)}, u32[]{:S(2)}) %collective-permute-start.2) | collective-permute-done | bytes 106528 | tf_op jit(solution)/shard_map/ppermute | solution.py:282
  13.4 0.0 collective-permute-done.1
  13.4 3.8 %collective-permute-start.6 = (f32[104,256]{1,0:T(8,128)S(1)}, f32[104,256]{1,0:T(8,128)S(1)}, u32[]{:S(2)}, u32[]{:S(2)}) collective-permute-start(f32[104,256]{1,0:T(8,128)S(1)} %add_add_fusion.1), channel_id=1, source_target_pairs={{0,24},{1,7},{2,4},{3,27},{4,2},{5,29},{6,30},{7,1},{8,14},{9,17},... | collective-permute-start | bytes 319496 | tf_op jit(solution)/shard_map/ppermute | solution.py:282
  17.2 0.0 collective-permute-start.5
  17.2 0.4 %collective-permute-start.4 = (f32[104,256]{1,0:T(8,128)S(1)}, f32[104,256]{1,0:T(8,128)S(1)}, u32[]{:S(2)}, u32[]{:S(2)}) collective-permute-start(f32[104,256]{1,0:T(8,128)S(1)} %add_add_fusion.1), channel_id=1, source_target_pairs={{0,9},{1,2},{2,1},{3,10},{4,7},{5,12},{6,15},{7,4},{8,11},{9,0},{1... | collective-permute-start | bytes 319496 | tf_op jit(solution)/shard_map/ppermute | solution.py:282
  17.6 2.5 %collective-permute-done.6 = f32[104,256]{1,0:T(8,128)S(1)} collective-permute-done((f32[104,256]{1,0:T(8,128)S(1)}, f32[104,256]{1,0:T(8,128)S(1)}, u32[]{:S(2)}, u32[]{:S(2)}) %collective-permute-start.6) | collective-permute-done | bytes 106528 | tf_op jit(solution)/shard_map/ppermute | solution.py:282
  20.1 3.0 %collective-permute-done.5 = f32[104,256]{1,0:T(8,128)S(1)} collective-permute-done((f32[104,256]{1,0:T(8,128)S(1)}, f32[104,256]{1,0:T(8,128)S(1)}, u32[]{:S(2)}, u32[]{:S(2)}) %collective-permute-start.5) | collective-permute-done | bytes 106528 | tf_op jit(solution)/shard_map/ppermute | solution.py:282
  23.0 0.0 collective-permute-done.4
  23.1 0.2 collective-permute-start.7
  23.2 0.0 copy-done
  23.2 0.1 shard_map.68.weighted_ref
  23.4 1.1 %collective-permute-done.7.other_ref = f32[104,256]{1,0:T(8,128)S(1)} collective-permute-done((f32[104,256]{1,0:T(8,128)S(1)}, f32[104,256]{1,0:T(8,128)S(1)}, u32[]{:S(2)}, u32[]{:S(2)}) %collective-permute-start.7) | collective-permute-done | bytes 106528 | tf_op jit(solution)/shard_map/ppermute | solution.py:282
  24.4 7.6 %shard_map.69 = (f32[512,256]{1,0:T(8,128)}, f32[256,256]{1,0:T(8,128)}, f32[64,256]{1,0:T(8,128)}) custom-call(f32[104,256]{1,0:T(8,128)S(1)} %add_add_fusion.mine_ref, f32[104,256]{1,0:T(8,128)S(1)} %collective-permute-done.7.other_ref, f32[512,256]{1,0:T(8,128)S(1)} %shard_map.68.weighted_ref), custom_call_target="tpu_custom_call" | custom-call | tf_op jit(solution)/shard_map/pallas_call | solution.py:266
  (3 shorter events, 0.1 us)
Async XLA Ops:
  3.9 1.5 %collective-permute-start = (f32[104,256]{1,0:T(8,128)S(1)}, f32[104,256]{1,0:T(8,128)S(1)}, u32[]{:S(2)}, u32[]{:S(2)}) collective-permute-start(f32[104,256]{1,0:T(8,128)S(1)} %get-tuple-element.7), channel_id=1, source_target_pairs={{0,1},{1,0},{2,3},{3,2},{4,5},{5,4},{6,7},{7,6},{8,9},{9,8},{10,11... | collective-permute-start | bytes 319496 | tf_op jit(solution)/shard_map/ppermute | solution.py:282
  5.4 17.9 %copy-start = (f32[512,256]{1,0:T(8,128)S(1)}, f32[512,256]{1,0:T(8,128)}, u32[]{:S(2)}) copy-start(f32[512,256]{1,0:T(8,128)} %snapshots_ref.1) | copy-start | bytes 1572868
  5.4 6.5 %collective-permute-start.3 = (f32[104,256]{1,0:T(8,128)S(1)}, f32[104,256]{1,0:T(8,128)S(1)}, u32[]{:S(2)}, u32[]{:S(2)}) collective-permute-start(f32[104,256]{1,0:T(8,128)S(1)} %add.21), channel_id=1, source_target_pairs={{0,6},{1,25},{2,26},{3,5},{4,28},{5,3},{6,0},{7,31},{8,16},{9,15},... | collective-permute-start | bytes 319496 | tf_op jit(solution)/shard_map/ppermute | solution.py:282
  9.2 4.1 %collective-permute-start.2 = (f32[104,256]{1,0:T(8,128)S(1)}, f32[104,256]{1,0:T(8,128)S(1)}, u32[]{:S(2)}, u32[]{:S(2)}) collective-permute-start(f32[104,256]{1,0:T(8,128)S(1)} %add.21), channel_id=1, source_target_pairs={{0,5},{1,16},{2,19},{3,6},{4,21},{5,0},{6,3},{7,22},{8,25},{9,12},... | collective-permute-start | bytes 319496 | tf_op jit(solution)/shard_map/ppermute | solution.py:282
  9.2 4.1 %collective-permute-start.1 = (f32[104,256]{1,0:T(8,128)S(1)}, f32[104,256]{1,0:T(8,128)S(1)}, u32[]{:S(2)}, u32[]{:S(2)}) collective-permute-start(f32[104,256]{1,0:T(8,128)S(1)} %add.21), channel_id=1, source_target_pairs={{0,3},{1,8},{2,11},{3,0},{4,13},{5,6},{6,5},{7,14},{8,1},{9,10},{1... | collective-permute-start | bytes 319496 | tf_op jit(solution)/shard_map/ppermute | solution.py:282
  13.4 6.7 %collective-permute-start.6 = (f32[104,256]{1,0:T(8,128)S(1)}, f32[104,256]{1,0:T(8,128)S(1)}, u32[]{:S(2)}, u32[]{:S(2)}) collective-permute-start(f32[104,256]{1,0:T(8,128)S(1)} %add_add_fusion.1), channel_id=1, source_target_pairs={{0,24},{1,7},{2,4},{3,27},{4,2},{5,29},{6,30},{7,1},{8,14},{9,17},... | collective-permute-start | bytes 319496 | tf_op jit(solution)/shard_map/ppermute | solution.py:282
  17.2 5.8 %collective-permute-start.5 = (f32[104,256]{1,0:T(8,128)S(1)}, f32[104,256]{1,0:T(8,128)S(1)}, u32[]{:S(2)}, u32[]{:S(2)}) collective-permute-start(f32[104,256]{1,0:T(8,128)S(1)} %add_add_fusion.1), channel_id=1, source_target_pairs={{0,17},{1,4},{2,7},{3,18},{4,1},{5,20},{6,23},{7,2},{8,13},{9,24},... | collective-permute-start | bytes 319496 | tf_op jit(solution)/shard_map/ppermute | solution.py:282
  17.2 5.8 %collective-permute-start.4 = (f32[104,256]{1,0:T(8,128)S(1)}, f32[104,256]{1,0:T(8,128)S(1)}, u32[]{:S(2)}, u32[]{:S(2)}) collective-permute-start(f32[104,256]{1,0:T(8,128)S(1)} %add_add_fusion.1), channel_id=1, source_target_pairs={{0,9},{1,2},{2,1},{3,10},{4,7},{5,12},{6,15},{7,4},{8,11},{9,0},{1... | collective-permute-start | bytes 319496 | tf_op jit(solution)/shard_map/ppermute | solution.py:282
  23.1 1.4 %collective-permute-start.7 = (f32[104,256]{1,0:T(8,128)S(1)}, f32[104,256]{1,0:T(8,128)S(1)}, u32[]{:S(2)}, u32[]{:S(2)}) collective-permute-start(f32[104,256]{1,0:T(8,128)S(1)} %add_add_fusion.mine_ref), channel_id=1, source_target_pairs={{0,1},{1,0},{2,3},{3,2},{4,5},{5,4},{6,7},{7,6},{8,9},{9,8},{10,11... | collective-permute-start | bytes 319496 | tf_op jit(solution)/shard_map/ppermute | solution.py:282

commit v13 on v11

--- a/solution.py
+++ b/solution.py
@@ -103,8 +103,19 @@
     return -(-(order // 2 + probes + 1) // (2 * BLOCK)) * 2 * BLOCK
 
 
+def chip_bits():
+    count = lax.axis_size("cells") * lax.axis_size("sub")
+    bits = [1 << k for k in range(1, count.bit_length() - 1)]
+    whole = len(bits) // 2 * 2
+    return [bits[k : k + 2] for k in range(0, whole, 2)], bits[whole:]
+
+
+def part_mask():
+    return 1 + sum(pair[0] for pair in chip_bits()[0])
+
+
 def own_part():
-    bits = lax.axis_index("cells") ^ lax.axis_index("sub")
+    bits = (lax.axis_index("cells") * lax.axis_size("sub") + lax.axis_index("sub")) & part_mask()
     for shift in (16, 8, 4, 2, 1):
         bits = bits ^ (bits >> shift)
     return bits & 1
@@ -259,23 +270,21 @@
 
 def exchange(value, masks):
     count = lax.axis_size("cells") * lax.axis_size("sub")
-    pairs = [(i, i ^ masks[bin(i).count("1") % 2]) for i in range(count)]
+    pairs = [(i, i ^ masks[bin(i & part_mask()).count("1") % 2]) for i in range(count)]
     return lax.ppermute(value, ("cells", "sub"), pairs)
 
 
 def reduce_halves(keep, send):
-    count = lax.axis_size("cells") * lax.axis_size("sub")
-    bits = [1 << k for k in range(1, count.bit_length() - 1)]
-    phases = [bits[k : k + 2] for k in range(0, len(bits) - 1, 2)]
+    phases, single = chip_bits()
     split = len(phases) // 2
     mine = keep + exchange(send, (1, 1))
-    for even, odd in zip(phases, phases[split:] + phases[:split]):
-        near = exchange(mine, (even[0] ^ 1, odd[0] ^ 1))
-        far = exchange(mine, (even[1] ^ 1, odd[1] ^ 1))
-        across = exchange(mine, (even[0] ^ even[1], odd[0] ^ odd[1]))
+    for (low, high), (other_low, other_high) in zip(phases, phases[split:] + phases[:split]):
+        near = exchange(mine, (low ^ 1, other_low ^ 1))
+        far = exchange(mine, (high, other_high))
+        across = exchange(mine, (low ^ high ^ 1, other_low ^ other_high ^ 1))
         mine = (mine + near) + (far + across)
-    for bit in bits[2 * len(phases) :]:
-        mine = mine + exchange(mine, (bit ^ 1, bit ^ 1))
+    for bit in single:
+        mine = mine + exchange(mine, (bit, bit))
     return mine, exchange(mine, (1, 1))
 
 

time: 31.9 us -> 31.7 us (level)
  starting transfers between devices: 9.12 us -> 8.76 us
    ppermute x8, starting transfers between devices: 9.12 us -> 8.76 us  [exchange(): return lax.ppermute(value, ('cells', 'sub'), pairs)]
where the time goes in v13:
time: 31.7 us; the launch traced here: 31.6 us
  waiting for transfers between devices  11.5 us (36%)
  Pallas kernels  9.96 us (31%)
  starting transfers between devices  8.76 us (28%)
  between operations  1.32 us (4%)
    ppermute x8, waiting for transfers between devices, exchange(): return lax.ppermute(value, ('cells', 'sub'), pairs)  11.5 us
    ppermute x8, starting transfers between devices, exchange(): return lax.ppermute(value, ('cells', 'sub'), pairs)  8.76 us
    pallas_call x1, Pallas kernels, finish(): pl.pallas_call(finish_kernel, out_shape=(jax.ShapeDtypeStruct((row_count,...  7.36 us
    pallas_call x1, Pallas kernels, local_sums(): pl.pallas_call(functools.partial(sums_kernel, total_rows), out_shape=(jax...  2.47 us
  transfers between devices with their start and end apart: 8, of which 6 were waited for; matrix products, arithmetic and copies ran while one was open for 0% of the time, Pallas kernels for 0%

profile of v13, /device:TPU:0, one launch (start us, length us, event | category | flops | bytes accessed | tf_op | source)
XLA Modules:
  0.0 31.6 jit_solution(15567690636137724738)
XLA Ops:
  1.3 2.5 %shard_map.67 = (f32[104,256]{1,0:T(8,128)S(1)}, f32[104,256]{1,0:T(8,128)S(1)}, f32[1,512]{1,0:T(1,128)S(1)}) custom-call(f32[512,256]{1,0:T(8,128)} %snapshots_ref.1, f32[512]{0:T(512)} %volumes_hbm.1, s32[1]{0:T(128)S(6)} %copy.7.live_ref, f32[64,512]{1,0:T(8,128)} %probes_hbm.1), custom_call_target="tpu_custom_call" | custom-call | tf_op jit(solution)/shard_map/pallas_call | solution.py:182
  3.8 0.5 %collective-permute-start = (f32[104,256]{1,0:T(8,128)S(1)}, f32[104,256]{1,0:T(8,128)S(1)}, u32[]{:S(2)}, u32[]{:S(2)}) collective-permute-start(f32[104,256]{1,0:T(8,128)S(1)} %get-tuple-element.7), channel_id=1, source_target_pairs={{0,1},{1,0},{2,3},{3,2},{4,5},{5,4},{6,7},{7,6},{8,9},{9,8},{10,11... | collective-permute-start | bytes 319496 | tf_op jit(solution)/shard_map/ppermute | solution.py:274
  4.3 1.0 %collective-permute-done = f32[104,256]{1,0:T(8,128)S(1)} collective-permute-done((f32[104,256]{1,0:T(8,128)S(1)}, f32[104,256]{1,0:T(8,128)S(1)}, u32[]{:S(2)}, u32[]{:S(2)}) %collective-permute-start) | collective-permute-done | bytes 106528 | tf_op jit(solution)/shard_map/ppermute | solution.py:274
  5.3 0.0 copy-start
  5.3 3.6 %collective-permute-start.3 = (f32[104,256]{1,0:T(8,128)S(1)}, f32[104,256]{1,0:T(8,128)S(1)}, u32[]{:S(2)}, u32[]{:S(2)}) collective-permute-start(f32[104,256]{1,0:T(8,128)S(1)} %add.21), channel_id=1, source_target_pairs={{0,7},{1,24},{2,27},{3,4},{4,3},{5,28},{6,31},{7,0},{8,17},{9,14},... | collective-permute-start | bytes 319496 | tf_op jit(solution)/shard_map/ppermute | solution.py:274
  8.9 0.5 %collective-permute-start.2 = (f32[104,256]{1,0:T(8,128)S(1)}, f32[104,256]{1,0:T(8,128)S(1)}, u32[]{:S(2)}, u32[]{:S(2)}) collective-permute-start(f32[104,256]{1,0:T(8,128)S(1)} %add.21), channel_id=1, source_target_pairs={{0,4},{1,17},{2,18},{3,7},{4,0},{5,21},{6,22},{7,3},{8,24},{9,13},... | collective-permute-start | bytes 319496 | tf_op jit(solution)/shard_map/ppermute | solution.py:274
  9.4 0.0 collective-permute-start.1
  9.4 1.9 %collective-permute-done.3 = f32[104,256]{1,0:T(8,128)S(1)} collective-permute-done((f32[104,256]{1,0:T(8,128)S(1)}, f32[104,256]{1,0:T(8,128)S(1)}, u32[]{:S(2)}, u32[]{:S(2)}) %collective-permute-start.3) | collective-permute-done | bytes 106528 | tf_op jit(solution)/shard_map/ppermute | solution.py:274
  11.3 2.3 %collective-permute-done.2 = f32[104,256]{1,0:T(8,128)S(1)} collective-permute-done((f32[104,256]{1,0:T(8,128)S(1)}, f32[104,256]{1,0:T(8,128)S(1)}, u32[]{:S(2)}, u32[]{:S(2)}) %collective-permute-start.2) | collective-permute-done | bytes 106528 | tf_op jit(solution)/shard_map/ppermute | solution.py:274
  13.6 0.0 collective-permute-done.1
  13.6 3.6 %collective-permute-start.6 = (f32[104,256]{1,0:T(8,128)S(1)}, f32[104,256]{1,0:T(8,128)S(1)}, u32[]{:S(2)}, u32[]{:S(2)}) collective-permute-start(f32[104,256]{1,0:T(8,128)S(1)} %add_add_fusion.1), channel_id=1, source_target_pairs={{0,25},{1,6},{2,5},{3,26},{4,29},{5,2},{6,1},{7,30},{8,15},{9,16},... | collective-permute-start | bytes 319496 | tf_op jit(solution)/shard_map/ppermute | solution.py:274
  17.2 0.0 collective-permute-start.5
  17.2 0.4 %collective-permute-start.4 = (f32[104,256]{1,0:T(8,128)S(1)}, f32[104,256]{1,0:T(8,128)S(1)}, u32[]{:S(2)}, u32[]{:S(2)}) collective-permute-start(f32[104,256]{1,0:T(8,128)S(1)} %add_add_fusion.1), channel_id=1, source_target_pairs={{0,9},{1,2},{2,1},{3,10},{4,13},{5,6},{6,5},{7,14},{8,11},{9,0},{1... | collective-permute-start | bytes 319496 | tf_op jit(solution)/shard_map/ppermute | solution.py:274
  17.6 2.2 %collective-permute-done.6 = f32[104,256]{1,0:T(8,128)S(1)} collective-permute-done((f32[104,256]{1,0:T(8,128)S(1)}, f32[104,256]{1,0:T(8,128)S(1)}, u32[]{:S(2)}, u32[]{:S(2)}) %collective-permute-start.6) | collective-permute-done | bytes 106528 | tf_op jit(solution)/shard_map/ppermute | solution.py:274
  19.7 3.1 %collective-permute-done.5 = f32[104,256]{1,0:T(8,128)S(1)} collective-permute-done((f32[104,256]{1,0:T(8,128)S(1)}, f32[104,256]{1,0:T(8,128)S(1)}, u32[]{:S(2)}, u32[]{:S(2)}) %collective-permute-start.5) | collective-permute-done | bytes 106528 | tf_op jit(solution)/shard_map/ppermute | solution.py:274
  22.8 0.0 collective-permute-done.4
  22.8 0.2 collective-permute-start.7
  23.0 0.0 copy-done
  23.0 0.1 shard_map.68.weighted_ref
  23.2 1.1 %collective-permute-done.7.other_ref = f32[104,256]{1,0:T(8,128)S(1)} collective-permute-done((f32[104,256]{1,0:T(8,128)S(1)}, f32[104,256]{1,0:T(8,128)S(1)}, u32[]{:S(2)}, u32[]{:S(2)}) %collective-permute-start.7) | collective-permute-done | bytes 106528 | tf_op jit(solution)/shard_map/ppermute | solution.py:274
  24.2 7.4 %shard_map.69 = (f32[512,256]{1,0:T(8,128)}, f32[256,256]{1,0:T(8,128)}, f32[64,256]{1,0:T(8,128)}) custom-call(f32[104,256]{1,0:T(8,128)S(1)} %add_add_fusion.mine_ref, f32[104,256]{1,0:T(8,128)S(1)} %collective-permute-done.7.other_ref, f32[512,256]{1,0:T(8,128)S(1)} %shard_map.68.weighted_ref), custom_call_target="tpu_custom_call" | custom-call | tf_op jit(solution)/shard_map/pallas_call | solution.py:258
  (3 shorter events, 0.1 us)
Async XLA Ops:
  3.8 1.5 %collective-permute-start = (f32[104,256]{1,0:T(8,128)S(1)}, f32[104,256]{1,0:T(8,128)S(1)}, u32[]{:S(2)}, u32[]{:S(2)}) collective-permute-start(f32[104,256]{1,0:T(8,128)S(1)} %get-tuple-element.7), channel_id=1, source_target_pairs={{0,1},{1,0},{2,3},{3,2},{4,5},{5,4},{6,7},{7,6},{8,9},{9,8},{10,11... | collective-permute-start | bytes 319496 | tf_op jit(solution)/shard_map/ppermute | solution.py:274
  5.3 17.8 %copy-start = (f32[512,256]{1,0:T(8,128)S(1)}, f32[512,256]{1,0:T(8,128)}, u32[]{:S(2)}) copy-start(f32[512,256]{1,0:T(8,128)} %snapshots_ref.1) | copy-start | bytes 1572868
  5.3 6.0 %collective-permute-start.3 = (f32[104,256]{1,0:T(8,128)S(1)}, f32[104,256]{1,0:T(8,128)S(1)}, u32[]{:S(2)}, u32[]{:S(2)}) collective-permute-start(f32[104,256]{1,0:T(8,128)S(1)} %add.21), channel_id=1, source_target_pairs={{0,7},{1,24},{2,27},{3,4},{4,3},{5,28},{6,31},{7,0},{8,17},{9,14},... | collective-permute-start | bytes 319496 | tf_op jit(solution)/shard_map/ppermute | solution.py:274
  8.9 4.7 %collective-permute-start.2 = (f32[104,256]{1,0:T(8,128)S(1)}, f32[104,256]{1,0:T(8,128)S(1)}, u32[]{:S(2)}, u32[]{:S(2)}) collective-permute-start(f32[104,256]{1,0:T(8,128)S(1)} %add.21), channel_id=1, source_target_pairs={{0,4},{1,17},{2,18},{3,7},{4,0},{5,21},{6,22},{7,3},{8,24},{9,13},... | collective-permute-start | bytes 319496 | tf_op jit(solution)/shard_map/ppermute | solution.py:274
  9.4 4.2 %collective-permute-start.1 = (f32[104,256]{1,0:T(8,128)S(1)}, f32[104,256]{1,0:T(8,128)S(1)}, u32[]{:S(2)}, u32[]{:S(2)}) collective-permute-start(f32[104,256]{1,0:T(8,128)S(1)} %add.21), channel_id=1, source_target_pairs={{0,3},{1,8},{2,11},{3,0},{4,7},{5,12},{6,15},{7,4},{8,1},{9,10},{1... | collective-permute-start | bytes 319496 | tf_op jit(solution)/shard_map/ppermute | solution.py:274
  13.6 6.1 %collective-permute-start.6 = (f32[104,256]{1,0:T(8,128)S(1)}, f32[104,256]{1,0:T(8,128)S(1)}, u32[]{:S(2)}, u32[]{:S(2)}) collective-permute-start(f32[104,256]{1,0:T(8,128)S(1)} %add_add_fusion.1), channel_id=1, source_target_pairs={{0,25},{1,6},{2,5},{3,26},{4,29},{5,2},{6,1},{7,30},{8,15},{9,16},... | collective-permute-start | bytes 319496 | tf_op jit(solution)/shard_map/ppermute | solution.py:274
  17.2 5.6 %collective-permute-start.5 = (f32[104,256]{1,0:T(8,128)S(1)}, f32[104,256]{1,0:T(8,128)S(1)}, u32[]{:S(2)}, u32[]{:S(2)}) collective-permute-start(f32[104,256]{1,0:T(8,128)S(1)} %add_add_fusion.1), channel_id=1, source_target_pairs={{0,16},{1,5},{2,6},{3,19},{4,20},{5,1},{6,2},{7,23},{8,12},{9,25},... | collective-permute-start | bytes 319496 | tf_op jit(solution)/shard_map/ppermute | solution.py:274
  17.2 5.6 %collective-permute-start.4 = (f32[104,256]{1,0:T(8,128)S(1)}, f32[104,256]{1,0:T(8,128)S(1)}, u32[]{:S(2)}, u32[]{:S(2)}) collective-permute-start(f32[104,256]{1,0:T(8,128)S(1)} %add_add_fusion.1), channel_id=1, source_target_pairs={{0,9},{1,2},{2,1},{3,10},{4,13},{5,6},{6,5},{7,14},{8,11},{9,0},{1... | collective-permute-start | bytes 319496 | tf_op jit(solution)/shard_map/ppermute | solution.py:274
  22.8 1.4 %collective-permute-start.7 = (f32[104,256]{1,0:T(8,128)S(1)}, f32[104,256]{1,0:T(8,128)S(1)}, u32[]{:S(2)}, u32[]{:S(2)}) collective-permute-start(f32[104,256]{1,0:T(8,128)S(1)} %add_add_fusion.mine_ref), channel_id=1, source_target_pairs={{0,1},{1,0},{2,3},{3,2},{4,5},{5,4},{6,7},{7,6},{8,9},{9,8},{10,11... | collective-permute-start | bytes 319496 | tf_op jit(solution)/shard_map/ppermute | solution.py:274

commit v14 on v13

--- a/solution.py
+++ b/solution.py
@@ -41,19 +41,14 @@
         return total
 
     lower_rows = []
-    following = [lanes_of(tiles[0], c) for c in range(BLOCK)]
-    carried = [lanes_of(tiles[1], c) for c in range(BLOCK)]
     for block in range(count):
         offset = block * BLOCK
         in_block = (lane_ids >= offset) & (lane_ids < offset + BLOCK)
-        columns = following
+        columns = [lanes_of(tiles[block], offset + c) for c in range(BLOCK)]
         own = jnp.where(in_block, jnp.where(spread_ids == offset, 1.0, 0.0), tiles[block])
         rows = [row_of(own, r) for r in range(BLOCK)]
         near = range(block + 1, min(block + 1 + AHEAD, count))
-        weights = {k: [lanes_of(tiles[k], offset + c) for c in range(BLOCK)] for k in near if k > block + 1}
-        weights[block + 1] = carried
-        bases = {k: [lanes_of(tiles[k], offset + BLOCK + c) for c in range(BLOCK)] for k in near if k <= block + 2}
-        changes = {k: [None] * BLOCK for k in bases}
+        weights = {k: [lanes_of(tiles[k], offset + c) for c in range(BLOCK)] for k in near}
         for k in near:
             tiles[k] = jnp.where(in_block, 0.0, tiles[k])
         pivots, inverse, scaled = [row_of(columns[0], 0)], [], {}
@@ -70,19 +65,11 @@
             for k in near:
                 here = weights[k][i]
                 weight = here * inv
-                if k == block + 1:
-                    splats = [row_of(here, c) for c in range(BLOCK)]
-                if k in changes:
-                    for c in range(BLOCK):
-                        change = weight * splats[c]
-                        changes[k][c] = change if i == 0 else changes[k][c] + change
                 for c in range(i + 1, BLOCK):
                     weights[k][c] = weights[k][c] - here * scaled[c, i]
                 tiles[k] = tiles[k] - weight * rows[i]
             for r in range(i + 1, BLOCK):
                 rows[r] = rows[r] - scaled[r, i] * rows[i]
-        updated = {k: [base - change for base, change in zip(bases[k], changes[k])] for k in bases}
-        following, carried = updated.get(block + 1), updated.get(block + 2)
         merged = gather(rows) * lax.rsqrt(gather(pivots))
         lower_rows.append(jnp.where(spread_ids <= offset, merged, 0.0))
         if block + 1 + AHEAD < count:

time: 31.7 us -> 35.4 us (1.12)
  Pallas kernels: 9.96 us -> 13.6 us
    pallas_call x1, Pallas kernels: 7.36 us -> 11 us  [finish(): pl.pallas_call(finish_kernel, out_shape=(jax.ShapeDtypeStruct((row_count,...]
where the time goes in v14:
time: 35.4 us; the launch traced here: 35.2 us
  Pallas kernels  13.6 us (38%)
  waiting for transfers between devices  11.5 us (32%)
  starting transfers between devices  8.76 us (25%)
  between operations  1.32 us (4%)
    ppermute x8, waiting for transfers between devices, exchange(): return lax.ppermute(value, ('cells', 'sub'), pairs)  11.5 us
    pallas_call x1, Pallas kernels, finish(): pl.pallas_call(finish_kernel, out_shape=(jax.ShapeDtypeStruct((row_count,...  11 us
    ppermute x8, starting transfers between devices, exchange(): return lax.ppermute(value, ('cells', 'sub'), pairs)  8.76 us
    pallas_call x1, Pallas kernels, local_sums(): pl.pallas_call(functools.partial(sums_kernel, total_rows), out_shape=(jax...  2.47 us
  transfers between devices with their start and end apart: 8, of which 6 were waited for; matrix products, arithmetic and copies ran while one was open for 0% of the time, Pallas kernels for 0%

profile of v14, /device:TPU:0, one launch (start us, length us, event | category | flops | bytes accessed | tf_op | source)
XLA Modules:
  0.0 35.2 jit_solution(17040094754558938692)
XLA Ops:
  1.3 2.5 %shard_map.67 = (f32[104,256]{1,0:T(8,128)S(1)}, f32[104,256]{1,0:T(8,128)S(1)}, f32[1,512]{1,0:T(1,128)S(1)}) custom-call(f32[512,256]{1,0:T(8,128)} %snapshots_ref.1, f32[512]{0:T(512)} %volumes_hbm.1, s32[1]{0:T(128)S(6)} %copy.7.live_ref, f32[64,512]{1,0:T(8,128)} %probes_hbm.1), custom_call_target="tpu_custom_call" | custom-call | tf_op jit(solution)/shard_map/pallas_call | solution.py:169
  3.8 0.5 %collective-permute-start = (f32[104,256]{1,0:T(8,128)S(1)}, f32[104,256]{1,0:T(8,128)S(1)}, u32[]{:S(2)}, u32[]{:S(2)}) collective-permute-start(f32[104,256]{1,0:T(8,128)S(1)} %get-tuple-element.7), channel_id=1, source_target_pairs={{0,1},{1,0},{2,3},{3,2},{4,5},{5,4},{6,7},{7,6},{8,9},{9,8},{10,11... | collective-permute-start | bytes 319496 | tf_op jit(solution)/shard_map/ppermute | solution.py:261
  4.3 1.0 %collective-permute-done = f32[104,256]{1,0:T(8,128)S(1)} collective-permute-done((f32[104,256]{1,0:T(8,128)S(1)}, f32[104,256]{1,0:T(8,128)S(1)}, u32[]{:S(2)}, u32[]{:S(2)}) %collective-permute-start) | collective-permute-done | bytes 106528 | tf_op jit(solution)/shard_map/ppermute | solution.py:261
  5.3 0.0 copy-start
  5.3 3.6 %collective-permute-start.3 = (f32[104,256]{1,0:T(8,128)S(1)}, f32[104,256]{1,0:T(8,128)S(1)}, u32[]{:S(2)}, u32[]{:S(2)}) collective-permute-start(f32[104,256]{1,0:T(8,128)S(1)} %add.21), channel_id=1, source_target_pairs={{0,7},{1,24},{2,27},{3,4},{4,3},{5,28},{6,31},{7,0},{8,17},{9,14},... | collective-permute-start | bytes 319496 | tf_op jit(solution)/shard_map/ppermute | solution.py:261
  8.9 0.5 %collective-permute-start.2 = (f32[104,256]{1,0:T(8,128)S(1)}, f32[104,256]{1,0:T(8,128)S(1)}, u32[]{:S(2)}, u32[]{:S(2)}) collective-permute-start(f32[104,256]{1,0:T(8,128)S(1)} %add.21), channel_id=1, source_target_pairs={{0,4},{1,17},{2,18},{3,7},{4,0},{5,21},{6,22},{7,3},{8,24},{9,13},... | collective-permute-start | bytes 319496 | tf_op jit(solution)/shard_map/ppermute | solution.py:261
  9.4 0.0 collective-permute-start.1
  9.4 1.9 %collective-permute-done.3 = f32[104,256]{1,0:T(8,128)S(1)} collective-permute-done((f32[104,256]{1,0:T(8,128)S(1)}, f32[104,256]{1,0:T(8,128)S(1)}, u32[]{:S(2)}, u32[]{:S(2)}) %collective-permute-start.3) | collective-permute-done | bytes 106528 | tf_op jit(solution)/shard_map/ppermute | solution.py:261
  11.3 2.3 %collective-permute-done.2 = f32[104,256]{1,0:T(8,128)S(1)} collective-permute-done((f32[104,256]{1,0:T(8,128)S(1)}, f32[104,256]{1,0:T(8,128)S(1)}, u32[]{:S(2)}, u32[]{:S(2)}) %collective-permute-start.2) | collective-permute-done | bytes 106528 | tf_op jit(solution)/shard_map/ppermute | solution.py:261
  13.6 0.0 collective-permute-done.1
  13.6 3.6 %collective-permute-start.6 = (f32[104,256]{1,0:T(8,128)S(1)}, f32[104,256]{1,0:T(8,128)S(1)}, u32[]{:S(2)}, u32[]{:S(2)}) collective-permute-start(f32[104,256]{1,0:T(8,128)S(1)} %add_add_fusion.1), channel_id=1, source_target_pairs={{0,25},{1,6},{2,5},{3,26},{4,29},{5,2},{6,1},{7,30},{8,15},{9,16},... | collective-permute-start | bytes 319496 | tf_op jit(solution)/shard_map/ppermute | solution.py:261
  17.2 0.0 collective-permute-start.5
  17.2 0.4 %collective-permute-start.4 = (f32[104,256]{1,0:T(8,128)S(1)}, f32[104,256]{1,0:T(8,128)S(1)}, u32[]{:S(2)}, u32[]{:S(2)}) collective-permute-start(f32[104,256]{1,0:T(8,128)S(1)} %add_add_fusion.1), channel_id=1, source_target_pairs={{0,9},{1,2},{2,1},{3,10},{4,13},{5,6},{6,5},{7,14},{8,11},{9,0},{1... | collective-permute-start | bytes 319496 | tf_op jit(solution)/shard_map/ppermute | solution.py:261
  17.6 2.2 %collective-permute-done.6 = f32[104,256]{1,0:T(8,128)S(1)} collective-permute-done((f32[104,256]{1,0:T(8,128)S(1)}, f32[104,256]{1,0:T(8,128)S(1)}, u32[]{:S(2)}, u32[]{:S(2)}) %collective-permute-start.6) | collective-permute-done | bytes 106528 | tf_op jit(solution)/shard_map/ppermute | solution.py:261
  19.7 3.1 %collective-permute-done.5 = f32[104,256]{1,0:T(8,128)S(1)} collective-permute-done((f32[104,256]{1,0:T(8,128)S(1)}, f32[104,256]{1,0:T(8,128)S(1)}, u32[]{:S(2)}, u32[]{:S(2)}) %collective-permute-start.5) | collective-permute-done | bytes 106528 | tf_op jit(solution)/shard_map/ppermute | solution.py:261
  22.8 0.0 collective-permute-done.4
  22.8 0.2 collective-permute-start.7
  23.0 0.0 copy-done
  23.0 0.1 shard_map.68.weighted_ref
  23.2 1.1 %collective-permute-done.7.other_ref = f32[104,256]{1,0:T(8,128)S(1)} collective-permute-done((f32[104,256]{1,0:T(8,128)S(1)}, f32[104,256]{1,0:T(8,128)S(1)}, u32[]{:S(2)}, u32[]{:S(2)}) %collective-permute-start.7) | collective-permute-done | bytes 106528 | tf_op jit(solution)/shard_map/ppermute | solution.py:261
  24.2 11.0 %shard_map.69 = (f32[512,256]{1,0:T(8,128)}, f32[256,256]{1,0:T(8,128)}, f32[64,256]{1,0:T(8,128)}) custom-call(f32[104,256]{1,0:T(8,128)S(1)} %add_add_fusion.mine_ref, f32[104,256]{1,0:T(8,128)S(1)} %collective-permute-done.7.other_ref, f32[512,256]{1,0:T(8,128)S(1)} %shard_map.68.weighted_ref), custom_call_target="tpu_custom_call" | custom-call | tf_op jit(solution)/shard_map/pallas_call | solution.py:245
  (3 shorter events, 0.1 us)
Async XLA Ops:
  3.8 1.5 %collective-permute-start = (f32[104,256]{1,0:T(8,128)S(1)}, f32[104,256]{1,0:T(8,128)S(1)}, u32[]{:S(2)}, u32[]{:S(2)}) collective-permute-start(f32[104,256]{1,0:T(8,128)S(1)} %get-tuple-element.7), channel_id=1, source_target_pairs={{0,1},{1,0},{2,3},{3,2},{4,5},{5,4},{6,7},{7,6},{8,9},{9,8},{10,11... | collective-permute-start | bytes 319496 | tf_op jit(solution)/shard_map/ppermute | solution.py:261
  5.3 17.8 %copy-start = (f32[512,256]{1,0:T(8,128)S(1)}, f32[512,256]{1,0:T(8,128)}, u32[]{:S(2)}) copy-start(f32[512,256]{1,0:T(8,128)} %snapshots_ref.1) | copy-start | bytes 1572868
  5.3 6.0 %collective-permute-start.3 = (f32[104,256]{1,0:T(8,128)S(1)}, f32[104,256]{1,0:T(8,128)S(1)}, u32[]{:S(2)}, u32[]{:S(2)}) collective-permute-start(f32[104,256]{1,0:T(8,128)S(1)} %add.21), channel_id=1, source_target_pairs={{0,7},{1,24},{2,27},{3,4},{4,3},{5,28},{6,31},{7,0},{8,17},{9,14},... | collective-permute-start | bytes 319496 | tf_op jit(solution)/shard_map/ppermute | solution.py:261
  8.9 4.7 %collective-permute-start.2 = (f32[104,256]{1,0:T(8,128)S(1)}, f32[104,256]{1,0:T(8,128)S(1)}, u32[]{:S(2)}, u32[]{:S(2)}) collective-permute-start(f32[104,256]{1,0:T(8,128)S(1)} %add.21), channel_id=1, source_target_pairs={{0,4},{1,17},{2,18},{3,7},{4,0},{5,21},{6,22},{7,3},{8,24},{9,13},... | collective-permute-start | bytes 319496 | tf_op jit(solution)/shard_map/ppermute | solution.py:261
  9.4 4.2 %collective-permute-start.1 = (f32[104,256]{1,0:T(8,128)S(1)}, f32[104,256]{1,0:T(8,128)S(1)}, u32[]{:S(2)}, u32[]{:S(2)}) collective-permute-start(f32[104,256]{1,0:T(8,128)S(1)} %add.21), channel_id=1, source_target_pairs={{0,3},{1,8},{2,11},{3,0},{4,7},{5,12},{6,15},{7,4},{8,1},{9,10},{1... | collective-permute-start | bytes 319496 | tf_op jit(solution)/shard_map/ppermute | solution.py:261
  13.6 6.1 %collective-permute-start.6 = (f32[104,256]{1,0:T(8,128)S(1)}, f32[104,256]{1,0:T(8,128)S(1)}, u32[]{:S(2)}, u32[]{:S(2)}) collective-permute-start(f32[104,256]{1,0:T(8,128)S(1)} %add_add_fusion.1), channel_id=1, source_target_pairs={{0,25},{1,6},{2,5},{3,26},{4,29},{5,2},{6,1},{7,30},{8,15},{9,16},... | collective-permute-start | bytes 319496 | tf_op jit(solution)/shard_map/ppermute | solution.py:261
  17.2 5.6 %collective-permute-start.5 = (f32[104,256]{1,0:T(8,128)S(1)}, f32[104,256]{1,0:T(8,128)S(1)}, u32[]{:S(2)}, u32[]{:S(2)}) collective-permute-start(f32[104,256]{1,0:T(8,128)S(1)} %add_add_fusion.1), channel_id=1, source_target_pairs={{0,16},{1,5},{2,6},{3,19},{4,20},{5,1},{6,2},{7,23},{8,12},{9,25},... | collective-permute-start | bytes 319496 | tf_op jit(solution)/shard_map/ppermute | solution.py:261
  17.2 5.6 %collective-permute-start.4 = (f32[104,256]{1,0:T(8,128)S(1)}, f32[104,256]{1,0:T(8,128)S(1)}, u32[]{:S(2)}, u32[]{:S(2)}) collective-permute-start(f32[104,256]{1,0:T(8,128)S(1)} %add_add_fusion.1), channel_id=1, source_target_pairs={{0,9},{1,2},{2,1},{3,10},{4,13},{5,6},{6,5},{7,14},{8,11},{9,0},{1... | collective-permute-start | bytes 319496 | tf_op jit(solution)/shard_map/ppermute | solution.py:261
  22.8 1.4 %collective-permute-start.7 = (f32[104,256]{1,0:T(8,128)S(1)}, f32[104,256]{1,0:T(8,128)S(1)}, u32[]{:S(2)}, u32[]{:S(2)}) collective-permute-start(f32[104,256]{1,0:T(8,128)S(1)} %add_add_fusion.mine_ref), channel_id=1, source_target_pairs={{0,1},{1,0},{2,3},{3,2},{4,5},{5,4},{6,7},{7,6},{8,9},{9,8},{10,11... | collective-permute-start | bytes 319496 | tf_op jit(solution)/shard_map/ppermute | solution.py:261

commit v15 on v13

--- a/solution.py
+++ b/solution.py
@@ -14,7 +14,8 @@
 
 
 def lanes_of(tile, column):
-    return jnp.broadcast_to(tile[:, column : column + 1], tile.shape)
+    index = jnp.full(tile.shape, column, jnp.int32)
+    return jnp.take_along_axis(tile, index, axis=1, mode="promise_in_bounds")
 
 
 def row_of(tile, index):

time: 31.7 us -> 31.7 us (level)
  no operation moved by 1% of the time
where the time goes in v15:
time: 31.7 us; the launch traced here: 31.5 us
  waiting for transfers between devices  11.5 us (36%)
  Pallas kernels  9.93 us (31%)
  starting transfers between devices  8.76 us (28%)
  between operations  1.32 us (4%)
    ppermute x8, waiting for transfers between devices, exchange(): return lax.ppermute(value, ('cells', 'sub'), pairs)  11.5 us
    ppermute x8, starting transfers between devices, exchange(): return lax.ppermute(value, ('cells', 'sub'), pairs)  8.76 us
    pallas_call x1, Pallas kernels, finish(): pl.pallas_call(finish_kernel, out_shape=(jax.ShapeDtypeStruct((row_count,...  7.33 us
    pallas_call x1, Pallas kernels, local_sums(): pl.pallas_call(functools.partial(sums_kernel, total_rows), out_shape=(jax...  2.47 us
  transfers between devices with their start and end apart: 8, of which 6 were waited for; matrix products, arithmetic and copies ran while one was open for 0% of the time, Pallas kernels for 0%

profile of v15, /device:TPU:0, one launch (start us, length us, event | category | flops | bytes accessed | tf_op | source)
XLA Modules:
  0.0 31.5 jit_solution(12516493137773263807)
XLA Ops:
  1.3 2.5 %shard_map.67 = (f32[104,256]{1,0:T(8,128)S(1)}, f32[104,256]{1,0:T(8,128)S(1)}, f32[1,512]{1,0:T(1,128)S(1)}) custom-call(f32[512,256]{1,0:T(8,128)} %snapshots_ref.1, f32[512]{0:T(512)} %volumes_hbm.1, s32[1]{0:T(128)S(6)} %copy.7.live_ref, f32[64,512]{1,0:T(8,128)} %probes_hbm.1), custom_call_target="tpu_custom_call" | custom-call | tf_op jit(solution)/shard_map/pallas_call | solution.py:183
  3.8 0.5 %collective-permute-start = (f32[104,256]{1,0:T(8,128)S(1)}, f32[104,256]{1,0:T(8,128)S(1)}, u32[]{:S(2)}, u32[]{:S(2)}) collective-permute-start(f32[104,256]{1,0:T(8,128)S(1)} %get-tuple-element.7), channel_id=1, source_target_pairs={{0,1},{1,0},{2,3},{3,2},{4,5},{5,4},{6,7},{7,6},{8,9},{9,8},{10,11... | collective-permute-start | bytes 319496 | tf_op jit(solution)/shard_map/ppermute | solution.py:275
  4.3 1.0 %collective-permute-done = f32[104,256]{1,0:T(8,128)S(1)} collective-permute-done((f32[104,256]{1,0:T(8,128)S(1)}, f32[104,256]{1,0:T(8,128)S(1)}, u32[]{:S(2)}, u32[]{:S(2)}) %collective-permute-start) | collective-permute-done | bytes 106528 | tf_op jit(solution)/shard_map/ppermute | solution.py:275
  5.3 0.0 copy-start
  5.3 3.6 %collective-permute-start.3 = (f32[104,256]{1,0:T(8,128)S(1)}, f32[104,256]{1,0:T(8,128)S(1)}, u32[]{:S(2)}, u32[]{:S(2)}) collective-permute-start(f32[104,256]{1,0:T(8,128)S(1)} %add.21), channel_id=1, source_target_pairs={{0,7},{1,24},{2,27},{3,4},{4,3},{5,28},{6,31},{7,0},{8,17},{9,14},... | collective-permute-start | bytes 319496 | tf_op jit(solution)/shard_map/ppermute | solution.py:275
  8.9 0.5 %collective-permute-start.2 = (f32[104,256]{1,0:T(8,128)S(1)}, f32[104,256]{1,0:T(8,128)S(1)}, u32[]{:S(2)}, u32[]{:S(2)}) collective-permute-start(f32[104,256]{1,0:T(8,128)S(1)} %add.21), channel_id=1, source_target_pairs={{0,4},{1,17},{2,18},{3,7},{4,0},{5,21},{6,22},{7,3},{8,24},{9,13},... | collective-permute-start | bytes 319496 | tf_op jit(solution)/shard_map/ppermute | solution.py:275
  9.4 0.0 collective-permute-start.1
  9.4 1.9 %collective-permute-done.3 = f32[104,256]{1,0:T(8,128)S(1)} collective-permute-done((f32[104,256]{1,0:T(8,128)S(1)}, f32[104,256]{1,0:T(8,128)S(1)}, u32[]{:S(2)}, u32[]{:S(2)}) %collective-permute-start.3) | collective-permute-done | bytes 106528 | tf_op jit(solution)/shard_map/ppermute | solution.py:275
  11.3 2.3 %collective-permute-done.2 = f32[104,256]{1,0:T(8,128)S(1)} collective-permute-done((f32[104,256]{1,0:T(8,128)S(1)}, f32[104,256]{1,0:T(8,128)S(1)}, u32[]{:S(2)}, u32[]{:S(2)}) %collective-permute-start.2) | collective-permute-done | bytes 106528 | tf_op jit(solution)/shard_map/ppermute | solution.py:275
  13.6 0.0 collective-permute-done.1
  13.6 3.6 %collective-permute-start.6 = (f32[104,256]{1,0:T(8,128)S(1)}, f32[104,256]{1,0:T(8,128)S(1)}, u32[]{:S(2)}, u32[]{:S(2)}) collective-permute-start(f32[104,256]{1,0:T(8,128)S(1)} %add_add_fusion.1), channel_id=1, source_target_pairs={{0,25},{1,6},{2,5},{3,26},{4,29},{5,2},{6,1},{7,30},{8,15},{9,16},... | collective-permute-start | bytes 319496 | tf_op jit(solution)/shard_map/ppermute | solution.py:275
  17.2 0.0 collective-permute-start.5
  17.2 0.4 %collective-permute-start.4 = (f32[104,256]{1,0:T(8,128)S(1)}, f32[104,256]{1,0:T(8,128)S(1)}, u32[]{:S(2)}, u32[]{:S(2)}) collective-permute-start(f32[104,256]{1,0:T(8,128)S(1)} %add_add_fusion.1), channel_id=1, source_target_pairs={{0,9},{1,2},{2,1},{3,10},{4,13},{5,6},{6,5},{7,14},{8,11},{9,0},{1... | collective-permute-start | bytes 319496 | tf_op jit(solution)/shard_map/ppermute | solution.py:275
  17.6 2.2 %collective-permute-done.6 = f32[104,256]{1,0:T(8,128)S(1)} collective-permute-done((f32[104,256]{1,0:T(8,128)S(1)}, f32[104,256]{1,0:T(8,128)S(1)}, u32[]{:S(2)}, u32[]{:S(2)}) %collective-permute-start.6) | collective-permute-done | bytes 106528 | tf_op jit(solution)/shard_map/ppermute | solution.py:275
  19.7 3.1 %collective-permute-done.5 = f32[104,256]{1,0:T(8,128)S(1)} collective-permute-done((f32[104,256]{1,0:T(8,128)S(1)}, f32[104,256]{1,0:T(8,128)S(1)}, u32[]{:S(2)}, u32[]{:S(2)}) %collective-permute-start.5) | collective-permute-done | bytes 106528 | tf_op jit(solution)/shard_map/ppermute | solution.py:275
  22.8 0.0 collective-permute-done.4
  22.8 0.2 collective-permute-start.7
  23.0 0.0 copy-done
  23.0 0.1 shard_map.68.weighted_ref
  23.2 1.1 %collective-permute-done.7.other_ref = f32[104,256]{1,0:T(8,128)S(1)} collective-permute-done((f32[104,256]{1,0:T(8,128)S(1)}, f32[104,256]{1,0:T(8,128)S(1)}, u32[]{:S(2)}, u32[]{:S(2)}) %collective-permute-start.7) | collective-permute-done | bytes 106528 | tf_op jit(solution)/shard_map/ppermute | solution.py:275
  24.2 7.3 %shard_map.69 = (f32[512,256]{1,0:T(8,128)}, f32[256,256]{1,0:T(8,128)}, f32[64,256]{1,0:T(8,128)}) custom-call(f32[104,256]{1,0:T(8,128)S(1)} %add_add_fusion.mine_ref, f32[104,256]{1,0:T(8,128)S(1)} %collective-permute-done.7.other_ref, f32[512,256]{1,0:T(8,128)S(1)} %shard_map.68.weighted_ref), custom_call_target="tpu_custom_call" | custom-call | tf_op jit(solution)/shard_map/pallas_call | solution.py:259
  (3 shorter events, 0.1 us)
Async XLA Ops:
  3.8 1.5 %collective-permute-start = (f32[104,256]{1,0:T(8,128)S(1)}, f32[104,256]{1,0:T(8,128)S(1)}, u32[]{:S(2)}, u32[]{:S(2)}) collective-permute-start(f32[104,256]{1,0:T(8,128)S(1)} %get-tuple-element.7), channel_id=1, source_target_pairs={{0,1},{1,0},{2,3},{3,2},{4,5},{5,4},{6,7},{7,6},{8,9},{9,8},{10,11... | collective-permute-start | bytes 319496 | tf_op jit(solution)/shard_map/ppermute | solution.py:275
  5.3 17.8 %copy-start = (f32[512,256]{1,0:T(8,128)S(1)}, f32[512,256]{1,0:T(8,128)}, u32[]{:S(2)}) copy-start(f32[512,256]{1,0:T(8,128)} %snapshots_ref.1) | copy-start | bytes 1572868
  5.3 6.0 %collective-permute-start.3 = (f32[104,256]{1,0:T(8,128)S(1)}, f32[104,256]{1,0:T(8,128)S(1)}, u32[]{:S(2)}, u32[]{:S(2)}) collective-permute-start(f32[104,256]{1,0:T(8,128)S(1)} %add.21), channel_id=1, source_target_pairs={{0,7},{1,24},{2,27},{3,4},{4,3},{5,28},{6,31},{7,0},{8,17},{9,14},... | collective-permute-start | bytes 319496 | tf_op jit(solution)/shard_map/ppermute | solution.py:275
  8.9 4.7 %collective-permute-start.2 = (f32[104,256]{1,0:T(8,128)S(1)}, f32[104,256]{1,0:T(8,128)S(1)}, u32[]{:S(2)}, u32[]{:S(2)}) collective-permute-start(f32[104,256]{1,0:T(8,128)S(1)} %add.21), channel_id=1, source_target_pairs={{0,4},{1,17},{2,18},{3,7},{4,0},{5,21},{6,22},{7,3},{8,24},{9,13},... | collective-permute-start | bytes 319496 | tf_op jit(solution)/shard_map/ppermute | solution.py:275
  9.4 4.2 %collective-permute-start.1 = (f32[104,256]{1,0:T(8,128)S(1)}, f32[104,256]{1,0:T(8,128)S(1)}, u32[]{:S(2)}, u32[]{:S(2)}) collective-permute-start(f32[104,256]{1,0:T(8,128)S(1)} %add.21), channel_id=1, source_target_pairs={{0,3},{1,8},{2,11},{3,0},{4,7},{5,12},{6,15},{7,4},{8,1},{9,10},{1... | collective-permute-start | bytes 319496 | tf_op jit(solution)/shard_map/ppermute | solution.py:275
  13.6 6.1 %collective-permute-start.6 = (f32[104,256]{1,0:T(8,128)S(1)}, f32[104,256]{1,0:T(8,128)S(1)}, u32[]{:S(2)}, u32[]{:S(2)}) collective-permute-start(f32[104,256]{1,0:T(8,128)S(1)} %add_add_fusion.1), channel_id=1, source_target_pairs={{0,25},{1,6},{2,5},{3,26},{4,29},{5,2},{6,1},{7,30},{8,15},{9,16},... | collective-permute-start | bytes 319496 | tf_op jit(solution)/shard_map/ppermute | solution.py:275
  17.2 5.6 %collective-permute-start.5 = (f32[104,256]{1,0:T(8,128)S(1)}, f32[104,256]{1,0:T(8,128)S(1)}, u32[]{:S(2)}, u32[]{:S(2)}) collective-permute-start(f32[104,256]{1,0:T(8,128)S(1)} %add_add_fusion.1), channel_id=1, source_target_pairs={{0,16},{1,5},{2,6},{3,19},{4,20},{5,1},{6,2},{7,23},{8,12},{9,25},... | collective-permute-start | bytes 319496 | tf_op jit(solution)/shard_map/ppermute | solution.py:275
  17.2 5.6 %collective-permute-start.4 = (f32[104,256]{1,0:T(8,128)S(1)}, f32[104,256]{1,0:T(8,128)S(1)}, u32[]{:S(2)}, u32[]{:S(2)}) collective-permute-start(f32[104,256]{1,0:T(8,128)S(1)} %add_add_fusion.1), channel_id=1, source_target_pairs={{0,9},{1,2},{2,1},{3,10},{4,13},{5,6},{6,5},{7,14},{8,11},{9,0},{1... | collective-permute-start | bytes 319496 | tf_op jit(solution)/shard_map/ppermute | solution.py:275
  22.8 1.4 %collective-permute-start.7 = (f32[104,256]{1,0:T(8,128)S(1)}, f32[104,256]{1,0:T(8,128)S(1)}, u32[]{:S(2)}, u32[]{:S(2)}) collective-permute-start(f32[104,256]{1,0:T(8,128)S(1)} %add_add_fusion.mine_ref), channel_id=1, source_target_pairs={{0,1},{1,0},{2,3},{3,2},{4,5},{5,4},{6,7},{7,6},{8,9},{9,8},{10,11... | collective-permute-start | bytes 319496 | tf_op jit(solution)/shard_map/ppermute | solution.py:275

commit v16 on v13

--- a/solution.py
+++ b/solution.py
@@ -43,6 +43,7 @@
     lower_rows = []
     following = [lanes_of(tiles[0], c) for c in range(BLOCK)]
     carried = [lanes_of(tiles[1], c) for c in range(BLOCK)]
+    pending = [lanes_of(tiles[1], BLOCK + c) for c in range(BLOCK)]
     for block in range(count):
         offset = block * BLOCK
         in_block = (lane_ids >= offset) & (lane_ids < offset + BLOCK)
@@ -52,8 +53,11 @@
         near = range(block + 1, min(block + 1 + AHEAD, count))
         weights = {k: [lanes_of(tiles[k], offset + c) for c in range(BLOCK)] for k in near if k > block + 1}
         weights[block + 1] = carried
-        bases = {k: [lanes_of(tiles[k], offset + BLOCK + c) for c in range(BLOCK)] for k in near if k <= block + 2}
+        bases = {k: [lanes_of(tiles[k], offset + BLOCK + c) for c in range(BLOCK)] for k in near if k == block + 2}
+        if block + 1 < count:
+            bases[block + 1] = pending
         changes = {k: [None] * BLOCK for k in bases}
+        pending, pending_changes = [lanes_of(tiles[k], offset + 2 * BLOCK + c) for k in near if k == block + 2 for c in range(BLOCK)], []
         for k in near:
             tiles[k] = jnp.where(in_block, 0.0, tiles[k])
         pivots, inverse, scaled = [row_of(columns[0], 0)], [], {}
@@ -76,12 +80,16 @@
                     for c in range(BLOCK):
                         change = weight * splats[c]
                         changes[k][c] = change if i == 0 else changes[k][c] + change
+                if k == block + 2:
+                    terms = [weight * row_of(here, c) for c in range(BLOCK)]
+                    pending_changes = [a + b for a, b in zip(pending_changes, terms)] if i else terms
                 for c in range(i + 1, BLOCK):
                     weights[k][c] = weights[k][c] - here * scaled[c, i]
                 tiles[k] = tiles[k] - weight * rows[i]
             for r in range(i + 1, BLOCK):
                 rows[r] = rows[r] - scaled[r, i] * rows[i]
         updated = {k: [base - change for base, change in zip(bases[k], changes[k])] for k in bases}
+        pending = [base - change for base, change in zip(pending, pending_changes)]
         following, carried = updated.get(block + 1), updated.get(block + 2)
         merged = gather(rows) * lax.rsqrt(gather(pivots))
         lower_rows.append(jnp.where(spread_ids <= offset, merged, 0.0))

time: 31.7 us -> 32.9 us (1.038)
  Pallas kernels: 9.96 us -> 11.1 us
    pallas_call x1, Pallas kernels: 7.36 us -> 8.49 us  [finish(): pl.pallas_call(finish_kernel, out_shape=(jax.ShapeDtypeStruct((row_count,...]
where the time goes in v16:
time: 32.9 us; the launch traced here: 32.7 us
  waiting for transfers between devices  11.5 us (35%)
  Pallas kernels  11.1 us (34%)
  starting transfers between devices  8.76 us (27%)
  between operations  1.32 us (4%)
    ppermute x8, waiting for transfers between devices, exchange(): return lax.ppermute(value, ('cells', 'sub'), pairs)  11.5 us
    ppermute x8, starting transfers between devices, exchange(): return lax.ppermute(value, ('cells', 'sub'), pairs)  8.76 us
    pallas_call x1, Pallas kernels, finish(): pl.pallas_call(finish_kernel, out_shape=(jax.ShapeDtypeStruct((row_count,...  8.49 us
    pallas_call x1, Pallas kernels, local_sums(): pl.pallas_call(functools.partial(sums_kernel, total_rows), out_shape=(jax...  2.47 us
  transfers between devices with their start and end apart: 8, of which 6 were waited for; matrix products, arithmetic and copies ran while one was open for 0% of the time, Pallas kernels for 0%

profile of v16, /device:TPU:0, one launch (start us, length us, event | category | flops | bytes accessed | tf_op | source)
XLA Modules:
  0.0 32.7 jit_solution(10663770701018130299)
XLA Ops:
  1.3 2.5 %shard_map.67 = (f32[104,256]{1,0:T(8,128)S(1)}, f32[104,256]{1,0:T(8,128)S(1)}, f32[1,512]{1,0:T(1,128)S(1)}) custom-call(f32[512,256]{1,0:T(8,128)} %snapshots_ref.1, f32[512]{0:T(512)} %volumes_hbm.1, s32[1]{0:T(128)S(6)} %copy.7.live_ref, f32[64,512]{1,0:T(8,128)} %probes_hbm.1), custom_call_target="tpu_custom_call" | custom-call | tf_op jit(solution)/shard_map/pallas_call | solution.py:190
  3.8 0.5 %collective-permute-start = (f32[104,256]{1,0:T(8,128)S(1)}, f32[104,256]{1,0:T(8,128)S(1)}, u32[]{:S(2)}, u32[]{:S(2)}) collective-permute-start(f32[104,256]{1,0:T(8,128)S(1)} %get-tuple-element.7), channel_id=1, source_target_pairs={{0,1},{1,0},{2,3},{3,2},{4,5},{5,4},{6,7},{7,6},{8,9},{9,8},{10,11... | collective-permute-start | bytes 319496 | tf_op jit(solution)/shard_map/ppermute | solution.py:282
  4.3 1.0 %collective-permute-done = f32[104,256]{1,0:T(8,128)S(1)} collective-permute-done((f32[104,256]{1,0:T(8,128)S(1)}, f32[104,256]{1,0:T(8,128)S(1)}, u32[]{:S(2)}, u32[]{:S(2)}) %collective-permute-start) | collective-permute-done | bytes 106528 | tf_op jit(solution)/shard_map/ppermute | solution.py:282
  5.3 0.0 copy-start
  5.3 3.6 %collective-permute-start.3 = (f32[104,256]{1,0:T(8,128)S(1)}, f32[104,256]{1,0:T(8,128)S(1)}, u32[]{:S(2)}, u32[]{:S(2)}) collective-permute-start(f32[104,256]{1,0:T(8,128)S(1)} %add.21), channel_id=1, source_target_pairs={{0,7},{1,24},{2,27},{3,4},{4,3},{5,28},{6,31},{7,0},{8,17},{9,14},... | collective-permute-start | bytes 319496 | tf_op jit(solution)/shard_map/ppermute | solution.py:282
  8.9 0.5 %collective-permute-start.2 = (f32[104,256]{1,0:T(8,128)S(1)}, f32[104,256]{1,0:T(8,128)S(1)}, u32[]{:S(2)}, u32[]{:S(2)}) collective-permute-start(f32[104,256]{1,0:T(8,128)S(1)} %add.21), channel_id=1, source_target_pairs={{0,4},{1,17},{2,18},{3,7},{4,0},{5,21},{6,22},{7,3},{8,24},{9,13},... | collective-permute-start | bytes 319496 | tf_op jit(solution)/shard_map/ppermute | solution.py:282
  9.4 0.0 collective-permute-start.1
  9.4 1.9 %collective-permute-done.3 = f32[104,256]{1,0:T(8,128)S(1)} collective-permute-done((f32[104,256]{1,0:T(8,128)S(1)}, f32[104,256]{1,0:T(8,128)S(1)}, u32[]{:S(2)}, u32[]{:S(2)}) %collective-permute-start.3) | collective-permute-done | bytes 106528 | tf_op jit(solution)/shard_map/ppermute | solution.py:282
  11.3 2.3 %collective-permute-done.2 = f32[104,256]{1,0:T(8,128)S(1)} collective-permute-done((f32[104,256]{1,0:T(8,128)S(1)}, f32[104,256]{1,0:T(8,128)S(1)}, u32[]{:S(2)}, u32[]{:S(2)}) %collective-permute-start.2) | collective-permute-done | bytes 106528 | tf_op jit(solution)/shard_map/ppermute | solution.py:282
  13.6 0.0 collective-permute-done.1
  13.6 3.6 %collective-permute-start.6 = (f32[104,256]{1,0:T(8,128)S(1)}, f32[104,256]{1,0:T(8,128)S(1)}, u32[]{:S(2)}, u32[]{:S(2)}) collective-permute-start(f32[104,256]{1,0:T(8,128)S(1)} %add_add_fusion.1), channel_id=1, source_target_pairs={{0,25},{1,6},{2,5},{3,26},{4,29},{5,2},{6,1},{7,30},{8,15},{9,16},... | collective-permute-start | bytes 319496 | tf_op jit(solution)/shard_map/ppermute | solution.py:282
  17.2 0.0 collective-permute-start.5
  17.2 0.4 %collective-permute-start.4 = (f32[104,256]{1,0:T(8,128)S(1)}, f32[104,256]{1,0:T(8,128)S(1)}, u32[]{:S(2)}, u32[]{:S(2)}) collective-permute-start(f32[104,256]{1,0:T(8,128)S(1)} %add_add_fusion.1), channel_id=1, source_target_pairs={{0,9},{1,2},{2,1},{3,10},{4,13},{5,6},{6,5},{7,14},{8,11},{9,0},{1... | collective-permute-start | bytes 319496 | tf_op jit(solution)/shard_map/ppermute | solution.py:282
  17.6 2.2 %collective-permute-done.6 = f32[104,256]{1,0:T(8,128)S(1)} collective-permute-done((f32[104,256]{1,0:T(8,128)S(1)}, f32[104,256]{1,0:T(8,128)S(1)}, u32[]{:S(2)}, u32[]{:S(2)}) %collective-permute-start.6) | collective-permute-done | bytes 106528 | tf_op jit(solution)/shard_map/ppermute | solution.py:282
  19.7 3.1 %collective-permute-done.5 = f32[104,256]{1,0:T(8,128)S(1)} collective-permute-done((f32[104,256]{1,0:T(8,128)S(1)}, f32[104,256]{1,0:T(8,128)S(1)}, u32[]{:S(2)}, u32[]{:S(2)}) %collective-permute-start.5) | collective-permute-done | bytes 106528 | tf_op jit(solution)/shard_map/ppermute | solution.py:282
  22.8 0.0 collective-permute-done.4
  22.8 0.2 collective-permute-start.7
  23.0 0.0 copy-done
  23.0 0.1 shard_map.68.weighted_ref
  23.2 1.1 %collective-permute-done.7.other_ref = f32[104,256]{1,0:T(8,128)S(1)} collective-permute-done((f32[104,256]{1,0:T(8,128)S(1)}, f32[104,256]{1,0:T(8,128)S(1)}, u32[]{:S(2)}, u32[]{:S(2)}) %collective-permute-start.7) | collective-permute-done | bytes 106528 | tf_op jit(solution)/shard_map/ppermute | solution.py:282
  24.2 8.5 %shard_map.69 = (f32[512,256]{1,0:T(8,128)}, f32[256,256]{1,0:T(8,128)}, f32[64,256]{1,0:T(8,128)}) custom-call(f32[104,256]{1,0:T(8,128)S(1)} %add_add_fusion.mine_ref, f32[104,256]{1,0:T(8,128)S(1)} %collective-permute-done.7.other_ref, f32[512,256]{1,0:T(8,128)S(1)} %shard_map.68.weighted_ref), custom_call_target="tpu_custom_call" | custom-call | tf_op jit(solution)/shard_map/pallas_call | solution.py:266
  (3 shorter events, 0.1 us)
Async XLA Ops:
  3.8 1.5 %collective-permute-start = (f32[104,256]{1,0:T(8,128)S(1)}, f32[104,256]{1,0:T(8,128)S(1)}, u32[]{:S(2)}, u32[]{:S(2)}) collective-permute-start(f32[104,256]{1,0:T(8,128)S(1)} %get-tuple-element.7), channel_id=1, source_target_pairs={{0,1},{1,0},{2,3},{3,2},{4,5},{5,4},{6,7},{7,6},{8,9},{9,8},{10,11... | collective-permute-start | bytes 319496 | tf_op jit(solution)/shard_map/ppermute | solution.py:282
  5.3 17.8 %copy-start = (f32[512,256]{1,0:T(8,128)S(1)}, f32[512,256]{1,0:T(8,128)}, u32[]{:S(2)}) copy-start(f32[512,256]{1,0:T(8,128)} %snapshots_ref.1) | copy-start | bytes 1572868
  5.3 6.0 %collective-permute-start.3 = (f32[104,256]{1,0:T(8,128)S(1)}, f32[104,256]{1,0:T(8,128)S(1)}, u32[]{:S(2)}, u32[]{:S(2)}) collective-permute-start(f32[104,256]{1,0:T(8,128)S(1)} %add.21), channel_id=1, source_target_pairs={{0,7},{1,24},{2,27},{3,4},{4,3},{5,28},{6,31},{7,0},{8,17},{9,14},... | collective-permute-start | bytes 319496 | tf_op jit(solution)/shard_map/ppermute | solution.py:282
  8.9 4.7 %collective-permute-start.2 = (f32[104,256]{1,0:T(8,128)S(1)}, f32[104,256]{1,0:T(8,128)S(1)}, u32[]{:S(2)}, u32[]{:S(2)}) collective-permute-start(f32[104,256]{1,0:T(8,128)S(1)} %add.21), channel_id=1, source_target_pairs={{0,4},{1,17},{2,18},{3,7},{4,0},{5,21},{6,22},{7,3},{8,24},{9,13},... | collective-permute-start | bytes 319496 | tf_op jit(solution)/shard_map/ppermute | solution.py:282
  9.4 4.2 %collective-permute-start.1 = (f32[104,256]{1,0:T(8,128)S(1)}, f32[104,256]{1,0:T(8,128)S(1)}, u32[]{:S(2)}, u32[]{:S(2)}) collective-permute-start(f32[104,256]{1,0:T(8,128)S(1)} %add.21), channel_id=1, source_target_pairs={{0,3},{1,8},{2,11},{3,0},{4,7},{5,12},{6,15},{7,4},{8,1},{9,10},{1... | collective-permute-start | bytes 319496 | tf_op jit(solution)/shard_map/ppermute | solution.py:282
  13.6 6.1 %collective-permute-start.6 = (f32[104,256]{1,0:T(8,128)S(1)}, f32[104,256]{1,0:T(8,128)S(1)}, u32[]{:S(2)}, u32[]{:S(2)}) collective-permute-start(f32[104,256]{1,0:T(8,128)S(1)} %add_add_fusion.1), channel_id=1, source_target_pairs={{0,25},{1,6},{2,5},{3,26},{4,29},{5,2},{6,1},{7,30},{8,15},{9,16},... | collective-permute-start | bytes 319496 | tf_op jit(solution)/shard_map/ppermute | solution.py:282
  17.2 5.6 %collective-permute-start.5 = (f32[104,256]{1,0:T(8,128)S(1)}, f32[104,256]{1,0:T(8,128)S(1)}, u32[]{:S(2)}, u32[]{:S(2)}) collective-permute-start(f32[104,256]{1,0:T(8,128)S(1)} %add_add_fusion.1), channel_id=1, source_target_pairs={{0,16},{1,5},{2,6},{3,19},{4,20},{5,1},{6,2},{7,23},{8,12},{9,25},... | collective-permute-start | bytes 319496 | tf_op jit(solution)/shard_map/ppermute | solution.py:282
  17.2 5.6 %collective-permute-start.4 = (f32[104,256]{1,0:T(8,128)S(1)}, f32[104,256]{1,0:T(8,128)S(1)}, u32[]{:S(2)}, u32[]{:S(2)}) collective-permute-start(f32[104,256]{1,0:T(8,128)S(1)} %add_add_fusion.1), channel_id=1, source_target_pairs={{0,9},{1,2},{2,1},{3,10},{4,13},{5,6},{6,5},{7,14},{8,11},{9,0},{1... | collective-permute-start | bytes 319496 | tf_op jit(solution)/shard_map/ppermute | solution.py:282
  22.8 1.4 %collective-permute-start.7 = (f32[104,256]{1,0:T(8,128)S(1)}, f32[104,256]{1,0:T(8,128)S(1)}, u32[]{:S(2)}, u32[]{:S(2)}) collective-permute-start(f32[104,256]{1,0:T(8,128)S(1)} %add_add_fusion.mine_ref), channel_id=1, source_target_pairs={{0,1},{1,0},{2,3},{3,2},{4,5},{5,4},{6,7},{7,6},{8,9},{9,8},{10,11... | collective-permute-start | bytes 319496 | tf_op jit(solution)/shard_map/ppermute | solution.py:282

commit v17 on v13

--- a/solution.py
+++ b/solution.py
@@ -25,7 +25,7 @@
     return lax.dot_general(left, right, (dims, ((), ())), precision=HIGHEST, preferred_element_type=F32)
 
 
-def eliminate(matrix):
+def eliminate(matrix, scratch):
     width = matrix.shape[1]
     count = width // BLOCK
     shape = (BLOCK, width)
@@ -71,7 +71,9 @@
                 here = weights[k][i]
                 weight = here * inv
                 if k == block + 1:
-                    splats = [row_of(here, c) for c in range(BLOCK)]
+                    slot = (block % 2 * BLOCK + i) * BLOCK
+                    scratch[slot : slot + BLOCK, :] = here
+                    splats = [jnp.broadcast_to(scratch[slot + c : slot + c + 1, :], shape) for c in range(BLOCK)]
                 if k in changes:
                     for c in range(BLOCK):
                         change = weight * splats[c]
@@ -215,7 +217,7 @@
     )(snapshots, scale)
 
 
-def finish_kernel(mine_ref, other_ref, weighted_ref, basis_ref, factor_ref, coef_ref):
+def finish_kernel(mine_ref, other_ref, weighted_ref, basis_ref, factor_ref, coef_ref, scratch):
     order = weighted_ref.shape[1]
     probes = coef_ref.shape[0]
     half = order // 2
@@ -231,7 +233,7 @@
     diagonal = packed[half + probes : half + probes + 1, :half]
 
     first = jnp.where(in_upper, square, turned)
-    inverse = eliminate(first)
+    inverse = eliminate(first, scratch)
     beside = product(inverse, packed[:half, half:], ((1,), (0,)))
     second = jnp.where(row_ids > column_ids, square, turned)
     second = jnp.where(row_ids == column_ids, diagonal, second) - product(beside, beside, ((0,), (0,)))
@@ -246,7 +248,7 @@
     basis_ref[:, :half] = left
     rest = weighted_ref[:, half:] - product(left, beside, ((1,), (0,)))
 
-    inverse_second = eliminate(second)
+    inverse_second = eliminate(second, scratch)
     coef_ref[:, half:] = product(cross_rest, inverse_second, ((1,), (1,)))
     basis_ref[:, half:] = product(rest, inverse_second, ((1,), (1,)))
     factor_ref[half:, half:] = jnp.where(in_upper, product(inverse_second, second, ((1,), (0,))), 0.0)
@@ -264,6 +266,7 @@
         ),
         in_specs=[whole] * 3,
         out_specs=(whole,) * 3,
+        scratch_shapes=[pltpu.VMEM((2 * BLOCK * BLOCK, order // 2), F32)],
         compiler_params=pltpu.CompilerParams(vmem_limit_bytes=32 * 1024 * 1024),
     )(mine, other, weighted)
 

time: 31.7 us -> 31.7 us (level)
  no operation moved by 1% of the time
where the time goes in v17:
time: 31.7 us; the launch traced here: 31.5 us
  waiting for transfers between devices  11.5 us (36%)
  Pallas kernels  9.88 us (31%)
  starting transfers between devices  8.76 us (28%)
  between operations  1.32 us (4%)
    ppermute x8, waiting for transfers between devices, exchange(): return lax.ppermute(value, ('cells', 'sub'), pairs)  11.5 us
    ppermute x8, starting transfers between devices, exchange(): return lax.ppermute(value, ('cells', 'sub'), pairs)  8.76 us
    pallas_call x1, Pallas kernels, finish(): pl.pallas_call(finish_kernel, out_shape=(jax.ShapeDtypeStruct((row_count,...  7.28 us
    pallas_call x1, Pallas kernels, local_sums(): pl.pallas_call(functools.partial(sums_kernel, total_rows), out_shape=(jax...  2.47 us
  transfers between devices with their start and end apart: 8, of which 6 were waited for; matrix products, arithmetic and copies ran while one was open for 0% of the time, Pallas kernels for 0%

profile of v17, /device:TPU:0, one launch (start us, length us, event | category | flops | bytes accessed | tf_op | source)
XLA Modules:
  0.0 31.5 jit_solution(12194691140053348076)
XLA Ops:
  1.3 2.5 %shard_map.67 = (f32[104,256]{1,0:T(8,128)S(1)}, f32[104,256]{1,0:T(8,128)S(1)}, f32[1,512]{1,0:T(1,128)S(1)}) custom-call(f32[512,256]{1,0:T(8,128)} %snapshots_ref.1, f32[512]{0:T(512)} %volumes_hbm.1, s32[1]{0:T(128)S(6)} %copy.7.live_ref, f32[64,512]{1,0:T(8,128)} %probes_hbm.1), custom_call_target="tpu_custom_call" | custom-call | tf_op jit(solution)/shard_map/pallas_call | solution.py:184
  3.8 0.5 %collective-permute-start = (f32[104,256]{1,0:T(8,128)S(1)}, f32[104,256]{1,0:T(8,128)S(1)}, u32[]{:S(2)}, u32[]{:S(2)}) collective-permute-start(f32[104,256]{1,0:T(8,128)S(1)} %get-tuple-element.7), channel_id=1, source_target_pairs={{0,1},{1,0},{2,3},{3,2},{4,5},{5,4},{6,7},{7,6},{8,9},{9,8},{10,11... | collective-permute-start | bytes 319496 | tf_op jit(solution)/shard_map/ppermute | solution.py:277
  4.3 1.0 %collective-permute-done = f32[104,256]{1,0:T(8,128)S(1)} collective-permute-done((f32[104,256]{1,0:T(8,128)S(1)}, f32[104,256]{1,0:T(8,128)S(1)}, u32[]{:S(2)}, u32[]{:S(2)}) %collective-permute-start) | collective-permute-done | bytes 106528 | tf_op jit(solution)/shard_map/ppermute | solution.py:277
  5.3 0.0 copy-start
  5.3 3.6 %collective-permute-start.3 = (f32[104,256]{1,0:T(8,128)S(1)}, f32[104,256]{1,0:T(8,128)S(1)}, u32[]{:S(2)}, u32[]{:S(2)}) collective-permute-start(f32[104,256]{1,0:T(8,128)S(1)} %add.21), channel_id=1, source_target_pairs={{0,7},{1,24},{2,27},{3,4},{4,3},{5,28},{6,31},{7,0},{8,17},{9,14},... | collective-permute-start | bytes 319496 | tf_op jit(solution)/shard_map/ppermute | solution.py:277
  8.9 0.5 %collective-permute-start.2 = (f32[104,256]{1,0:T(8,128)S(1)}, f32[104,256]{1,0:T(8,128)S(1)}, u32[]{:S(2)}, u32[]{:S(2)}) collective-permute-start(f32[104,256]{1,0:T(8,128)S(1)} %add.21), channel_id=1, source_target_pairs={{0,4},{1,17},{2,18},{3,7},{4,0},{5,21},{6,22},{7,3},{8,24},{9,13},... | collective-permute-start | bytes 319496 | tf_op jit(solution)/shard_map/ppermute | solution.py:277
  9.4 0.0 collective-permute-start.1
  9.4 1.9 %collective-permute-done.3 = f32[104,256]{1,0:T(8,128)S(1)} collective-permute-done((f32[104,256]{1,0:T(8,128)S(1)}, f32[104,256]{1,0:T(8,128)S(1)}, u32[]{:S(2)}, u32[]{:S(2)}) %collective-permute-start.3) | collective-permute-done | bytes 106528 | tf_op jit(solution)/shard_map/ppermute | solution.py:277
  11.3 2.3 %collective-permute-done.2 = f32[104,256]{1,0:T(8,128)S(1)} collective-permute-done((f32[104,256]{1,0:T(8,128)S(1)}, f32[104,256]{1,0:T(8,128)S(1)}, u32[]{:S(2)}, u32[]{:S(2)}) %collective-permute-start.2) | collective-permute-done | bytes 106528 | tf_op jit(solution)/shard_map/ppermute | solution.py:277
  13.6 0.0 collective-permute-done.1
  13.6 3.6 %collective-permute-start.6 = (f32[104,256]{1,0:T(8,128)S(1)}, f32[104,256]{1,0:T(8,128)S(1)}, u32[]{:S(2)}, u32[]{:S(2)}) collective-permute-start(f32[104,256]{1,0:T(8,128)S(1)} %add_add_fusion.1), channel_id=1, source_target_pairs={{0,25},{1,6},{2,5},{3,26},{4,29},{5,2},{6,1},{7,30},{8,15},{9,16},... | collective-permute-start | bytes 319496 | tf_op jit(solution)/shard_map/ppermute | solution.py:277
  17.2 0.0 collective-permute-start.5
  17.2 0.4 %collective-permute-start.4 = (f32[104,256]{1,0:T(8,128)S(1)}, f32[104,256]{1,0:T(8,128)S(1)}, u32[]{:S(2)}, u32[]{:S(2)}) collective-permute-start(f32[104,256]{1,0:T(8,128)S(1)} %add_add_fusion.1), channel_id=1, source_target_pairs={{0,9},{1,2},{2,1},{3,10},{4,13},{5,6},{6,5},{7,14},{8,11},{9,0},{1... | collective-permute-start | bytes 319496 | tf_op jit(solution)/shard_map/ppermute | solution.py:277
  17.6 2.2 %collective-permute-done.6 = f32[104,256]{1,0:T(8,128)S(1)} collective-permute-done((f32[104,256]{1,0:T(8,128)S(1)}, f32[104,256]{1,0:T(8,128)S(1)}, u32[]{:S(2)}, u32[]{:S(2)}) %collective-permute-start.6) | collective-permute-done | bytes 106528 | tf_op jit(solution)/shard_map/ppermute | solution.py:277
  19.7 3.1 %collective-permute-done.5 = f32[104,256]{1,0:T(8,128)S(1)} collective-permute-done((f32[104,256]{1,0:T(8,128)S(1)}, f32[104,256]{1,0:T(8,128)S(1)}, u32[]{:S(2)}, u32[]{:S(2)}) %collective-permute-start.5) | collective-permute-done | bytes 106528 | tf_op jit(solution)/shard_map/ppermute | solution.py:277
  22.8 0.0 collective-permute-done.4
  22.8 0.2 collective-permute-start.7
  23.0 0.0 copy-done
  23.0 0.1 shard_map.68.weighted_ref
  23.2 1.1 %collective-permute-done.7.other_ref = f32[104,256]{1,0:T(8,128)S(1)} collective-permute-done((f32[104,256]{1,0:T(8,128)S(1)}, f32[104,256]{1,0:T(8,128)S(1)}, u32[]{:S(2)}, u32[]{:S(2)}) %collective-permute-start.7) | collective-permute-done | bytes 106528 | tf_op jit(solution)/shard_map/ppermute | solution.py:277
  24.2 7.3 %shard_map.69 = (f32[512,256]{1,0:T(8,128)}, f32[256,256]{1,0:T(8,128)}, f32[64,256]{1,0:T(8,128)}) custom-call(f32[104,256]{1,0:T(8,128)S(1)} %add_add_fusion.mine_ref, f32[104,256]{1,0:T(8,128)S(1)} %collective-permute-done.7.other_ref, f32[512,256]{1,0:T(8,128)S(1)} %shard_map.68.weighted_ref), custom_call_target="tpu_custom_call" | custom-call | tf_op jit(solution)/shard_map/pallas_call | solution.py:260
  (3 shorter events, 0.1 us)
Async XLA Ops:
  3.8 1.5 %collective-permute-start = (f32[104,256]{1,0:T(8,128)S(1)}, f32[104,256]{1,0:T(8,128)S(1)}, u32[]{:S(2)}, u32[]{:S(2)}) collective-permute-start(f32[104,256]{1,0:T(8,128)S(1)} %get-tuple-element.7), channel_id=1, source_target_pairs={{0,1},{1,0},{2,3},{3,2},{4,5},{5,4},{6,7},{7,6},{8,9},{9,8},{10,11... | collective-permute-start | bytes 319496 | tf_op jit(solution)/shard_map/ppermute | solution.py:277
  5.3 17.8 %copy-start = (f32[512,256]{1,0:T(8,128)S(1)}, f32[512,256]{1,0:T(8,128)}, u32[]{:S(2)}) copy-start(f32[512,256]{1,0:T(8,128)} %snapshots_ref.1) | copy-start | bytes 1572868
  5.3 6.0 %collective-permute-start.3 = (f32[104,256]{1,0:T(8,128)S(1)}, f32[104,256]{1,0:T(8,128)S(1)}, u32[]{:S(2)}, u32[]{:S(2)}) collective-permute-start(f32[104,256]{1,0:T(8,128)S(1)} %add.21), channel_id=1, source_target_pairs={{0,7},{1,24},{2,27},{3,4},{4,3},{5,28},{6,31},{7,0},{8,17},{9,14},... | collective-permute-start | bytes 319496 | tf_op jit(solution)/shard_map/ppermute | solution.py:277
  8.9 4.7 %collective-permute-start.2 = (f32[104,256]{1,0:T(8,128)S(1)}, f32[104,256]{1,0:T(8,128)S(1)}, u32[]{:S(2)}, u32[]{:S(2)}) collective-permute-start(f32[104,256]{1,0:T(8,128)S(1)} %add.21), channel_id=1, source_target_pairs={{0,4},{1,17},{2,18},{3,7},{4,0},{5,21},{6,22},{7,3},{8,24},{9,13},... | collective-permute-start | bytes 319496 | tf_op jit(solution)/shard_map/ppermute | solution.py:277
  9.4 4.2 %collective-permute-start.1 = (f32[104,256]{1,0:T(8,128)S(1)}, f32[104,256]{1,0:T(8,128)S(1)}, u32[]{:S(2)}, u32[]{:S(2)}) collective-permute-start(f32[104,256]{1,0:T(8,128)S(1)} %add.21), channel_id=1, source_target_pairs={{0,3},{1,8},{2,11},{3,0},{4,7},{5,12},{6,15},{7,4},{8,1},{9,10},{1... | collective-permute-start | bytes 319496 | tf_op jit(solution)/shard_map/ppermute | solution.py:277
  13.6 6.1 %collective-permute-start.6 = (f32[104,256]{1,0:T(8,128)S(1)}, f32[104,256]{1,0:T(8,128)S(1)}, u32[]{:S(2)}, u32[]{:S(2)}) collective-permute-start(f32[104,256]{1,0:T(8,128)S(1)} %add_add_fusion.1), channel_id=1, source_target_pairs={{0,25},{1,6},{2,5},{3,26},{4,29},{5,2},{6,1},{7,30},{8,15},{9,16},... | collective-permute-start | bytes 319496 | tf_op jit(solution)/shard_map/ppermute | solution.py:277
  17.2 5.6 %collective-permute-start.5 = (f32[104,256]{1,0:T(8,128)S(1)}, f32[104,256]{1,0:T(8,128)S(1)}, u32[]{:S(2)}, u32[]{:S(2)}) collective-permute-start(f32[104,256]{1,0:T(8,128)S(1)} %add_add_fusion.1), channel_id=1, source_target_pairs={{0,16},{1,5},{2,6},{3,19},{4,20},{5,1},{6,2},{7,23},{8,12},{9,25},... | collective-permute-start | bytes 319496 | tf_op jit(solution)/shard_map/ppermute | solution.py:277
  17.2 5.6 %collective-permute-start.4 = (f32[104,256]{1,0:T(8,128)S(1)}, f32[104,256]{1,0:T(8,128)S(1)}, u32[]{:S(2)}, u32[]{:S(2)}) collective-permute-start(f32[104,256]{1,0:T(8,128)S(1)} %add_add_fusion.1), channel_id=1, source_target_pairs={{0,9},{1,2},{2,1},{3,10},{4,13},{5,6},{6,5},{7,14},{8,11},{9,0},{1... | collective-permute-start | bytes 319496 | tf_op jit(solution)/shard_map/ppermute | solution.py:277
  22.8 1.4 %collective-permute-start.7 = (f32[104,256]{1,0:T(8,128)S(1)}, f32[104,256]{1,0:T(8,128)S(1)}, u32[]{:S(2)}, u32[]{:S(2)}) collective-permute-start(f32[104,256]{1,0:T(8,128)S(1)} %add_add_fusion.mine_ref), channel_id=1, source_target_pairs={{0,1},{1,0},{2,3},{3,2},{4,5},{5,4},{6,7},{7,6},{8,9},{9,8},{10,11... | collective-permute-start | bytes 319496 | tf_op jit(solution)/shard_map/ppermute | solution.py:277

commit v18 on v13

--- a/solution.py
+++ b/solution.py
@@ -279,9 +279,9 @@
     split = len(phases) // 2
     mine = keep + exchange(send, (1, 1))
     for (low, high), (other_low, other_high) in zip(phases, phases[split:] + phases[:split]):
+        across = exchange(mine, (low ^ high ^ 1, other_low ^ other_high ^ 1))
+        far = exchange(mine, (high, other_high))
         near = exchange(mine, (low ^ 1, other_low ^ 1))
-        far = exchange(mine, (high, other_high))
-        across = exchange(mine, (low ^ high ^ 1, other_low ^ other_high ^ 1))
         mine = (mine + near) + (far + across)
     for bit in single:
         mine = mine + exchange(mine, (bit, bit))

time: 31.7 us -> 31.7 us (level)
  no operation moved by 1% of the time
where the time goes in v18:
time: 31.7 us; the launch traced here: 31.6 us
  waiting for transfers between devices  11.5 us (36%)
  Pallas kernels  9.96 us (31%)
  starting transfers between devices  8.76 us (28%)
  between operations  1.32 us (4%)
    ppermute x8, waiting for transfers between devices, exchange(): return lax.ppermute(value, ('cells', 'sub'), pairs)  11.5 us
    ppermute x8, starting transfers between devices, exchange(): return lax.ppermute(value, ('cells', 'sub'), pairs)  8.76 us
    pallas_call x1, Pallas kernels, finish(): pl.pallas_call(finish_kernel, out_shape=(jax.ShapeDtypeStruct((row_count,...  7.36 us
    pallas_call x1, Pallas kernels, local_sums(): pl.pallas_call(functools.partial(sums_kernel, total_rows), out_shape=(jax...  2.47 us
  transfers between devices with their start and end apart: 8, of which 6 were waited for; matrix products, arithmetic and copies ran while one was open for 0% of the time, Pallas kernels for 0%

profile of v18, /device:TPU:0, one launch (start us, length us, event | category | flops | bytes accessed | tf_op | source)
XLA Modules:
  0.0 31.6 jit_solution(15567690636137724738)
XLA Ops:
  1.3 2.5 %shard_map.67 = (f32[104,256]{1,0:T(8,128)S(1)}, f32[104,256]{1,0:T(8,128)S(1)}, f32[1,512]{1,0:T(1,128)S(1)}) custom-call(f32[512,256]{1,0:T(8,128)} %snapshots_ref.1, f32[512]{0:T(512)} %volumes_hbm.1, s32[1]{0:T(128)S(6)} %copy.7.live_ref, f32[64,512]{1,0:T(8,128)} %probes_hbm.1), custom_call_target="tpu_custom_call" | custom-call | tf_op jit(solution)/shard_map/pallas_call | solution.py:182
  3.8 0.5 %collective-permute-start = (f32[104,256]{1,0:T(8,128)S(1)}, f32[104,256]{1,0:T(8,128)S(1)}, u32[]{:S(2)}, u32[]{:S(2)}) collective-permute-start(f32[104,256]{1,0:T(8,128)S(1)} %get-tuple-element.7), channel_id=1, source_target_pairs={{0,1},{1,0},{2,3},{3,2},{4,5},{5,4},{6,7},{7,6},{8,9},{9,8},{10,11... | collective-permute-start | bytes 319496 | tf_op jit(solution)/shard_map/ppermute | solution.py:274
  4.3 1.0 %collective-permute-done = f32[104,256]{1,0:T(8,128)S(1)} collective-permute-done((f32[104,256]{1,0:T(8,128)S(1)}, f32[104,256]{1,0:T(8,128)S(1)}, u32[]{:S(2)}, u32[]{:S(2)}) %collective-permute-start) | collective-permute-done | bytes 106528 | tf_op jit(solution)/shard_map/ppermute | solution.py:274
  5.3 0.0 copy-start
  5.3 3.6 %collective-permute-start.3 = (f32[104,256]{1,0:T(8,128)S(1)}, f32[104,256]{1,0:T(8,128)S(1)}, u32[]{:S(2)}, u32[]{:S(2)}) collective-permute-start(f32[104,256]{1,0:T(8,128)S(1)} %add.21), channel_id=1, source_target_pairs={{0,7},{1,24},{2,27},{3,4},{4,3},{5,28},{6,31},{7,0},{8,17},{9,14},... | collective-permute-start | bytes 319496 | tf_op jit(solution)/shard_map/ppermute | solution.py:274
  8.9 0.5 %collective-permute-start.2 = (f32[104,256]{1,0:T(8,128)S(1)}, f32[104,256]{1,0:T(8,128)S(1)}, u32[]{:S(2)}, u32[]{:S(2)}) collective-permute-start(f32[104,256]{1,0:T(8,128)S(1)} %add.21), channel_id=1, source_target_pairs={{0,4},{1,17},{2,18},{3,7},{4,0},{5,21},{6,22},{7,3},{8,24},{9,13},... | collective-permute-start | bytes 319496 | tf_op jit(solution)/shard_map/ppermute | solution.py:274
  9.4 0.0 collective-permute-start.1
  9.4 1.9 %collective-permute-done.3 = f32[104,256]{1,0:T(8,128)S(1)} collective-permute-done((f32[104,256]{1,0:T(8,128)S(1)}, f32[104,256]{1,0:T(8,128)S(1)}, u32[]{:S(2)}, u32[]{:S(2)}) %collective-permute-start.3) | collective-permute-done | bytes 106528 | tf_op jit(solution)/shard_map/ppermute | solution.py:274
  11.3 2.3 %collective-permute-done.2 = f32[104,256]{1,0:T(8,128)S(1)} collective-permute-done((f32[104,256]{1,0:T(8,128)S(1)}, f32[104,256]{1,0:T(8,128)S(1)}, u32[]{:S(2)}, u32[]{:S(2)}) %collective-permute-start.2) | collective-permute-done | bytes 106528 | tf_op jit(solution)/shard_map/ppermute | solution.py:274
  13.6 0.0 collective-permute-done.1
  13.6 3.6 %collective-permute-start.6 = (f32[104,256]{1,0:T(8,128)S(1)}, f32[104,256]{1,0:T(8,128)S(1)}, u32[]{:S(2)}, u32[]{:S(2)}) collective-permute-start(f32[104,256]{1,0:T(8,128)S(1)} %add_add_fusion.1), channel_id=1, source_target_pairs={{0,25},{1,6},{2,5},{3,26},{4,29},{5,2},{6,1},{7,30},{8,15},{9,16},... | collective-permute-start | bytes 319496 | tf_op jit(solution)/shard_map/ppermute | solution.py:274
  17.2 0.0 collective-permute-start.5
  17.2 0.4 %collective-permute-start.4 = (f32[104,256]{1,0:T(8,128)S(1)}, f32[104,256]{1,0:T(8,128)S(1)}, u32[]{:S(2)}, u32[]{:S(2)}) collective-permute-start(f32[104,256]{1,0:T(8,128)S(1)} %add_add_fusion.1), channel_id=1, source_target_pairs={{0,9},{1,2},{2,1},{3,10},{4,13},{5,6},{6,5},{7,14},{8,11},{9,0},{1... | collective-permute-start | bytes 319496 | tf_op jit(solution)/shard_map/ppermute | solution.py:274
  17.6 2.2 %collective-permute-done.6 = f32[104,256]{1,0:T(8,128)S(1)} collective-permute-done((f32[104,256]{1,0:T(8,128)S(1)}, f32[104,256]{1,0:T(8,128)S(1)}, u32[]{:S(2)}, u32[]{:S(2)}) %collective-permute-start.6) | collective-permute-done | bytes 106528 | tf_op jit(solution)/shard_map/ppermute | solution.py:274
  19.7 3.1 %collective-permute-done.5 = f32[104,256]{1,0:T(8,128)S(1)} collective-permute-done((f32[104,256]{1,0:T(8,128)S(1)}, f32[104,256]{1,0:T(8,128)S(1)}, u32[]{:S(2)}, u32[]{:S(2)}) %collective-permute-start.5) | collective-permute-done | bytes 106528 | tf_op jit(solution)/shard_map/ppermute | solution.py:274
  22.8 0.0 collective-permute-done.4
  22.8 0.2 collective-permute-start.7
  23.0 0.0 copy-done
  23.0 0.1 shard_map.68.weighted_ref
  23.2 1.1 %collective-permute-done.7.other_ref = f32[104,256]{1,0:T(8,128)S(1)} collective-permute-done((f32[104,256]{1,0:T(8,128)S(1)}, f32[104,256]{1,0:T(8,128)S(1)}, u32[]{:S(2)}, u32[]{:S(2)}) %collective-permute-start.7) | collective-permute-done | bytes 106528 | tf_op jit(solution)/shard_map/ppermute | solution.py:274
  24.2 7.4 %shard_map.69 = (f32[512,256]{1,0:T(8,128)}, f32[256,256]{1,0:T(8,128)}, f32[64,256]{1,0:T(8,128)}) custom-call(f32[104,256]{1,0:T(8,128)S(1)} %add_add_fusion.mine_ref, f32[104,256]{1,0:T(8,128)S(1)} %collective-permute-done.7.other_ref, f32[512,256]{1,0:T(8,128)S(1)} %shard_map.68.weighted_ref), custom_call_target="tpu_custom_call" | custom-call | tf_op jit(solution)/shard_map/pallas_call | solution.py:258
  (3 shorter events, 0.1 us)
Async XLA Ops:
  3.8 1.5 %collective-permute-start = (f32[104,256]{1,0:T(8,128)S(1)}, f32[104,256]{1,0:T(8,128)S(1)}, u32[]{:S(2)}, u32[]{:S(2)}) collective-permute-start(f32[104,256]{1,0:T(8,128)S(1)} %get-tuple-element.7), channel_id=1, source_target_pairs={{0,1},{1,0},{2,3},{3,2},{4,5},{5,4},{6,7},{7,6},{8,9},{9,8},{10,11... | collective-permute-start | bytes 319496 | tf_op jit(solution)/shard_map/ppermute | solution.py:274
  5.3 17.8 %copy-start = (f32[512,256]{1,0:T(8,128)S(1)}, f32[512,256]{1,0:T(8,128)}, u32[]{:S(2)}) copy-start(f32[512,256]{1,0:T(8,128)} %snapshots_ref.1) | copy-start | bytes 1572868
  5.3 6.0 %collective-permute-start.3 = (f32[104,256]{1,0:T(8,128)S(1)}, f32[104,256]{1,0:T(8,128)S(1)}, u32[]{:S(2)}, u32[]{:S(2)}) collective-permute-start(f32[104,256]{1,0:T(8,128)S(1)} %add.21), channel_id=1, source_target_pairs={{0,7},{1,24},{2,27},{3,4},{4,3},{5,28},{6,31},{7,0},{8,17},{9,14},... | collective-permute-start | bytes 319496 | tf_op jit(solution)/shard_map/ppermute | solution.py:274
  8.9 4.7 %collective-permute-start.2 = (f32[104,256]{1,0:T(8,128)S(1)}, f32[104,256]{1,0:T(8,128)S(1)}, u32[]{:S(2)}, u32[]{:S(2)}) collective-permute-start(f32[104,256]{1,0:T(8,128)S(1)} %add.21), channel_id=1, source_target_pairs={{0,4},{1,17},{2,18},{3,7},{4,0},{5,21},{6,22},{7,3},{8,24},{9,13},... | collective-permute-start | bytes 319496 | tf_op jit(solution)/shard_map/ppermute | solution.py:274
  9.4 4.2 %collective-permute-start.1 = (f32[104,256]{1,0:T(8,128)S(1)}, f32[104,256]{1,0:T(8,128)S(1)}, u32[]{:S(2)}, u32[]{:S(2)}) collective-permute-start(f32[104,256]{1,0:T(8,128)S(1)} %add.21), channel_id=1, source_target_pairs={{0,3},{1,8},{2,11},{3,0},{4,7},{5,12},{6,15},{7,4},{8,1},{9,10},{1... | collective-permute-start | bytes 319496 | tf_op jit(solution)/shard_map/ppermute | solution.py:274
  13.6 6.1 %collective-permute-start.6 = (f32[104,256]{1,0:T(8,128)S(1)}, f32[104,256]{1,0:T(8,128)S(1)}, u32[]{:S(2)}, u32[]{:S(2)}) collective-permute-start(f32[104,256]{1,0:T(8,128)S(1)} %add_add_fusion.1), channel_id=1, source_target_pairs={{0,25},{1,6},{2,5},{3,26},{4,29},{5,2},{6,1},{7,30},{8,15},{9,16},... | collective-permute-start | bytes 319496 | tf_op jit(solution)/shard_map/ppermute | solution.py:274
  17.2 5.6 %collective-permute-start.5 = (f32[104,256]{1,0:T(8,128)S(1)}, f32[104,256]{1,0:T(8,128)S(1)}, u32[]{:S(2)}, u32[]{:S(2)}) collective-permute-start(f32[104,256]{1,0:T(8,128)S(1)} %add_add_fusion.1), channel_id=1, source_target_pairs={{0,16},{1,5},{2,6},{3,19},{4,20},{5,1},{6,2},{7,23},{8,12},{9,25},... | collective-permute-start | bytes 319496 | tf_op jit(solution)/shard_map/ppermute | solution.py:274
  17.2 5.6 %collective-permute-start.4 = (f32[104,256]{1,0:T(8,128)S(1)}, f32[104,256]{1,0:T(8,128)S(1)}, u32[]{:S(2)}, u32[]{:S(2)}) collective-permute-start(f32[104,256]{1,0:T(8,128)S(1)} %add_add_fusion.1), channel_id=1, source_target_pairs={{0,9},{1,2},{2,1},{3,10},{4,13},{5,6},{6,5},{7,14},{8,11},{9,0},{1... | collective-permute-start | bytes 319496 | tf_op jit(solution)/shard_map/ppermute | solution.py:274
  22.8 1.4 %collective-permute-start.7 = (f32[104,256]{1,0:T(8,128)S(1)}, f32[104,256]{1,0:T(8,128)S(1)}, u32[]{:S(2)}, u32[]{:S(2)}) collective-permute-start(f32[104,256]{1,0:T(8,128)S(1)} %add_add_fusion.mine_ref), channel_id=1, source_target_pairs={{0,1},{1,0},{2,3},{3,2},{4,5},{5,4},{6,7},{7,6},{8,9},{9,8},{10,11... | collective-permute-start | bytes 319496 | tf_op jit(solution)/shard_map/ppermute | solution.py:274
